TPU v7x, 32 devices: a whole 2x2x4 slice. The times are simulated.
32 devices in a mesh: ctx: 32 (over z, y, x, core).
Axes of the slice: x: 2, y: 2, z: 4, core: 2. Of those that a mesh axis runs over, the one named last changes fastest.
Arguments:
- query: bfloat16 [8192, 1280], P('ctx'), may hold values from -16 to 16
- key: bfloat16 [8192, 1280], P('ctx'), may hold values from -16 to 16
- value: bfloat16 [8192, 1280], P('ctx'), may hold values from -6 to 6
- grad_out: bfloat16 [8192, 1280], P('ctx'), may hold values from -16 to 16
- offsets: int32 [2, 10], replicated, may hold values from 0 to 255, as said below
Outputs:
- grad_query: bfloat16 [8192, 1280], P('ctx')
- grad_key: bfloat16 [8192, 1280], P('ctx')
- grad_value: bfloat16 [8192, 1280], P('ctx')
Inputs may be any that keep to these rules, and one draw needn't show every extreme that they name: Row 0 holds 0 or 1 for each head, half of the heads taking each; row 1 holds distinct offsets below 256, one of them 256 - 1.
All inputs are finite; a program needn't handle non-finite values.
Results may differ from a plain program's by a relative error of at most 0.007.
Values may be sent and summed in bfloat16 or wider, within the bound.
No kernel may reach another device: no remote copies, remote signals or barrier semaphores. Data moves between devices by JAX's collectives and lax.ppermute only.
A program may use at most 64 MiB of HBM per device.

v0:
```python
import functools

import jax
import jax.numpy as jnp
from jax import lax
from jax.experimental import pallas as pl
from jax.experimental.pallas import tpu as pltpu
from jax.sharding import PartitionSpec as P

NEG = -1e30
F32 = jnp.float32
BF16 = jnp.bfloat16
STAT_ROWS = 4
VMEM_LIMIT = 16 * 1024 * 1024
LOG2E = 1.4426950408889634


def iota(shape, dim):
    return lax.broadcasted_iota(jnp.int32, shape, dim)


def dot_nt(a, b):
    return lax.dot_general(a, b, (((1,), (1,)), ((), ())), preferred_element_type=F32)


def dot_tn(a, b):
    return lax.dot_general(a, b, (((0,), (0,)), ((), ())), preferred_element_type=F32)


def dot_nn(a, b):
    return lax.dot_general(a, b, (((1,), (0,)), ((), ())), preferred_element_type=F32)


def block_rows(rows, heads):
    row = iota(rows.shape, 0)
    return jnp.concatenate(
        [jnp.where(row == h, rows, 0.0).astype(BF16) for h in range(heads)], axis=1
    )


def own_columns(wide_rows, heads):
    dh = wide_rows.shape[1] // heads
    row = iota((16, dh), 0)
    return sum(
        jnp.where(row == h, wide_rows[:, h * dh : (h + 1) * dh], 0.0) for h in range(heads)
    )


def offset_column(off_ref, level, heads, rows):
    row = jnp.bitwise_and(iota((rows, 1), 0), 15)
    column = jnp.zeros((rows, 1), jnp.int32)
    for h in range(heads):
        column = jnp.where(row == h, off_ref[level, h], column)
    return column


def level_one_keys(off_ref, heads, rows, length):
    pair = offset_column(off_ref, 0, heads, rows)
    wide = offset_column(off_ref, 1, heads, rows)
    lane = iota((rows, length), 1)
    chosen = jnp.bitwise_and(wide, 1) == pair
    return jnp.logical_and(jnp.bitwise_and(lane, 1) == pair, chosen)


def row_weights(off_ref, heads, length):
    both = level_one_keys(off_ref, heads, 32, length).astype(F32)
    return jnp.where(iota((32, length), 0) < 16, 1.0 + both, both)


def pack_kernel(heads, off_ref, q_ref, g_ref, out_ref, buf, acc, sems):
    dh = out_ref.shape[1]
    copies = []
    for s, ref in enumerate((q_ref, g_ref)):
        for h in range(heads):
            base = pl.multiple_of(jnp.bitwise_and(off_ref[1, h], ~15), 16)
            slot = s * heads + h
            copy = pltpu.make_async_copy(
                ref.at[pl.ds(base, 16), pl.ds(h * dh, dh)], buf.at[slot], sems.at[slot]
            )
            copy.start()
            copies.append(copy)
    acc[...] = jnp.zeros_like(acc)
    row = iota((16, dh), 0)
    for s in range(2):
        for h in range(heads):
            slot = s * heads + h
            copies[slot].wait()
            own = row == jnp.bitwise_and(off_ref[1, h], 15)
            block = jnp.where(own, buf[slot].astype(F32), 0.0)
            acc[16 * s + h : 16 * s + h + 1, :] = jnp.sum(block, axis=0, keepdims=True)
    out_ref[...] = acc[...].astype(BF16)


def stats_kernel(
    heads, span, off_hbm, own_ref, far_ref, k_ref, v_ref, load_ref, s_ref, dp_ref,
    off_ref, acc, load, off_sem, sems,
):
    offsets = pltpu.make_async_copy(off_hbm, off_ref, off_sem)
    offsets.start()
    dh = own_ref.shape[1]
    length = k_ref.shape[0]
    own, far = own_ref[...].astype(F32), far_ref[...].astype(F32)

    def both_rows(first):
        return jnp.concatenate(
            [block_rows(rows[first : first + 16, :], heads) for rows in (own, far)], axis=0
        )

    s = dot_nt(both_rows(0), k_ref[...]) * (dh**-0.5 * LOG2E)
    dp = dot_nt(both_rows(16), v_ref[...])
    s_ref[...] = s
    dp_ref[...] = dp
    offsets.wait()
    part, slots = heads // 2, load_ref.shape[1]

    def slot(array, h):
        return (h // part) * slots + array * part + h % part

    place = iota((16, dh), 0)
    for i, ref in enumerate((k_ref, v_ref)):
        for h in range(heads):
            base = pl.multiple_of(jnp.bitwise_and(off_ref[1, h], ~15), 16)
            block = ref[pl.ds(base, 16), h * dh : (h + 1) * dh].astype(F32)
            block = jnp.where(place == jnp.bitwise_and(off_ref[1, h], 15), block, 0.0)
            acc[slot(i, h) : slot(i, h) + 1, :] = jnp.sum(block, axis=0, keepdims=True)
    for i, first in ((2, 0), (3, 16)):
        for c in range(2):
            row = slot(i, c * part)
            acc[row : row + part, :] = own[first + c * part : first + (c + 1) * part, :]
    weight = row_weights(off_ref, heads, length)
    masked = jnp.where(weight > 0.0, s, NEG)
    m = jnp.max(masked, axis=1, keepdims=True)
    e = jnp.exp2(masked - m) * weight
    t = jnp.sum(e, axis=1, keepdims=True)
    d = jnp.sum(e * dp, axis=1, keepdims=True)
    lane = iota((32, 128), 1)
    table = jnp.where(lane == 0, m, jnp.where(lane == 1, t, jnp.where(lane == 2, d, 0.0)))
    table = jnp.concatenate([table, jnp.zeros((96, 128), F32)], axis=0).T[0:STAT_ROWS, :]
    high = table.astype(BF16).astype(F32)
    rest = table - high
    middle = rest.astype(BF16).astype(F32)
    low = (rest - middle).astype(BF16).astype(F32)
    table = high + pltpu.roll(middle, 32, 1) + pltpu.roll(low, 64, 1)
    for c in range(2):
        acc[c * slots + 4 * part : (c + 1) * slots, :] = table
    halves = acc[...].astype(BF16).reshape(2, slots, dh)
    repeat = load.shape[0]
    for i in range(repeat // 2):
        load[2 * i : 2 * i + 2] = halves
    copies = [
        pltpu.make_async_copy(load, load_ref.at[pl.ds(i * repeat, repeat)], sems.at[i])
        for i in range(span // repeat)
    ]
    for copy in copies:
        copy.start()
    for copy in copies:
        copy.wait()


def near_head(off_ref, h, inputs, outputs, wait, send):
    q_ref, k_ref, v_ref, g_ref, kf_ref, vf_ref = inputs
    dq_ref, dk_ref, dv_ref, ret_ref = outputs
    length, dh = q_ref.shape[0], q_ref.shape[1] // off_ref.shape[1]
    half = length // 2
    scale = dh**-0.5
    cols = slice(h * dh, (h + 1) * dh)
    wait(h)
    pair, wide = off_ref[0, h], off_ref[1, h]
    q, k, v, g = q_ref[:, cols], k_ref[:, cols], v_ref[:, cols], g_ref[:, cols]
    pick = (iota((half, length), 1) == 2 * iota((half, length), 0) + pair).astype(BF16)
    kc = dot_nn(pick, kf_ref[:, cols]).astype(BF16)
    yield
    lanes = iota((1, length), 1)
    chosen = jnp.bitwise_and(lanes, 1) == pair
    a_t = chosen.astype(F32)
    a_u = (jnp.bitwise_and(iota((length, 1), 0), 1) == pair).astype(F32)
    s1 = dot_nt(k, q)
    s2 = dot_nt(kc, q) + jnp.where(chosen, 0.0, NEG)
    vc = dot_nn(pick, vf_ref[:, cols]).astype(BF16)
    yield
    m = jnp.maximum(jnp.max(s1, axis=0, keepdims=True), jnp.max(s2, axis=0, keepdims=True))
    m = m * (scale * LOG2E)
    dp1 = dot_nt(v, g)
    dp2 = dot_nt(vc, g)
    yield
    e1 = jnp.exp2(s1 * (scale * LOG2E) - m) * (1.0 + a_t * a_u)
    e2 = jnp.exp2(s2 * (scale * LOG2E) - m)
    total = jnp.sum(e1, axis=0, keepdims=True) + jnp.sum(e2, axis=0, keepdims=True)
    part = jnp.sum(e1 * dp1, axis=0, keepdims=True) + jnp.sum(e2 * dp2, axis=0, keepdims=True)
    yield
    inverse = jnp.where(lanes == wide, 0.0, 1.0 / total)
    delta = part * inverse
    p1 = e1 * inverse
    p2 = e2 * inverse
    ds1 = (scale * p1 * (dp1 - delta)).astype(BF16)
    ds2 = (scale * p2 * (dp2 - delta)).astype(BF16)
    p1 = p1.astype(BF16)
    p2 = p2.astype(BF16)
    yield
    dk_ref[:, cols] = dot_nn(ds1, q)
    dv_ref[:, cols] = dot_nn(p1, g)
    ret_ref[:half, cols] = dot_nn(ds2, q).astype(BF16)
    ret_ref[half:, cols] = dot_nn(p2, g).astype(BF16)
    dq_ref[:, cols] = (dot_tn(k, ds1) + dot_tn(kc, ds2)).T.astype(BF16)
    send(h)
    yield


def main_kernel(
    heads, off_hbm, after_ref, own_ref, q_ref, k_ref, v_ref, g_ref, kf_ref, vf_ref,
    dq_hbm, dk_hbm, dv_hbm, ret_hbm, far_hbm,
    off_ref, dq_ref, dk_ref, dv_ref, ret_ref, far_scores, off_sem, far_sem, out_sems,
):
    offsets = pltpu.make_async_copy(off_hbm, off_ref, off_sem)
    offsets.start()
    dh = q_ref.shape[1] // heads
    near = (dq_ref, dk_ref, dv_ref, ret_ref)
    writes = []

    def wait(h):
        if h == 0:
            offsets.wait()

    def send(h):
        if h % 2 == 1:
            cols = slice((h - 1) * dh, (h + 1) * dh)
            for i, (a, b) in enumerate(zip(near, (dq_hbm, dk_hbm, dv_hbm, ret_hbm))):
                sem = out_sems.at[h // 2, i]
                copy = pltpu.make_async_copy(a.at[:, cols], b.at[:, cols], sem)
                copy.start()
                writes.append(copy)

    inputs = (q_ref, k_ref, v_ref, g_ref, kf_ref, vf_ref)
    work = [near_head(off_ref, h, inputs, near, wait, send) for h in range(heads)]
    steps, lag = 6, 2
    for turn in range(steps + lag * (heads - 1)):
        for h in reversed(range(heads)):
            if 0 <= turn - lag * h < steps:
                next(work[h])
        if turn == steps:
            own = own_ref[...].astype(F32)
            queries, grads = block_rows(own[:16, :], heads), block_rows(own[16:, :], heads)
            far_scores[:16, :] = dot_nt(queries, kf_ref[...]) * (dh**-0.5 * LOG2E)
            far_scores[16:, :] = dot_nt(grads, vf_ref[...])
            copy = pltpu.make_async_copy(far_scores, far_hbm, far_sem)
            copy.start()
            writes.append(copy)
    for copy in writes:
        copy.wait()


def wide_kernel(
    heads, span, recv_ref, mine_ref, theirs_ref, flat
):
    part, slots, dh = heads // 2, recv_ref.shape[1], recv_ref.shape[2]
    scale = dh**-0.5
    me = lax.rem(lax.axis_index("ctx"), span)
    mate = jnp.bitwise_xor(me, 1)
    first = jnp.bitwise_and(me, 1) == 0
    flat[...] = recv_ref[...].astype(F32).reshape(span * slots, dh)

    def gathered(slot):
        return flat[pl.ds(slot, span, stride=slots), :]

    even = jnp.bitwise_and(iota((8, 128), 1), 1) == 0

    def stat(index):
        x = gathered(4 * part + index)
        x = x + pltpu.roll(x, 96, 1) + pltpu.roll(x, 64, 1)
        if span < 128:
            x = jnp.concatenate([x, jnp.zeros((128 - span, 128), F32)], axis=0)
        x = x.T
        near = jnp.where(first, x[0:8, :], x[part : part + 8, :])
        other = jnp.where(first, x[16:24, :], x[16 + part : 24 + part, :])
        other = jnp.where(even, pltpu.roll(other, 127, 1), pltpu.roll(other, 1, 1))
        return near[:, :span], other[:, :span]

    (m_a, m_b), (t_a, t_b), (d_a, d_b) = stat(0), stat(1), stat(2)
    row = iota((16, span), 0)
    device = iota((span, 1), 0)
    k_w, v_w, q_w, g_w = [
        [gathered(i * part + j).astype(BF16) for j in range(part)] for i in range(4)
    ]
    m_c, t_c, d_c = [jnp.zeros((8, span), F32) for _ in range(3)]
    s_key, dp_key, s_row, dp_row = [jnp.zeros((16, span), F32) for _ in range(4)]

    def two_rows(x, j, table):
        for index, device_of in enumerate((me, mate)):
            one = jnp.sum(jnp.where(device == device_of, x, 0.0), axis=0, keepdims=True)
            table = jnp.where(row == 8 * index + j, one, table)
        return table

    for j in range(part):
        s = dot_nt(k_w[j], q_w[j]) * (scale * LOG2E)
        dp = dot_nt(v_w[j], g_w[j])
        m = jnp.max(s, axis=0, keepdims=True)
        e = jnp.exp2(s - m)
        here = row[:8] == j
        m_c = jnp.where(here, m, m_c)
        t_c = jnp.where(here, jnp.sum(e, axis=0, keepdims=True), t_c)
        d_c = jnp.where(here, jnp.sum(e * dp, axis=0, keepdims=True), d_c)
        s_key = two_rows(s, j, s_key)
        dp_key = two_rows(dp, j, dp_key)
        s_row = two_rows(dot_nt(q_w[j], k_w[j]) * (scale * LOG2E), j, s_row)
        dp_row = two_rows(dot_nt(g_w[j], v_w[j]), j, dp_row)
    m_all = jnp.maximum(jnp.maximum(m_a, m_b), m_c)
    w_a, w_b, w_c = jnp.exp2(m_a - m_all), jnp.exp2(m_b - m_all), jnp.exp2(m_c - m_all)
    inverse = 1.0 / (t_a * w_a + t_b * w_b + t_c * w_c)
    delta = (d_a * w_a + d_b * w_b + d_c * w_c) * inverse

    def twice(x):
        return jnp.concatenate([x, x], axis=0)

    def column(x, index):
        return jnp.sum(jnp.where(iota((8, span), 1) == index, x, 0.0), axis=1, keepdims=True)

    p_key = jnp.exp2(s_key - twice(m_all)) * twice(inverse)
    ds_key = scale * p_key * (dp_key - twice(delta))
    of_me = [column(x, me) for x in (m_all, inverse, delta)]
    of_mate = [column(x, mate) for x in (m_all, inverse, delta)]
    m_r, i_r, d_r = [jnp.concatenate(pair, axis=0) for pair in zip(of_me, of_mate)]
    ds_row = scale * (jnp.exp2(s_row - m_r) * i_r) * (dp_row - d_r)

    def times(left, right):
        index = jnp.bitwise_and(row, 7)
        return sum(
            dot_nn(jnp.where(index == j, left, 0.0).astype(BF16), right[j]) for j in range(part)
        )

    terms = (times(ds_row, k_w), times(ds_key, q_w), times(p_key, g_w))
    lane = iota((8, dh), 1)
    for ref, base, columns in ((mine_ref, 0, of_me + of_mate), (theirs_ref, 8, of_mate + of_me)):
        for i, term in enumerate(terms):
            ref[8 * i : 8 * i + 8, :] = term[base : base + 8, :]
        table = jnp.zeros((8, dh), F32)
        for i, value in enumerate(columns):
            table = jnp.where(lane == i, value, table)
        ref[24:32, :] = table


def final_kernel(
    heads, off_hbm, mine_ref, got_ref, own_ref, far_ref, s_ref, dp_ref,
    k_ref, kf_ref, ret, dki, dvi, far_hbm, dq_in, dq_ref, dk_ref, dv_ref,
    off_ref, far_scores, full, blocks, dko, dvo, off_sem, far_sem, block_sems, write_sems,
):
    offsets = pltpu.make_async_copy(off_hbm, off_ref, off_sem)
    offsets.start()
    scores = pltpu.make_async_copy(far_hbm, far_scores, far_sem)
    scores.start()
    length, dh = k_ref.shape[0], own_ref.shape[1]
    half, part = length // 2, heads // 2
    scale = dh**-0.5

    def place(ref, h):
        base = pl.multiple_of(jnp.bitwise_and(off_ref[1, h], ~15), 16)
        return ref.at[pl.ds(base, 16), pl.ds(h * dh, dh)]

    chunks = [slice(2 * j * dh, 2 * (j + 1) * dh) for j in range(part)]
    own, far = own_ref[...].astype(F32), far_ref[...].astype(F32)
    first = jnp.bitwise_and(lax.axis_index("ctx"), 1) == 0
    mine, got = mine_ref[...], got_ref[...]
    low, high = jnp.where(first, mine, got), jnp.where(first, got, mine)
    full[...] = jnp.zeros_like(full)
    for i in range(4):
        full[16 * i : 16 * i + part, :] = low[8 * i : 8 * i + part, :]
        full[16 * i + part : 16 * i + heads, :] = high[8 * i : 8 * i + part, :]
    dq_wide, dk_rows, dv_rows, table = [full[16 * i : 16 * i + 16, :] for i in range(4)]
    m_me, i_me, d_me = [table[:, i : i + 1] for i in range(3)]
    m_two, i_two, d_two = [
        jnp.concatenate([table[:, i : i + 1], table[:, i + 3 : i + 4]], axis=0) for i in range(3)
    ]
    offsets.wait()
    reads = [
        pltpu.make_async_copy(place(dq_in, h), blocks.at[h], block_sems.at[h]) for h in range(heads)
    ]
    for copy in reads:
        copy.start()
    weight = row_weights(off_ref, heads, length)
    p_two = jnp.exp2(jnp.where(weight > 0.0, s_ref[...] - m_two, NEG)) * weight * i_two
    ds_two = scale * p_two * (dp_ref[...] - d_two)
    met = level_one_keys(off_ref, heads, 16, length)
    scores.wait()
    p_far = jnp.exp2(jnp.where(met, far_scores[:16, :] - m_me, NEG)) * i_me
    ds_far = scale * p_far * (far_scores[16:, :] - d_me)
    dq_rows = dq_wide + own_columns(
        dot_nn(ds_two[0:16, :].astype(BF16), k_ref[...]) + dot_nn(ds_far.astype(BF16), kf_ref[...]),
        heads,
    )
    wide = offset_column(off_ref, 1, heads, 32)
    spot = (iota((32, length), 1) == wide).astype(F32)

    def spread(left, first, rows):
        high = rows.astype(BF16).astype(F32)
        left = jnp.concatenate([left, spot], axis=0).T.astype(BF16)
        parts = (own[first : first + 16, :], far[first : first + 16, :], high, rows - high)
        return left, jnp.concatenate([block_rows(part, heads) for part in parts], axis=0)

    writes = []
    for index, (base, out, out_ref, left, right) in enumerate(
        (
            (dki, dko, dk_ref) + spread(ds_two, 0, dk_rows),
            (dvi, dvo, dv_ref) + spread(p_two, 16, dv_rows),
        )
    ):
        back = slice(index * half, (index + 1) * half)
        for j, chunk in enumerate(chunks):
            for h in (2 * j, 2 * j + 1):
                cols = slice(h * dh, (h + 1) * dh)
                pick = iota((length, half), 0) == 2 * iota((length, half), 1) + off_ref[0, h]
                added = dot_nn(left, right[:, cols]) + dot_nn(pick.astype(BF16), ret[back, cols])
                out[:, cols] = (base[:, cols] + added).astype(BF16)
            sem = write_sems.at[index, j]
            copy = pltpu.make_async_copy(out.at[:, chunk], out_ref.at[:, chunk], sem)
            copy.start()
            writes.append(copy)
    for h in range(heads):
        reads[h].wait()
        here = iota((16, dh), 0) == jnp.bitwise_and(off_ref[1, h], 15)
        blocks[h] = jnp.where(here, dq_rows[h : h + 1, :], blocks[h].astype(F32)).astype(BF16)
        copy = pltpu.make_async_copy(blocks.at[h], place(dq_ref, h), block_sems.at[h])
        copy.start()
        writes.append(copy)
    for copy in writes:
        copy.wait()


def on_device(query, key, value, grad_out, offsets):
    length, width = query.shape
    heads = offsets.shape[1]
    dh = width // heads
    size = lax.axis_size("ctx")
    span = min(size, 128)
    slots = 2 * heads + STAT_ROWS
    mates = [(i, i ^ 1) for i in range(size)]
    vmem = pl.BlockSpec(memory_space=pltpu.VMEM)
    smem = pl.BlockSpec(memory_space=pltpu.SMEM)
    hbm = pl.BlockSpec(memory_space=pltpu.HBM)
    params = pltpu.CompilerParams(vmem_limit_bytes=VMEM_LIMIT)
    small = pl.CostEstimate(flops=1000, bytes_accessed=1000, transcendentals=0)
    large = pl.CostEstimate(flops=7 * 10**9, bytes_accessed=1000, transcendentals=0)

    def call(kernel, name, out_shape, in_specs, out_specs, scratch, cost=small, **kwargs):
        return pl.pallas_call(
            kernel,
            out_shape=out_shape,
            in_specs=in_specs,
            out_specs=out_specs,
            scratch_shapes=scratch,
            compiler_params=params,
            cost_estimate=cost,
            name=name,
            **kwargs,
        )

    def far_memory(*arrays):
        return [pltpu.with_memory_space_constraint(array, pltpu.HBM) for array in arrays]

    def near_memory(*arrays):
        return [pltpu.with_memory_space_constraint(array, pltpu.VMEM) for array in arrays]

    own = call(
        functools.partial(pack_kernel, heads),
        "pack_rows",
        pltpu.VMEM((32, dh), BF16),
        [smem] + [hbm] * 2,
        vmem,
        [
            pltpu.VMEM((2 * heads, 16, dh), BF16),
            pltpu.VMEM((32, dh), F32),
            pltpu.SemaphoreType.DMA((2 * heads,)),
        ],
    )(*far_memory(offsets, query, grad_out))
    far = lax.ppermute(own, "ctx", mates)
    key_far = lax.ppermute(key, "ctx", mates)
    value_far = lax.ppermute(value, "ctx", mates)
    repeat = min(span, 8)
    load, s_rows, dp_rows = call(
        functools.partial(stats_kernel, heads, span),
        "row_stats",
        (
            pltpu.HBM((span, slots, dh), BF16),
            pltpu.VMEM((32, length), F32),
            pltpu.VMEM((32, length), F32),
        ),
        [hbm] + [vmem] * 4,
        (hbm, vmem, vmem),
        [
            pltpu.SMEM(offsets.shape, jnp.int32),
            pltpu.VMEM((2 * slots, dh), F32),
            pltpu.VMEM((repeat, slots, dh), BF16),
            pltpu.SemaphoreType.DMA,
            pltpu.SemaphoreType.DMA((span // repeat,)),
        ],
    )(*far_memory(offsets), *near_memory(own, far, key, value))
    groups = None
    if size > span:
        groups = [list(range(base, base + span)) for base in range(0, size, span)]
    received = lax.all_to_all(load, "ctx", 0, 0, axis_index_groups=groups, tiled=True)
    whole = pltpu.VMEM((length, width), BF16)
    wide = pltpu.VMEM((length, width), F32)
    rows = pltpu.VMEM((32, dh), F32)
    dq, dk, dv, partial, far_scores = call(
        functools.partial(main_kernel, heads),
        "near_levels",
        (
            pltpu.HBM((length, width), BF16),
            pltpu.HBM((length, width), F32),
            pltpu.HBM((length, width), F32),
            pltpu.HBM((length, width), BF16),
            pltpu.HBM((32, length), F32),
        ),
        [hbm] + [vmem] * 8,
        (hbm,) * 5,
        [
            pltpu.SMEM(offsets.shape, jnp.int32),
            whole,
            wide,
            wide,
            whole,
            pltpu.VMEM((32, length), F32),
            pltpu.SemaphoreType.DMA,
            pltpu.SemaphoreType.DMA,
            pltpu.SemaphoreType.DMA((heads // 2, 4)),
        ],
        cost=large,
    )(
        *far_memory(offsets),
        *near_memory(s_rows, own, query, key, value, grad_out, key_far, value_far),
    )
    returned = lax.ppermute(partial, "ctx", mates)
    mine, theirs = call(
        functools.partial(wide_kernel, heads, span),
        "third_level",
        (rows, rows),
        [vmem],
        (vmem,) * 2,
        [pltpu.VMEM((span * slots, dh), F32)],
        cost=large,
    )(*near_memory(received))
    got = lax.ppermute(theirs, "ctx", mates)
    return call(
        functools.partial(final_kernel, heads),
        "join",
        (pltpu.HBM((length, width), BF16),) * 3,
        [hbm] + [vmem] * 11 + [hbm] * 2,
        (hbm,) * 3,
        [
            pltpu.SMEM(offsets.shape, jnp.int32),
            pltpu.VMEM((32, length), F32),
            pltpu.VMEM((64, dh), F32),
            pltpu.VMEM((heads, 16, dh), BF16),
            whole,
            whole,
            pltpu.SemaphoreType.DMA,
            pltpu.SemaphoreType.DMA,
            pltpu.SemaphoreType.DMA((heads,)),
            pltpu.SemaphoreType.DMA((2, heads // 2)),
        ],
        input_output_aliases={13: 0},
    )(
        *far_memory(offsets),
        *near_memory(mine, got, own, far, s_rows, dp_rows),
        *near_memory(key, key_far, returned, dk, dv),
        *far_memory(far_scores, dq),
    )


def solution(mesh):
    placed = (P("ctx", None), P("ctx", None), P("ctx", None), P("ctx", None), P())
    return jax.shard_map(
        on_device,
        mesh=mesh,
        in_specs=placed,
        out_specs=(P("ctx", None), P("ctx", None), P("ctx", None)),
        check_vma=False,
    )
```

profile of v0, /device:TPU:0, one launch (start us, length us, event | category | flops | bytes accessed | tf_op | source)
XLA Modules:
  0.0 28.6 jit_solution(15734024331381862252)
XLA Ops:
  0.6 0.0 copy-start.7
  0.6 0.0 copy-start
  0.7 0.0 copy-start.6
  0.7 0.0 copy-start.5
  0.7 0.5 %collective-permute-start.3 = (bf16[256,1280]{1,0:T(8,128)(2,1)}, bf16[256,1280]{1,0:T(8,128)(2,1)}, u32[]{:S(2)}, u32[]{:S(2)}) collective-permute-start(bf16[256,1280]{1,0:T(8,128)(2,1)} %v_ref.3), channel_id=1, source_target_pairs={{0,1},{1,0},{2,3},{3,2},{4,5},{5,4},{6,7},{7,6},{8,9},{9,8},{10,11... | collective-permute-start | bytes 1966088 | tf_op jit(solution)/shard_map/ppermute | solution.py:475
  1.2 0.1 collective-permute-start.2
  1.3 2.0 %pack_rows.1.own_ref = bf16[32,128]{1,0:T(8,128)(2,1)S(1)} custom-call(s32[2,10]{1,0:T(2,128)} %off_hbm.5, bf16[256,1280]{1,0:T(8,128)(2,1)} %q_ref.3, bf16[256,1280]{1,0:T(8,128)(2,1)} %g_ref.3), custom_call_target="tpu_custom_call" | custom-call | flops 1000 | bytes 1000 | tf_op jit(solution)/shard_map/pack_rows/pallas_call | solution.py:461
  3.2 0.5 %collective-permute-start = (bf16[32,128]{1,0:T(8,128)(2,1)S(1)}, bf16[32,128]{1,0:T(8,128)(2,1)S(1)}, u32[]{:S(2)}, u32[]{:S(2)}) collective-permute-start(bf16[32,128]{1,0:T(8,128)(2,1)S(1)} %pack_rows.1.own_ref), channel_id=1, source_target_pairs={{0,1},{1,0},{2,3},{3,2},{4,5},{5,4},{6,7},{7,6},{8,9},{9,8},{10,11... | collective-permute-start | bytes 24584 | tf_op jit(solution)/shard_map/ppermute | solution.py:473
  3.7 0.8 %collective-permute-done.far_ref = bf16[32,128]{1,0:T(8,128)(2,1)S(1)} collective-permute-done((bf16[32,128]{1,0:T(8,128)(2,1)S(1)}, bf16[32,128]{1,0:T(8,128)(2,1)S(1)}, u32[]{:S(2)}, u32[]{:S(2)}) %collective-permute-start) | collective-permute-done | bytes 8224 | tf_op jit(solution)/shard_map/ppermute | solution.py:473
  4.6 0.0 copy-done.7
  4.6 2.1 %row_stats.1 = (bf16[32,24,128]{2,1,0:T(8,128)(2,1)}, f32[32,256]{1,0:T(8,128)S(1)}, f32[32,256]{1,0:T(8,128)S(1)}) custom-call(s32[2,10]{1,0:T(2,128)} %off_hbm.5, bf16[32,128]{1,0:T(8,128)(2,1)S(1)} %pack_rows.1.own_ref, bf16[32,128]{1,0:T(8,128)(2,1)S(1)} %collective-permute-done.far_ref, bf16[256,1280]{1,0:T(8,128)(2,1)S(1)} %copy-done, ...), custom_call_target="tpu_custom_call" | custom-call | flops 1000 | bytes 1000 | tf_op jit(solution)/shard_map/row_stats/pallas_call | solution.py:477
  6.6 7.2 %all-to-all-start = ((bf16[32,24,128]{2,1,0:T(8,128)(2,1)}), bf16[32,24,128]{2,1,0:T(8,128)(2,1)S(1)}, u32[]{:S(2)}, u32[]{:S(2)}) async-start(bf16[32,24,128]{2,1,0:T(8,128)(2,1)} %get-tuple-element.13), calls=%async_computation | async-start | bytes 393216 | tf_op jit(solution)/shard_map/all_to_all | solution.py:498
  13.8 0.0 collective-permute-done.3.vf_ref
  13.8 0.0 collective-permute-done.2.kf_ref
  13.9 0.0 copy-start.3
  13.9 7.6 %near_levels.1 = (bf16[256,1280]{1,0:T(8,128)(2,1)}, f32[256,1280]{1,0:T(8,128)}, f32[256,1280]{1,0:T(8,128)}, bf16[256,1280]{1,0:T(8,128)(2,1)}, f32[32,256]{1,0:T(8,128)}) custom-call(s32[2,10]{1,0:T(2,128)} %off_hbm.5, f32[32,256]{1,0:T(8,128)S(1)} %get-tuple-element.16.after_ref.s_ref, bf16[32,128]{1,0:T(8,128)(2,1)S(1)} %pack_rows.1.own_ref, ...), custom_call_target="tpu_custom_call" | custom-call | flops 7000000000 | bytes 1000 | tf_op jit(solution)/shard_map/near_levels/pallas_call | solution.py:502
  21.5 0.3 %collective-permute-start.4 = (bf16[256,1280]{1,0:T(8,128)(2,1)}, bf16[256,1280]{1,0:T(8,128)(2,1)}, u32[]{:S(2)}, u32[]{:S(2)}) collective-permute-start(bf16[256,1280]{1,0:T(8,128)(2,1)} %get-tuple-element.18), channel_id=1, source_target_pairs={{0,1},{1,0},{2,3},{3,2},{4,5},{5,4},{6,7},{7,6},{8,9},{9,8},{10,11... | collective-permute-start | bytes 1966088 | tf_op jit(solution)/shard_map/ppermute | solution.py:530
  21.9 0.9 %all-to-all-done.recv_ref = bf16[32,24,128]{2,1,0:T(8,128)(2,1)S(1)} async-done(((bf16[32,24,128]{2,1,0:T(8,128)(2,1)}), bf16[32,24,128]{2,1,0:T(8,128)(2,1)S(1)}, u32[]{:S(2)}, u32[]{:S(2)}) %all-to-all-start) | async-done | bytes 196640 | tf_op jit(solution)/shard_map/all_to_all | solution.py:498
  22.7 0.6 %third_level.1 = (f32[32,128]{1,0:T(8,128)S(1)}, f32[32,128]{1,0:T(8,128)S(1)}) custom-call(bf16[32,24,128]{2,1,0:T(8,128)(2,1)S(1)} %all-to-all-done.recv_ref), custom_call_target="tpu_custom_call" | custom-call | flops 7000000000 | bytes 1000 | tf_op jit(solution)/shard_map/third_level/pallas_call | solution.py:531
  23.4 0.6 %collective-permute-start.1 = (f32[32,128]{1,0:T(8,128)S(1)}, f32[32,128]{1,0:T(8,128)S(1)}, u32[]{:S(2)}, u32[]{:S(2)}) collective-permute-start(f32[32,128]{1,0:T(8,128)S(1)} %get-tuple-element.15), channel_id=1, source_target_pairs={{0,1},{1,0},{2,3},{3,2},{4,5},{5,4},{6,7},{7,6},{8,9},{9,8},{10,11... | collective-permute-start | bytes 49160 | tf_op jit(solution)/shard_map/ppermute | solution.py:540
  24.0 0.8 %collective-permute-done.1.got_ref = f32[32,128]{1,0:T(8,128)S(1)} collective-permute-done((f32[32,128]{1,0:T(8,128)S(1)}, f32[32,128]{1,0:T(8,128)S(1)}, u32[]{:S(2)}, u32[]{:S(2)}) %collective-permute-start.1) | collective-permute-done | bytes 16416 | tf_op jit(solution)/shard_map/ppermute | solution.py:540
  24.8 0.0 collective-permute-done.4.ret
  24.8 0.0 copy-done.1
  24.8 3.7 %join.1 = (bf16[256,1280]{1,0:T(8,128)(2,1)}, bf16[256,1280]{1,0:T(8,128)(2,1)}, bf16[256,1280]{1,0:T(8,128)(2,1)}) custom-call(s32[2,10]{1,0:T(2,128)} %off_hbm.5, f32[32,128]{1,0:T(8,128)S(1)} %get-tuple-element.14.mine_ref, f32[32,128]{1,0:T(8,128)S(1)} %collective-permute-done.1.got_ref, ...), custom_call_target="tpu_custom_call", output_to_operand_aliasing={{0}: (13, {})} | custom-call | flops 1000 | bytes 1000 | tf_op jit(solution)/shard_map/join/pallas_call | solution.py:541
  (9 shorter events, 0.0 us)
Async XLA Ops:
  0.6 3.9 %copy-start.7 = (bf16[256,1280]{1,0:T(8,128)(2,1)S(1)}, bf16[256,1280]{1,0:T(8,128)(2,1)}, u32[]{:S(2)}) copy-start(bf16[256,1280]{1,0:T(8,128)(2,1)} %v_ref.3) | copy-start | bytes 1966084
  0.6 3.9 %copy-start = (bf16[256,1280]{1,0:T(8,128)(2,1)S(1)}, bf16[256,1280]{1,0:T(8,128)(2,1)}, u32[]{:S(2)}) copy-start(bf16[256,1280]{1,0:T(8,128)(2,1)} %k_ref.5) | copy-start | bytes 1966084
  0.7 13.2 %copy-start.6 = (bf16[256,1280]{1,0:T(8,128)(2,1)S(1)}, bf16[256,1280]{1,0:T(8,128)(2,1)}, u32[]{:S(2)}) copy-start(bf16[256,1280]{1,0:T(8,128)(2,1)} %g_ref.3) | copy-start | bytes 1966084
  0.7 13.2 %copy-start.5 = (bf16[256,1280]{1,0:T(8,128)(2,1)S(1)}, bf16[256,1280]{1,0:T(8,128)(2,1)}, u32[]{:S(2)}) copy-start(bf16[256,1280]{1,0:T(8,128)(2,1)} %q_ref.3) | copy-start | bytes 1966084
  0.7 13.2 %collective-permute-start.3 = (bf16[256,1280]{1,0:T(8,128)(2,1)}, bf16[256,1280]{1,0:T(8,128)(2,1)}, u32[]{:S(2)}, u32[]{:S(2)}) collective-permute-start(bf16[256,1280]{1,0:T(8,128)(2,1)} %v_ref.3), channel_id=1, source_target_pairs={{0,1},{1,0},{2,3},{3,2},{4,5},{5,4},{6,7},{7,6},{8,9},{9,8},{10,11... | collective-permute-start | bytes 1966088 | tf_op jit(solution)/shard_map/ppermute | solution.py:475
  1.2 12.7 %collective-permute-start.2 = (bf16[256,1280]{1,0:T(8,128)(2,1)}, bf16[256,1280]{1,0:T(8,128)(2,1)S(1)}, u32[]{:S(2)}, u32[]{:S(2)}) collective-permute-start(bf16[256,1280]{1,0:T(8,128)(2,1)} %k_ref.5), channel_id=1, source_target_pairs={{0,1},{1,0},{2,3},{3,2},{4,5},{5,4},{6,7},{7,6},{8,9},{9,8},{10,11... | collective-permute-start | bytes 1966088 | tf_op jit(solution)/shard_map/ppermute | solution.py:474
  3.2 1.3 %collective-permute-start = (bf16[32,128]{1,0:T(8,128)(2,1)S(1)}, bf16[32,128]{1,0:T(8,128)(2,1)S(1)}, u32[]{:S(2)}, u32[]{:S(2)}) collective-permute-start(bf16[32,128]{1,0:T(8,128)(2,1)S(1)} %pack_rows.1.own_ref), channel_id=1, source_target_pairs={{0,1},{1,0},{2,3},{3,2},{4,5},{5,4},{6,7},{7,6},{8,9},{9,8},{10,11... | collective-permute-start | bytes 24584 | tf_op jit(solution)/shard_map/ppermute | solution.py:473
  6.6 16.1 %all-to-all-start = ((bf16[32,24,128]{2,1,0:T(8,128)(2,1)}), bf16[32,24,128]{2,1,0:T(8,128)(2,1)S(1)}, u32[]{:S(2)}, u32[]{:S(2)}) async-start(bf16[32,24,128]{2,1,0:T(8,128)(2,1)} %get-tuple-element.13), calls=%async_computation | async-start | bytes 393216 | tf_op jit(solution)/shard_map/all_to_all | solution.py:498
  13.9 7.7 %copy-start.3 = (bf16[256,1280]{1,0:T(8,128)(2,1)}, bf16[256,1280]{1,0:T(8,128)(2,1)S(1)}, u32[]{:S(2)}) copy-start(bf16[256,1280]{1,0:T(8,128)(2,1)S(1)} %collective-permute-done.2.kf_ref) | copy-start | bytes 1966084
  21.5 3.3 %copy-start.1 = (f32[256,1280]{1,0:T(8,128)S(1)}, f32[256,1280]{1,0:T(8,128)}, u32[]{:S(2)}) copy-start(f32[256,1280]{1,0:T(8,128)} %get-tuple-element.19.dki) | copy-start | bytes 3932164
  21.5 3.3 %copy-start.2 = (f32[256,1280]{1,0:T(8,128)S(1)}, f32[256,1280]{1,0:T(8,128)}, u32[]{:S(2)}) copy-start(f32[256,1280]{1,0:T(8,128)} %get-tuple-element.20.dvi) | copy-start | bytes 3932164
  21.5 3.3 %collective-permute-start.4 = (bf16[256,1280]{1,0:T(8,128)(2,1)}, bf16[256,1280]{1,0:T(8,128)(2,1)}, u32[]{:S(2)}, u32[]{:S(2)}) collective-permute-start(bf16[256,1280]{1,0:T(8,128)(2,1)} %get-tuple-element.18), channel_id=1, source_target_pairs={{0,1},{1,0},{2,3},{3,2},{4,5},{5,4},{6,7},{7,6},{8,9},{9,8},{10,11... | collective-permute-start | bytes 1966088 | tf_op jit(solution)/shard_map/ppermute | solution.py:530
  22.7 2.1 %copy-start.4 = (bf16[256,1280]{1,0:T(8,128)(2,1)S(1)}, bf16[256,1280]{1,0:T(8,128)(2,1)}, u32[]{:S(2)}) copy-start(bf16[256,1280]{1,0:T(8,128)(2,1)} %copy-done.3) | copy-start | bytes 1966084
  23.4 1.5 %collective-permute-start.1 = (f32[32,128]{1,0:T(8,128)S(1)}, f32[32,128]{1,0:T(8,128)S(1)}, u32[]{:S(2)}, u32[]{:S(2)}) collective-permute-start(f32[32,128]{1,0:T(8,128)S(1)} %get-tuple-element.15), channel_id=1, source_target_pairs={{0,1},{1,0},{2,3},{3,2},{4,5},{5,4},{6,7},{7,6},{8,9},{9,8},{10,11... | collective-permute-start | bytes 49160 | tf_op jit(solution)/shard_map/ppermute | solution.py:540
where the time goes:
time: 29 us; the launch traced here: 28.6 us
  Pallas kernels  16 us (55%)
  starting transfers between devices  9.22 us (32%)
  waiting for transfers between devices  2.54 us (9%)
  between operations  0.77 us (3%)
    pallas_call x1, Pallas kernels, on_device(): call(functools.partial(main_kernel, heads), 'near_levels', (pltpu.HBM((le...  7.61 us
    all_to_all x1, starting transfers between devices, on_device(): lax.all_to_all(load, 'ctx', 0, 0, axis_index_groups=groups, tiled=True)  7.19 us
    pallas_call x1, Pallas kernels, on_device(): call(functools.partial(final_kernel, heads), 'join', (pltpu.HBM((length,...  3.74 us
    pallas_call x1, Pallas kernels, on_device(): call(functools.partial(stats_kernel, heads, span), 'row_stats', (pltpu.HB...  2.05 us
    pallas_call x1, Pallas kernels, on_device(): call(functools.partial(pack_kernel, heads), 'pack_rows', pltpu.VMEM((32,...  1.97 us
    all_to_all x1, waiting for transfers between devices, on_device(): lax.all_to_all(load, 'ctx', 0, 0, axis_index_groups=groups, tiled=True)  0.87 us
    ppermute x1, waiting for transfers between devices, on_device(): got = lax.ppermute(theirs, 'ctx', mates)  0.84 us
    ppermute x1, waiting for transfers between devices, on_device(): far = lax.ppermute(own, 'ctx', mates)  0.83 us
  transfers between devices with their start and end apart: 6, of which 3 were waited for; matrix products, arithmetic and copies ran while one was open for 0% of the time, Pallas kernels for 43%

commit v1 on v0

--- a/solution.py
+++ b/solution.py
@@ -67,10 +67,12 @@
     return jnp.where(iota((32, length), 0) < 16, 1.0 + both, both)
 
 
-def pack_kernel(heads, off_ref, q_ref, g_ref, out_ref, buf, acc, sems):
-    dh = out_ref.shape[1]
+def pack_kernel(
+    heads, off_ref, k_ref, v_ref, q_ref, g_ref, out_ref, spot_ref, weight_ref, buf, acc, sems
+):
+    length, dh = k_ref.shape[0], out_ref.shape[1]
     copies = []
-    for s, ref in enumerate((q_ref, g_ref)):
+    for s, ref in enumerate((k_ref, v_ref, q_ref, g_ref)):
         for h in range(heads):
             base = pl.multiple_of(jnp.bitwise_and(off_ref[1, h], ~15), 16)
             slot = s * heads + h
@@ -79,55 +81,46 @@
             )
             copy.start()
             copies.append(copy)
+    wide = offset_column(off_ref, 1, heads, 32)
+    spot_ref[...] = (iota((32, length), 1) == wide).astype(F32)
+    weight_ref[...] = row_weights(off_ref, heads, length)
     acc[...] = jnp.zeros_like(acc)
     row = iota((16, dh), 0)
-    for s in range(2):
+    for s in range(4):
         for h in range(heads):
             slot = s * heads + h
             copies[slot].wait()
             own = row == jnp.bitwise_and(off_ref[1, h], 15)
             block = jnp.where(own, buf[slot].astype(F32), 0.0)
-            acc[16 * s + h : 16 * s + h + 1, :] = jnp.sum(block, axis=0, keepdims=True)
+            acc[slot : slot + 1, :] = jnp.sum(block, axis=0, keepdims=True)
     out_ref[...] = acc[...].astype(BF16)
 
 
 def stats_kernel(
-    heads, span, off_hbm, own_ref, far_ref, k_ref, v_ref, load_ref, s_ref, dp_ref,
-    off_ref, acc, load, off_sem, sems,
+    heads, span, own_ref, spot_ref, weight_ref, qf_ref, gf_ref, k_ref, v_ref,
+    load_ref, s_hbm, dp_hbm, far_hbm, s_ref, dp_ref, far_ref, acc, load, sems, row_sems,
 ):
-    offsets = pltpu.make_async_copy(off_hbm, off_ref, off_sem)
-    offsets.start()
     dh = own_ref.shape[1]
-    length = k_ref.shape[0]
-    own, far = own_ref[...].astype(F32), far_ref[...].astype(F32)
-
-    def both_rows(first):
-        return jnp.concatenate(
-            [block_rows(rows[first : first + 16, :], heads) for rows in (own, far)], axis=0
-        )
-
-    s = dot_nt(both_rows(0), k_ref[...]) * (dh**-0.5 * LOG2E)
-    dp = dot_nt(both_rows(16), v_ref[...])
+    part, slots = heads // 2, load_ref.shape[1]
+    own = own_ref[...].astype(F32)
+    spot = spot_ref[0:16, :].astype(BF16)
+
+    def both_rows(array, whole, first):
+        far = own_columns(dot_nn(spot, whole), heads)
+        far_ref[first : first + 16, :] = far.astype(BF16)
+        near = own[array * heads : array * heads + 16, :]
+        return jnp.concatenate([block_rows(near, heads), block_rows(far, heads)], axis=0)
+
+    queries, grads = both_rows(2, qf_ref[...], 0), both_rows(3, gf_ref[...], 16)
+    s = dot_nt(queries, k_ref[...]) * (dh**-0.5 * LOG2E)
+    dp = dot_nt(grads, v_ref[...])
     s_ref[...] = s
     dp_ref[...] = dp
-    offsets.wait()
-    part, slots = heads // 2, load_ref.shape[1]
-
-    def slot(array, h):
-        return (h // part) * slots + array * part + h % part
-
-    place = iota((16, dh), 0)
-    for i, ref in enumerate((k_ref, v_ref)):
-        for h in range(heads):
-            base = pl.multiple_of(jnp.bitwise_and(off_ref[1, h], ~15), 16)
-            block = ref[pl.ds(base, 16), h * dh : (h + 1) * dh].astype(F32)
-            block = jnp.where(place == jnp.bitwise_and(off_ref[1, h], 15), block, 0.0)
-            acc[slot(i, h) : slot(i, h) + 1, :] = jnp.sum(block, axis=0, keepdims=True)
-    for i, first in ((2, 0), (3, 16)):
+    for i in range(4):
         for c in range(2):
-            row = slot(i, c * part)
-            acc[row : row + part, :] = own[first + c * part : first + (c + 1) * part, :]
-    weight = row_weights(off_ref, heads, length)
+            slot, row = c * slots + i * part, i * heads + c * part
+            acc[slot : slot + part, :] = own[row : row + part, :]
+    weight = weight_ref[...]
     masked = jnp.where(weight > 0.0, s, NEG)
     m = jnp.max(masked, axis=1, keepdims=True)
     e = jnp.exp2(masked - m) * weight
@@ -151,6 +144,8 @@
         pltpu.make_async_copy(load, load_ref.at[pl.ds(i * repeat, repeat)], sems.at[i])
         for i in range(span // repeat)
     ]
+    for i, (near, away) in enumerate(((s_ref, s_hbm), (dp_ref, dp_hbm), (far_ref, far_hbm))):
+        copies.append(pltpu.make_async_copy(near, away, row_sems.at[i]))
     for copy in copies:
         copy.start()
     for copy in copies:
@@ -239,7 +234,8 @@
                 next(work[h])
         if turn == steps:
             own = own_ref[...].astype(F32)
-            queries, grads = block_rows(own[:16, :], heads), block_rows(own[16:, :], heads)
+            queries = block_rows(own[2 * heads : 2 * heads + 16, :], heads)
+            grads = block_rows(own[3 * heads : 3 * heads + 16, :], heads)
             far_scores[:16, :] = dot_nt(queries, kf_ref[...]) * (dh**-0.5 * LOG2E)
             far_scores[16:, :] = dot_nt(grads, vf_ref[...])
             copy = pltpu.make_async_copy(far_scores, far_hbm, far_sem)
@@ -339,9 +335,9 @@
 
 
 def final_kernel(
-    heads, off_hbm, mine_ref, got_ref, own_ref, far_ref, s_ref, dp_ref,
-    k_ref, kf_ref, ret, dki, dvi, far_hbm, dq_in, dq_ref, dk_ref, dv_ref,
-    off_ref, far_scores, full, blocks, dko, dvo, off_sem, far_sem, block_sems, write_sems,
+    heads, off_hbm, mine_ref, got_ref, own_ref, far_ref, spot_ref, weight_ref, s_ref, dp_ref,
+    k_ref, kf_ref, dki, dvi, ret_hbm, far_hbm, dq_in, dq_ref, dk_ref, dv_ref,
+    off_ref, ret, far_scores, full, blocks, dko, dvo, off_sem, far_sem, ret_sems, block_sems, write_sems,
 ):
     offsets = pltpu.make_async_copy(off_hbm, off_ref, off_sem)
     offsets.start()
@@ -356,6 +352,12 @@
         return ref.at[pl.ds(base, 16), pl.ds(h * dh, dh)]
 
     chunks = [slice(2 * j * dh, 2 * (j + 1) * dh) for j in range(part)]
+    fetches = [
+        pltpu.make_async_copy(ret_hbm.at[:, cols], ret.at[:, cols], ret_sems.at[j])
+        for j, cols in enumerate(chunks)
+    ]
+    for copy in fetches:
+        copy.start()
     own, far = own_ref[...].astype(F32), far_ref[...].astype(F32)
     first = jnp.bitwise_and(lax.axis_index("ctx"), 1) == 0
     mine, got = mine_ref[...], got_ref[...]
@@ -369,16 +371,10 @@
     m_two, i_two, d_two = [
         jnp.concatenate([table[:, i : i + 1], table[:, i + 3 : i + 4]], axis=0) for i in range(3)
     ]
-    offsets.wait()
-    reads = [
-        pltpu.make_async_copy(place(dq_in, h), blocks.at[h], block_sems.at[h]) for h in range(heads)
-    ]
-    for copy in reads:
-        copy.start()
-    weight = row_weights(off_ref, heads, length)
+    weight = weight_ref[...]
     p_two = jnp.exp2(jnp.where(weight > 0.0, s_ref[...] - m_two, NEG)) * weight * i_two
     ds_two = scale * p_two * (dp_ref[...] - d_two)
-    met = level_one_keys(off_ref, heads, 16, length)
+    met = weight[0:16, :] > 1.0
     scores.wait()
     p_far = jnp.exp2(jnp.where(met, far_scores[:16, :] - m_me, NEG)) * i_me
     ds_far = scale * p_far * (far_scores[16:, :] - d_me)
@@ -386,24 +382,32 @@
         dot_nn(ds_two[0:16, :].astype(BF16), k_ref[...]) + dot_nn(ds_far.astype(BF16), kf_ref[...]),
         heads,
     )
-    wide = offset_column(off_ref, 1, heads, 32)
-    spot = (iota((32, length), 1) == wide).astype(F32)
-
-    def spread(left, first, rows):
+    spot = spot_ref[...]
+    offsets.wait()
+    reads = [
+        pltpu.make_async_copy(place(dq_in, h), blocks.at[h], block_sems.at[h]) for h in range(heads)
+    ]
+    for copy in reads:
+        copy.start()
+
+    def spread(left, array, rows):
+        near = own[(array + 2) * heads : (array + 2) * heads + 16, :]
         high = rows.astype(BF16).astype(F32)
         left = jnp.concatenate([left, spot], axis=0).T.astype(BF16)
-        parts = (own[first : first + 16, :], far[first : first + 16, :], high, rows - high)
+        parts = (near, far[16 * array : 16 * array + 16, :], high, rows - high)
         return left, jnp.concatenate([block_rows(part, heads) for part in parts], axis=0)
 
     writes = []
     for index, (base, out, out_ref, left, right) in enumerate(
         (
             (dki, dko, dk_ref) + spread(ds_two, 0, dk_rows),
-            (dvi, dvo, dv_ref) + spread(p_two, 16, dv_rows),
+            (dvi, dvo, dv_ref) + spread(p_two, 1, dv_rows),
         )
     ):
         back = slice(index * half, (index + 1) * half)
         for j, chunk in enumerate(chunks):
+            if index == 0:
+                fetches[j].wait()
             for h in (2 * j, 2 * j + 1):
                 cols = slice(h * dh, (h + 1) * dh)
                 pick = iota((length, half), 0) == 2 * iota((length, half), 1) + off_ref[0, h]
@@ -458,40 +462,47 @@
     def near_memory(*arrays):
         return [pltpu.with_memory_space_constraint(array, pltpu.VMEM) for array in arrays]
 
-    own = call(
+    query_far = lax.ppermute(query, "ctx", mates)
+    grad_far = lax.ppermute(grad_out, "ctx", mates)
+    table = pltpu.VMEM((32, length), F32)
+    own, spot, weight = call(
         functools.partial(pack_kernel, heads),
         "pack_rows",
-        pltpu.VMEM((32, dh), BF16),
-        [smem] + [hbm] * 2,
-        vmem,
+        (pltpu.VMEM((48, dh), BF16), table, table),
+        [smem] + [hbm] * 4,
+        (vmem,) * 3,
         [
-            pltpu.VMEM((2 * heads, 16, dh), BF16),
-            pltpu.VMEM((32, dh), F32),
-            pltpu.SemaphoreType.DMA((2 * heads,)),
+            pltpu.VMEM((4 * heads, 16, dh), BF16),
+            pltpu.VMEM((48, dh), F32),
+            pltpu.SemaphoreType.DMA((4 * heads,)),
         ],
-    )(*far_memory(offsets, query, grad_out))
-    far = lax.ppermute(own, "ctx", mates)
-    key_far = lax.ppermute(key, "ctx", mates)
-    value_far = lax.ppermute(value, "ctx", mates)
+        cost=large,
+    )(*far_memory(offsets, key, value, query, grad_out))
+    key_later, value_later, own = lax.optimization_barrier((key, value, own))
+    key_far = lax.ppermute(key_later, "ctx", mates)
+    value_far = lax.ppermute(value_later, "ctx", mates)
     repeat = min(span, 8)
-    load, s_rows, dp_rows = call(
+    load, s_rows, dp_rows, far = call(
         functools.partial(stats_kernel, heads, span),
         "row_stats",
         (
             pltpu.HBM((span, slots, dh), BF16),
-            pltpu.VMEM((32, length), F32),
-            pltpu.VMEM((32, length), F32),
+            pltpu.HBM((32, length), F32),
+            pltpu.HBM((32, length), F32),
+            pltpu.HBM((32, dh), BF16),
         ),
-        [hbm] + [vmem] * 4,
-        (hbm, vmem, vmem),
+        [vmem] * 7,
+        (hbm,) * 4,
         [
-            pltpu.SMEM(offsets.shape, jnp.int32),
+            table,
+            table,
+            pltpu.VMEM((32, dh), BF16),
             pltpu.VMEM((2 * slots, dh), F32),
             pltpu.VMEM((repeat, slots, dh), BF16),
-            pltpu.SemaphoreType.DMA,
             pltpu.SemaphoreType.DMA((span // repeat,)),
+            pltpu.SemaphoreType.DMA((3,)),
         ],
-    )(*far_memory(offsets), *near_memory(own, far, key, value))
+    )(*near_memory(own, spot, weight, query_far, grad_far, key, value))
     groups = None
     if size > span:
         groups = [list(range(base, base + span)) for base in range(0, size, span)]
@@ -509,7 +520,7 @@
             pltpu.HBM((length, width), BF16),
             pltpu.HBM((32, length), F32),
         ),
-        [hbm] + [vmem] * 8,
+        [hbm] * 2 + [vmem] * 7,
         (hbm,) * 5,
         [
             pltpu.SMEM(offsets.shape, jnp.int32),
@@ -524,8 +535,8 @@
         ],
         cost=large,
     )(
-        *far_memory(offsets),
-        *near_memory(s_rows, own, query, key, value, grad_out, key_far, value_far),
+        *far_memory(offsets, s_rows),
+        *near_memory(own, query, key, value, grad_out, key_far, value_far),
     )
     returned = lax.ppermute(partial, "ctx", mates)
     mine, theirs = call(
@@ -542,10 +553,11 @@
         functools.partial(final_kernel, heads),
         "join",
         (pltpu.HBM((length, width), BF16),) * 3,
-        [hbm] + [vmem] * 11 + [hbm] * 2,
+        [hbm] + [vmem] * 12 + [hbm] * 3,
         (hbm,) * 3,
         [
             pltpu.SMEM(offsets.shape, jnp.int32),
+            whole,
             pltpu.VMEM((32, length), F32),
             pltpu.VMEM((64, dh), F32),
             pltpu.VMEM((heads, 16, dh), BF16),
@@ -553,15 +565,16 @@
             whole,
             pltpu.SemaphoreType.DMA,
             pltpu.SemaphoreType.DMA,
+            pltpu.SemaphoreType.DMA((heads // 2,)),
             pltpu.SemaphoreType.DMA((heads,)),
             pltpu.SemaphoreType.DMA((2, heads // 2)),
         ],
-        input_output_aliases={13: 0},
+        input_output_aliases={15: 0},
     )(
         *far_memory(offsets),
-        *near_memory(mine, got, own, far, s_rows, dp_rows),
-        *near_memory(key, key_far, returned, dk, dv),
-        *far_memory(far_scores, dq),
+        *near_memory(mine, got, own, far, spot, weight, s_rows, dp_rows),
+        *near_memory(key, key_far, dk, dv),
+        *far_memory(returned, far_scores, dq),
     )
 
 

time: 29 us -> 28.3 us (0.976)
  waiting for transfers between devices: 2.54 us -> 1.59 us
    ppermute x3 -> x4, waiting for transfers between devices: 0.83 us -> 0.01 us  [the longest x1 0.01 us: on_device(): query_far = lax.ppermute(query, 'ctx', mates)]
    pallas_call x1, Pallas kernels: 2.05 us -> 1.72 us  [on_device(): call(functools.partial(stats_kernel, heads, span), 'row_stats', (pltpu.HB...]
    ppermute x3 -> x4, starting transfers between devices: 1.09 us -> 1.18 us  [the longest x1 0.52 us: on_device(): query_far = lax.ppermute(query, 'ctx', mates)]
  transfers between devices with their start and end apart: 6 -> 7, of which waited for: 3 -> 2; matrix products, arithmetic and copies ran while one was open for 0% -> 0% of each run, Pallas kernels for 43% -> 44%
where the time goes in v1:
time: 28.3 us; the launch traced here: 28 us
  Pallas kernels  16.1 us (57%)
  starting transfers between devices  9.38 us (33%)
  waiting for transfers between devices  1.59 us (6%)
  between operations  0.8 us (3%)
    pallas_call x1, Pallas kernels, on_device(): call(functools.partial(main_kernel, heads), 'near_levels', (pltpu.HBM((le...  7.74 us
    all_to_all x1, starting transfers between devices, on_device(): lax.all_to_all(load, 'ctx', 0, 0, axis_index_groups=groups, tiled=True)  7.27 us
    pallas_call x1, Pallas kernels, on_device(): call(functools.partial(final_kernel, heads), 'join', (pltpu.HBM((length,...  3.81 us
    pallas_call x1, Pallas kernels, on_device(): call(functools.partial(pack_kernel, heads), 'pack_rows', (pltpu.VMEM((48,...  2.24 us
    pallas_call x1, Pallas kernels, on_device(): call(functools.partial(stats_kernel, heads, span), 'row_stats', (pltpu.HB...  1.72 us
    ppermute x1, waiting for transfers between devices, on_device(): got = lax.ppermute(theirs, 'ctx', mates)  0.84 us
    all_to_all x1, waiting for transfers between devices, on_device(): lax.all_to_all(load, 'ctx', 0, 0, axis_index_groups=groups, tiled=True)  0.74 us
    pallas_call x1, Pallas kernels, on_device(): call(functools.partial(wide_kernel, heads, span), 'third_level', (rows, r...  0.63 us
  transfers between devices with their start and end apart: 7, of which 2 were waited for; matrix products, arithmetic and copies ran while one was open for 0% of the time, Pallas kernels for 44%

profile of v1, /device:TPU:0, one launch (start us, length us, event | category | flops | bytes accessed | tf_op | source)
XLA Modules:
  0.0 28.0 jit_solution(7022307046352687848)
XLA Ops:
  0.6 0.0 copy-start
  0.7 0.5 %collective-permute-start = (bf16[256,1280]{1,0:T(8,128)(2,1)}, bf16[256,1280]{1,0:T(8,128)(2,1)S(1)}, u32[]{:S(2)}, u32[]{:S(2)}) collective-permute-start(bf16[256,1280]{1,0:T(8,128)(2,1)} %q_ref.3), channel_id=1, source_target_pairs={{0,1},{1,0},{2,3},{3,2},{4,5},{5,4},{6,7},{7,6},{8,9},{9,8},{10,11... | collective-permute-start | bytes 1966088 | tf_op jit(solution)/shard_map/ppermute | solution.py:465
  1.2 0.1 collective-permute-start.1
  1.2 2.2 %pack_rows.1 = (bf16[48,128]{1,0:T(8,128)(2,1)S(1)}, f32[32,256]{1,0:T(8,128)S(1)}, f32[32,256]{1,0:T(8,128)S(1)}) custom-call(s32[2,10]{1,0:T(2,128)} %off_hbm.3, bf16[256,1280]{1,0:T(8,128)(2,1)} %k_ref.7, bf16[256,1280]{1,0:T(8,128)(2,1)} %v_ref.5, bf16[256,1280]{1,0:T(8,128)(2,1)} %q_ref.3, bf16[256,1280]{1,0:T(8,128)(2,1)} %g_ref.3), custom_call_target="tpu_custom_call" | custom-call | flops 7000000000 | bytes 1000 | tf_op jit(solution)/shard_map/pack_rows/pallas_call | solution.py:468
  3.5 0.5 %collective-permute-start.3 = (bf16[256,1280]{1,0:T(8,128)(2,1)S(1)}, bf16[256,1280]{1,0:T(8,128)(2,1)S(1)}, u32[]{:S(2)}, u32[]{:S(2)}) collective-permute-start(bf16[256,1280]{1,0:T(8,128)(2,1)S(1)} %copy-done), channel_id=1, source_target_pairs={{0,1},{1,0},{2,3},{3,2},{4,5},{5,4},{6,7},{7,6},{8,9},{9,8},{10,11... | collective-permute-start | bytes 1966088 | tf_op jit(solution)/shard_map/ppermute | solution.py:482
  4.0 0.1 collective-permute-start.4
  4.1 0.0 collective-permute-done.qf_ref
  4.1 0.0 collective-permute-done.1.gf_ref
  4.1 0.0 copy-start.10
  4.1 1.7 %row_stats.1 = (bf16[32,24,128]{2,1,0:T(8,128)(2,1)}, f32[32,256]{1,0:T(8,128)}, f32[32,256]{1,0:T(8,128)}, bf16[32,128]{1,0:T(8,128)(2,1)}) custom-call(bf16[48,128]{1,0:T(8,128)(2,1)S(1)} %get-tuple-element.21.own_ref, f32[32,256]{1,0:T(8,128)S(1)} %get-tuple-element.22.spot_ref, f32[32,256]{1,0:T(8,128)S(1)} %get-tuple-element.23.weight_ref, ...), custom_call_target="tpu_custom_call" | custom-call | flops 1000 | bytes 1000 | tf_op jit(solution)/shard_map/row_stats/pallas_call | solution.py:485
  5.8 7.3 %all-to-all-start = ((bf16[32,24,128]{2,1,0:T(8,128)(2,1)}), bf16[32,24,128]{2,1,0:T(8,128)(2,1)S(1)}, u32[]{:S(2)}, u32[]{:S(2)}) async-start(bf16[32,24,128]{2,1,0:T(8,128)(2,1)} %get-tuple-element.24), calls=%async_computation | async-start | bytes 393216 | tf_op jit(solution)/shard_map/all_to_all | solution.py:509
  13.1 0.0 collective-permute-done.3.kf_ref
  13.1 0.0 copy-start.3
  13.1 0.0 collective-permute-done.4.vf_ref
  13.2 0.0 copy-done.9
  13.2 0.0 copy-done.10
  13.2 7.7 %near_levels.1 = (bf16[256,1280]{1,0:T(8,128)(2,1)}, f32[256,1280]{1,0:T(8,128)}, f32[256,1280]{1,0:T(8,128)}, bf16[256,1280]{1,0:T(8,128)(2,1)}, f32[32,256]{1,0:T(8,128)}) custom-call(s32[2,10]{1,0:T(2,128)} %off_hbm.3, f32[32,256]{1,0:T(8,128)} %get-tuple-element.28.after_ref.s_ref, bf16[48,128]{1,0:T(8,128)(2,1)S(1)} %get-tuple-element.21.own_ref, ...), custom_call_target="tpu_custom_call" | custom-call | flops 7000000000 | bytes 1000 | tf_op jit(solution)/shard_map/near_levels/pallas_call | solution.py:513
  21.0 0.3 %collective-permute-start.5 = (bf16[256,1280]{1,0:T(8,128)(2,1)}, bf16[256,1280]{1,0:T(8,128)(2,1)}, u32[]{:S(2)}, u32[]{:S(2)}) collective-permute-start(bf16[256,1280]{1,0:T(8,128)(2,1)} %get-tuple-element.34), channel_id=1, source_target_pairs={{0,1},{1,0},{2,3},{3,2},{4,5},{5,4},{6,7},{7,6},{8,9},{9,8},{10,11... | collective-permute-start | bytes 1966088 | tf_op jit(solution)/shard_map/ppermute | solution.py:541
  21.3 0.7 %all-to-all-done.recv_ref = bf16[32,24,128]{2,1,0:T(8,128)(2,1)S(1)} async-done(((bf16[32,24,128]{2,1,0:T(8,128)(2,1)}), bf16[32,24,128]{2,1,0:T(8,128)(2,1)S(1)}, u32[]{:S(2)}, u32[]{:S(2)}) %all-to-all-start) | async-done | bytes 196640 | tf_op jit(solution)/shard_map/all_to_all | solution.py:509
  22.0 0.6 %third_level.1 = (f32[32,128]{1,0:T(8,128)S(1)}, f32[32,128]{1,0:T(8,128)S(1)}) custom-call(bf16[32,24,128]{2,1,0:T(8,128)(2,1)S(1)} %all-to-all-done.recv_ref), custom_call_target="tpu_custom_call" | custom-call | flops 7000000000 | bytes 1000 | tf_op jit(solution)/shard_map/third_level/pallas_call | solution.py:542
  22.6 0.6 %collective-permute-start.2 = (f32[32,128]{1,0:T(8,128)S(1)}, f32[32,128]{1,0:T(8,128)S(1)}, u32[]{:S(2)}, u32[]{:S(2)}) collective-permute-start(f32[32,128]{1,0:T(8,128)S(1)} %get-tuple-element.26), channel_id=1, source_target_pairs={{0,1},{1,0},{2,3},{3,2},{4,5},{5,4},{6,7},{7,6},{8,9},{9,8},{10,11... | collective-permute-start | bytes 49160 | tf_op jit(solution)/shard_map/ppermute | solution.py:551
  23.3 0.8 %collective-permute-done.2.got_ref = f32[32,128]{1,0:T(8,128)S(1)} collective-permute-done((f32[32,128]{1,0:T(8,128)S(1)}, f32[32,128]{1,0:T(8,128)S(1)}, u32[]{:S(2)}, u32[]{:S(2)}) %collective-permute-start.2) | collective-permute-done | bytes 16416 | tf_op jit(solution)/shard_map/ppermute | solution.py:551
  24.1 0.0 collective-permute-done.5.ret_hbm
  24.1 3.8 %join.1 = (bf16[256,1280]{1,0:T(8,128)(2,1)}, bf16[256,1280]{1,0:T(8,128)(2,1)}, bf16[256,1280]{1,0:T(8,128)(2,1)}) custom-call(s32[2,10]{1,0:T(2,128)} %off_hbm.3, f32[32,128]{1,0:T(8,128)S(1)} %get-tuple-element.25.mine_ref, f32[32,128]{1,0:T(8,128)S(1)} %collective-permute-done.2.got_ref, ...), custom_call_target="tpu_custom_call", output_to_operand_aliasing={{0}: (15, {})} | custom-call | flops 1000 | bytes 1000 | tf_op jit(solution)/shard_map/join/pallas_call | solution.py:552
  (17 shorter events, 0.0 us)
Async XLA Ops:
  0.6 2.9 %copy-start = (bf16[256,1280]{1,0:T(8,128)(2,1)S(1)}, bf16[256,1280]{1,0:T(8,128)(2,1)}, u32[]{:S(2)}) copy-start(bf16[256,1280]{1,0:T(8,128)(2,1)} %k_ref.7) | copy-start | bytes 1966084
  0.6 3.4 %copy-start.5 = (bf16[256,1280]{1,0:T(8,128)(2,1)S(1)}, bf16[256,1280]{1,0:T(8,128)(2,1)}, u32[]{:S(2)}) copy-start(bf16[256,1280]{1,0:T(8,128)(2,1)} %v_ref.5) | copy-start | bytes 1966084
  0.7 3.4 %collective-permute-start = (bf16[256,1280]{1,0:T(8,128)(2,1)}, bf16[256,1280]{1,0:T(8,128)(2,1)S(1)}, u32[]{:S(2)}, u32[]{:S(2)}) collective-permute-start(bf16[256,1280]{1,0:T(8,128)(2,1)} %q_ref.3), channel_id=1, source_target_pairs={{0,1},{1,0},{2,3},{3,2},{4,5},{5,4},{6,7},{7,6},{8,9},{9,8},{10,11... | collective-permute-start | bytes 1966088 | tf_op jit(solution)/shard_map/ppermute | solution.py:465
  1.2 2.9 %collective-permute-start.1 = (bf16[256,1280]{1,0:T(8,128)(2,1)}, bf16[256,1280]{1,0:T(8,128)(2,1)S(1)}, u32[]{:S(2)}, u32[]{:S(2)}) collective-permute-start(bf16[256,1280]{1,0:T(8,128)(2,1)} %g_ref.3), channel_id=1, source_target_pairs={{0,1},{1,0},{2,3},{3,2},{4,5},{5,4},{6,7},{7,6},{8,9},{9,8},{10,11... | collective-permute-start | bytes 1966088 | tf_op jit(solution)/shard_map/ppermute | solution.py:466
  3.5 9.6 %collective-permute-start.3 = (bf16[256,1280]{1,0:T(8,128)(2,1)S(1)}, bf16[256,1280]{1,0:T(8,128)(2,1)S(1)}, u32[]{:S(2)}, u32[]{:S(2)}) collective-permute-start(bf16[256,1280]{1,0:T(8,128)(2,1)S(1)} %copy-done), channel_id=1, source_target_pairs={{0,1},{1,0},{2,3},{3,2},{4,5},{5,4},{6,7},{7,6},{8,9},{9,8},{10,11... | collective-permute-start | bytes 1966088 | tf_op jit(solution)/shard_map/ppermute | solution.py:482
  4.0 9.1 %collective-permute-start.4 = (bf16[256,1280]{1,0:T(8,128)(2,1)S(1)}, bf16[256,1280]{1,0:T(8,128)(2,1)}, u32[]{:S(2)}, u32[]{:S(2)}) collective-permute-start(bf16[256,1280]{1,0:T(8,128)(2,1)S(1)} %copy-done.5), channel_id=1, source_target_pairs={{0,1},{1,0},{2,3},{3,2},{4,5},{5,4},{6,7},{7,6},{8,9},{9,8},{10,11... | collective-permute-start | bytes 1966088 | tf_op jit(solution)/shard_map/ppermute | solution.py:483
  4.1 9.1 %copy-start.9 = (bf16[256,1280]{1,0:T(8,128)(2,1)S(1)}, bf16[256,1280]{1,0:T(8,128)(2,1)}, u32[]{:S(2)}) copy-start(bf16[256,1280]{1,0:T(8,128)(2,1)} %q_ref.3) | copy-start | bytes 1966084
  4.1 9.1 %copy-start.10 = (bf16[256,1280]{1,0:T(8,128)(2,1)S(1)}, bf16[256,1280]{1,0:T(8,128)(2,1)}, u32[]{:S(2)}) copy-start(bf16[256,1280]{1,0:T(8,128)(2,1)} %g_ref.3) | copy-start | bytes 1966084
  5.8 16.2 %all-to-all-start = ((bf16[32,24,128]{2,1,0:T(8,128)(2,1)}), bf16[32,24,128]{2,1,0:T(8,128)(2,1)S(1)}, u32[]{:S(2)}, u32[]{:S(2)}) async-start(bf16[32,24,128]{2,1,0:T(8,128)(2,1)} %get-tuple-element.24), calls=%async_computation | async-start | bytes 393216 | tf_op jit(solution)/shard_map/all_to_all | solution.py:509
  13.1 7.8 %copy-start.3 = (bf16[256,1280]{1,0:T(8,128)(2,1)}, bf16[256,1280]{1,0:T(8,128)(2,1)S(1)}, u32[]{:S(2)}) copy-start(bf16[256,1280]{1,0:T(8,128)(2,1)S(1)} %collective-permute-done.3.kf_ref) | copy-start | bytes 1966084
  20.9 3.2 %copy-start.1 = (f32[256,1280]{1,0:T(8,128)S(1)}, f32[256,1280]{1,0:T(8,128)}, u32[]{:S(2)}) copy-start(f32[256,1280]{1,0:T(8,128)} %get-tuple-element.32.dki) | copy-start | bytes 3932164
  20.9 3.2 %copy-start.2 = (f32[256,1280]{1,0:T(8,128)S(1)}, f32[256,1280]{1,0:T(8,128)}, u32[]{:S(2)}) copy-start(f32[256,1280]{1,0:T(8,128)} %get-tuple-element.33.dvi) | copy-start | bytes 3932164
  21.0 3.2 %collective-permute-start.5 = (bf16[256,1280]{1,0:T(8,128)(2,1)}, bf16[256,1280]{1,0:T(8,128)(2,1)}, u32[]{:S(2)}, u32[]{:S(2)}) collective-permute-start(bf16[256,1280]{1,0:T(8,128)(2,1)} %get-tuple-element.34), channel_id=1, source_target_pairs={{0,1},{1,0},{2,3},{3,2},{4,5},{5,4},{6,7},{7,6},{8,9},{9,8},{10,11... | collective-permute-start | bytes 1966088 | tf_op jit(solution)/shard_map/ppermute | solution.py:541
  22.0 2.1 %copy-start.4 = (bf16[256,1280]{1,0:T(8,128)(2,1)S(1)}, bf16[256,1280]{1,0:T(8,128)(2,1)}, u32[]{:S(2)}) copy-start(bf16[256,1280]{1,0:T(8,128)(2,1)} %copy-done.3) | copy-start | bytes 1966084
  22.0 2.1 %copy-start.6 = (f32[32,256]{1,0:T(8,128)S(1)}, f32[32,256]{1,0:T(8,128)}, u32[]{:S(2)}) copy-start(f32[32,256]{1,0:T(8,128)} %get-tuple-element.28.after_ref.s_ref) | copy-start | bytes 98308
  22.0 2.1 %copy-start.7 = (f32[32,256]{1,0:T(8,128)S(1)}, f32[32,256]{1,0:T(8,128)}, u32[]{:S(2)}) copy-start(f32[32,256]{1,0:T(8,128)} %get-tuple-element.29.dp_ref) | copy-start | bytes 98308
  22.0 2.1 %copy-start.8 = (bf16[32,128]{1,0:T(8,128)(2,1)S(1)}, bf16[32,128]{1,0:T(8,128)(2,1)}, u32[]{:S(2)}) copy-start(bf16[32,128]{1,0:T(8,128)(2,1)} %get-tuple-element.27.far_ref) | copy-start | bytes 24580
  22.6 1.5 %collective-permute-start.2 = (f32[32,128]{1,0:T(8,128)S(1)}, f32[32,128]{1,0:T(8,128)S(1)}, u32[]{:S(2)}, u32[]{:S(2)}) collective-permute-start(f32[32,128]{1,0:T(8,128)S(1)} %get-tuple-element.26), channel_id=1, source_target_pairs={{0,1},{1,0},{2,3},{3,2},{4,5},{5,4},{6,7},{7,6},{8,9},{9,8},{10,11... | collective-permute-start | bytes 49160 | tf_op jit(solution)/shard_map/ppermute | solution.py:551

commit v2 on v1

--- a/solution.py
+++ b/solution.py
@@ -152,16 +152,18 @@
         copy.wait()
 
 
-def near_head(off_ref, h, inputs, outputs, wait, send):
+def near_head(off_ref, h, inputs, outputs, waits, send):
     q_ref, k_ref, v_ref, g_ref, kf_ref, vf_ref = inputs
     dq_ref, dk_ref, dv_ref, ret_ref = outputs
     length, dh = q_ref.shape[0], q_ref.shape[1] // off_ref.shape[1]
     half = length // 2
     scale = dh**-0.5
     cols = slice(h * dh, (h + 1) * dh)
-    wait(h)
+    q, k, v, g = q_ref[:, cols], k_ref[:, cols], v_ref[:, cols], g_ref[:, cols]
+    if h == 0:
+        s1, dp1 = dot_nt(k, q), dot_nt(v, g)
+        waits[0].wait()
     pair, wide = off_ref[0, h], off_ref[1, h]
-    q, k, v, g = q_ref[:, cols], k_ref[:, cols], v_ref[:, cols], g_ref[:, cols]
     pick = (iota((half, length), 1) == 2 * iota((half, length), 0) + pair).astype(BF16)
     kc = dot_nn(pick, kf_ref[:, cols]).astype(BF16)
     yield
@@ -169,13 +171,17 @@
     chosen = jnp.bitwise_and(lanes, 1) == pair
     a_t = chosen.astype(F32)
     a_u = (jnp.bitwise_and(iota((length, 1), 0), 1) == pair).astype(F32)
-    s1 = dot_nt(k, q)
+    if h > 0:
+        s1 = dot_nt(k, q)
     s2 = dot_nt(kc, q) + jnp.where(chosen, 0.0, NEG)
+    if h == 0:
+        waits[1].wait()
     vc = dot_nn(pick, vf_ref[:, cols]).astype(BF16)
     yield
     m = jnp.maximum(jnp.max(s1, axis=0, keepdims=True), jnp.max(s2, axis=0, keepdims=True))
     m = m * (scale * LOG2E)
-    dp1 = dot_nt(v, g)
+    if h > 0:
+        dp1 = dot_nt(v, g)
     dp2 = dot_nt(vc, g)
     yield
     e1 = jnp.exp2(s1 * (scale * LOG2E) - m) * (1.0 + a_t * a_u)
@@ -202,21 +208,26 @@
 
 
 def main_kernel(
-    heads, off_hbm, after_ref, own_ref, q_ref, k_ref, v_ref, g_ref, kf_ref, vf_ref,
-    dq_hbm, dk_hbm, dv_hbm, ret_hbm, far_hbm,
-    off_ref, dq_ref, dk_ref, dv_ref, ret_ref, far_scores, off_sem, far_sem, out_sems,
+    heads, off_hbm, after_ref, vf_hbm, own_ref, q_ref, k_ref, v_ref, g_ref, kf_ref,
+    dq_hbm, dk_hbm, dv_hbm, ret_hbm, far_hbm, blocks_hbm,
+    off_ref, vf_ref, dq_ref, dk_ref, dv_ref, ret_ref, far_scores, blocks,
+    off_sem, in_sem, far_sem, block_sem, out_sems,
 ):
     offsets = pltpu.make_async_copy(off_hbm, off_ref, off_sem)
     offsets.start()
+    values = pltpu.make_async_copy(vf_hbm, vf_ref, in_sem)
+    values.start()
     dh = q_ref.shape[1] // heads
     near = (dq_ref, dk_ref, dv_ref, ret_ref)
     writes = []
 
-    def wait(h):
-        if h == 0:
-            offsets.wait()
-
     def send(h):
+        base = pl.multiple_of(jnp.bitwise_and(off_ref[1, h], ~15), 16)
+        blocks[h] = dq_ref[pl.ds(base, 16), h * dh : (h + 1) * dh]
+        if h == heads - 1:
+            copy = pltpu.make_async_copy(blocks, blocks_hbm, block_sem)
+            copy.start()
+            writes.append(copy)
         if h % 2 == 1:
             cols = slice((h - 1) * dh, (h + 1) * dh)
             for i, (a, b) in enumerate(zip(near, (dq_hbm, dk_hbm, dv_hbm, ret_hbm))):
@@ -226,7 +237,7 @@
                 writes.append(copy)
 
     inputs = (q_ref, k_ref, v_ref, g_ref, kf_ref, vf_ref)
-    work = [near_head(off_ref, h, inputs, near, wait, send) for h in range(heads)]
+    work = [near_head(off_ref, h, inputs, near, (offsets, values), send) for h in range(heads)]
     steps, lag = 6, 2
     for turn in range(steps + lag * (heads - 1)):
         for h in reversed(range(heads)):
@@ -336,14 +347,20 @@
 
 def final_kernel(
     heads, off_hbm, mine_ref, got_ref, own_ref, far_ref, spot_ref, weight_ref, s_ref, dp_ref,
-    k_ref, kf_ref, dki, dvi, ret_hbm, far_hbm, dq_in, dq_ref, dk_ref, dv_ref,
-    off_ref, ret, far_scores, full, blocks, dko, dvo, off_sem, far_sem, ret_sems, block_sems, write_sems,
+    dki, dvi, blocks_in, ret, k_hbm, kf_hbm, far_hbm, dq_in, dq_ref, dk_ref, dv_ref,
+    off_ref, k_ref, kf_ref, far_scores, full, blocks, dko, dvo, off_sem, key_sems, far_sem, block_sems, write_sems,
 ):
     offsets = pltpu.make_async_copy(off_hbm, off_ref, off_sem)
     offsets.start()
     scores = pltpu.make_async_copy(far_hbm, far_scores, far_sem)
     scores.start()
-    length, dh = k_ref.shape[0], own_ref.shape[1]
+    keys = [
+        pltpu.make_async_copy(k_hbm, k_ref, key_sems.at[0]),
+        pltpu.make_async_copy(kf_hbm, kf_ref, key_sems.at[1]),
+    ]
+    for copy in keys:
+        copy.start()
+    length, dh = k_hbm.shape[0], own_ref.shape[1]
     half, part = length // 2, heads // 2
     scale = dh**-0.5
 
@@ -352,12 +369,6 @@
         return ref.at[pl.ds(base, 16), pl.ds(h * dh, dh)]
 
     chunks = [slice(2 * j * dh, 2 * (j + 1) * dh) for j in range(part)]
-    fetches = [
-        pltpu.make_async_copy(ret_hbm.at[:, cols], ret.at[:, cols], ret_sems.at[j])
-        for j, cols in enumerate(chunks)
-    ]
-    for copy in fetches:
-        copy.start()
     own, far = own_ref[...].astype(F32), far_ref[...].astype(F32)
     first = jnp.bitwise_and(lax.axis_index("ctx"), 1) == 0
     mine, got = mine_ref[...], got_ref[...]
@@ -378,17 +389,9 @@
     scores.wait()
     p_far = jnp.exp2(jnp.where(met, far_scores[:16, :] - m_me, NEG)) * i_me
     ds_far = scale * p_far * (far_scores[16:, :] - d_me)
-    dq_rows = dq_wide + own_columns(
-        dot_nn(ds_two[0:16, :].astype(BF16), k_ref[...]) + dot_nn(ds_far.astype(BF16), kf_ref[...]),
-        heads,
-    )
     spot = spot_ref[...]
     offsets.wait()
-    reads = [
-        pltpu.make_async_copy(place(dq_in, h), blocks.at[h], block_sems.at[h]) for h in range(heads)
-    ]
-    for copy in reads:
-        copy.start()
+    writes = []
 
     def spread(left, array, rows):
         near = own[(array + 2) * heads : (array + 2) * heads + 16, :]
@@ -397,7 +400,6 @@
         parts = (near, far[16 * array : 16 * array + 16, :], high, rows - high)
         return left, jnp.concatenate([block_rows(part, heads) for part in parts], axis=0)
 
-    writes = []
     for index, (base, out, out_ref, left, right) in enumerate(
         (
             (dki, dko, dk_ref) + spread(ds_two, 0, dk_rows),
@@ -406,8 +408,6 @@
     ):
         back = slice(index * half, (index + 1) * half)
         for j, chunk in enumerate(chunks):
-            if index == 0:
-                fetches[j].wait()
             for h in (2 * j, 2 * j + 1):
                 cols = slice(h * dh, (h + 1) * dh)
                 pick = iota((length, half), 0) == 2 * iota((length, half), 1) + off_ref[0, h]
@@ -417,10 +417,16 @@
             copy = pltpu.make_async_copy(out.at[:, chunk], out_ref.at[:, chunk], sem)
             copy.start()
             writes.append(copy)
+    for copy in keys:
+        copy.wait()
+    dq_rows = dq_wide + own_columns(
+        dot_nn(ds_two[0:16, :].astype(BF16), k_ref[...]) + dot_nn(ds_far.astype(BF16), kf_ref[...]),
+        heads,
+    )
     for h in range(heads):
-        reads[h].wait()
         here = iota((16, dh), 0) == jnp.bitwise_and(off_ref[1, h], 15)
-        blocks[h] = jnp.where(here, dq_rows[h : h + 1, :], blocks[h].astype(F32)).astype(BF16)
+        block = jnp.where(here, dq_rows[h : h + 1, :], blocks_in[h].astype(F32))
+        blocks[h] = block.astype(BF16)
         copy = pltpu.make_async_copy(blocks.at[h], place(dq_ref, h), block_sems.at[h])
         copy.start()
         writes.append(copy)
@@ -510,7 +516,7 @@
     whole = pltpu.VMEM((length, width), BF16)
     wide = pltpu.VMEM((length, width), F32)
     rows = pltpu.VMEM((32, dh), F32)
-    dq, dk, dv, partial, far_scores = call(
+    dq, dk, dv, partial, far_scores, blocks = call(
         functools.partial(main_kernel, heads),
         "near_levels",
         (
@@ -519,24 +525,29 @@
             pltpu.HBM((length, width), F32),
             pltpu.HBM((length, width), BF16),
             pltpu.HBM((32, length), F32),
+            pltpu.HBM((heads, 16, dh), BF16),
         ),
-        [hbm] * 2 + [vmem] * 7,
-        (hbm,) * 5,
+        [hbm] * 3 + [vmem] * 6,
+        (hbm,) * 6,
         [
             pltpu.SMEM(offsets.shape, jnp.int32),
+            whole,
             whole,
             wide,
             wide,
             whole,
             pltpu.VMEM((32, length), F32),
+            pltpu.VMEM((heads, 16, dh), BF16),
+            pltpu.SemaphoreType.DMA,
+            pltpu.SemaphoreType.DMA,
             pltpu.SemaphoreType.DMA,
             pltpu.SemaphoreType.DMA,
             pltpu.SemaphoreType.DMA((heads // 2, 4)),
         ],
         cost=large,
     )(
-        *far_memory(offsets, s_rows),
-        *near_memory(own, query, key, value, grad_out, key_far, value_far),
+        *far_memory(offsets, s_rows, value_far),
+        *near_memory(own, query, key, value, grad_out, key_far),
     )
     returned = lax.ppermute(partial, "ctx", mates)
     mine, theirs = call(
@@ -553,10 +564,11 @@
         functools.partial(final_kernel, heads),
         "join",
         (pltpu.HBM((length, width), BF16),) * 3,
-        [hbm] + [vmem] * 12 + [hbm] * 3,
+        [hbm] + [vmem] * 12 + [hbm] * 4,
         (hbm,) * 3,
         [
             pltpu.SMEM(offsets.shape, jnp.int32),
+            whole,
             whole,
             pltpu.VMEM((32, length), F32),
             pltpu.VMEM((64, dh), F32),
@@ -564,17 +576,17 @@
             whole,
             whole,
             pltpu.SemaphoreType.DMA,
+            pltpu.SemaphoreType.DMA((2,)),
             pltpu.SemaphoreType.DMA,
-            pltpu.SemaphoreType.DMA((heads // 2,)),
             pltpu.SemaphoreType.DMA((heads,)),
             pltpu.SemaphoreType.DMA((2, heads // 2)),
         ],
-        input_output_aliases={15: 0},
+        input_output_aliases={16: 0},
     )(
         *far_memory(offsets),
         *near_memory(mine, got, own, far, spot, weight, s_rows, dp_rows),
-        *near_memory(key, key_far, dk, dv),
-        *far_memory(returned, far_scores, dq),
+        *near_memory(dk, dv, blocks, returned),
+        *far_memory(key, key_far, far_scores, dq),
     )
 
 

time: 28.3 us -> 27.4 us (0.968)
  Pallas kernels: 16.1 us -> 14.6 us
  waiting for transfers between devices: 1.59 us -> 2.31 us
    pallas_call x1, Pallas kernels: 3.81 us -> 3 us  [on_device(): call(functools.partial(final_kernel, heads), 'join', (pltpu.HBM((length,...]
    all_to_all x1, waiting for transfers between devices: 0.74 us -> 1.46 us  [on_device(): lax.all_to_all(load, 'ctx', 0, 0, axis_index_groups=groups, tiled=True)]
    pallas_call x1, Pallas kernels: 7.74 us -> 7.02 us  [on_device(): call(functools.partial(main_kernel, heads), 'near_levels', (pltpu.HBM((le...]
    ppermute x1, starting transfers between devices: 0.09 us -> 0.49 us  [on_device(): value_far = lax.ppermute(value_later, 'ctx', mates)]
    ppermute x1, starting transfers between devices: 0.49 us -> 0.09 us  [on_device(): key_far = lax.ppermute(key_later, 'ctx', mates)]
  transfers between devices with their start and end apart: 7 -> 7, of which waited for: 2 -> 2; matrix products, arithmetic and copies ran while one was open for 0% -> 0% of each run, Pallas kernels for 44% -> 43%
where the time goes in v2:
time: 27.4 us; the launch traced here: 27.1 us
  Pallas kernels  14.6 us (53%)
  starting transfers between devices  9.38 us (34%)
  waiting for transfers between devices  2.31 us (8%)
  between operations  0.8 us (3%)
    all_to_all x1, starting transfers between devices, on_device(): lax.all_to_all(load, 'ctx', 0, 0, axis_index_groups=groups, tiled=True)  7.27 us
    pallas_call x1, Pallas kernels, on_device(): call(functools.partial(main_kernel, heads), 'near_levels', (pltpu.HBM((le...  7.02 us
    pallas_call x1, Pallas kernels, on_device(): call(functools.partial(final_kernel, heads), 'join', (pltpu.HBM((length,...  3 us
    pallas_call x1, Pallas kernels, on_device(): call(functools.partial(pack_kernel, heads), 'pack_rows', (pltpu.VMEM((48,...  2.24 us
    pallas_call x1, Pallas kernels, on_device(): call(functools.partial(stats_kernel, heads, span), 'row_stats', (pltpu.HB...  1.7 us
    all_to_all x1, waiting for transfers between devices, on_device(): lax.all_to_all(load, 'ctx', 0, 0, axis_index_groups=groups, tiled=True)  1.46 us
    ppermute x1, waiting for transfers between devices, on_device(): got = lax.ppermute(theirs, 'ctx', mates)  0.84 us
    pallas_call x1, Pallas kernels, on_device(): call(functools.partial(wide_kernel, heads, span), 'third_level', (rows, r...  0.63 us
  transfers between devices with their start and end apart: 7, of which 2 were waited for; matrix products, arithmetic and copies ran while one was open for 0% of the time, Pallas kernels for 43%

profile of v2, /device:TPU:0, one launch (start us, length us, event | category | flops | bytes accessed | tf_op | source)
XLA Modules:
  0.0 27.1 jit_solution(3851369151210709080)
XLA Ops:
  0.6 0.0 copy-start
  0.7 0.5 %collective-permute-start = (bf16[256,1280]{1,0:T(8,128)(2,1)}, bf16[256,1280]{1,0:T(8,128)(2,1)S(1)}, u32[]{:S(2)}, u32[]{:S(2)}) collective-permute-start(bf16[256,1280]{1,0:T(8,128)(2,1)} %q_ref.3), channel_id=1, source_target_pairs={{0,1},{1,0},{2,3},{3,2},{4,5},{5,4},{6,7},{7,6},{8,9},{9,8},{10,11... | collective-permute-start | bytes 1966088 | tf_op jit(solution)/shard_map/ppermute | solution.py:471
  1.2 0.1 collective-permute-start.1
  1.3 2.2 %pack_rows.1 = (bf16[48,128]{1,0:T(8,128)(2,1)S(1)}, f32[32,256]{1,0:T(8,128)S(1)}, f32[32,256]{1,0:T(8,128)S(1)}) custom-call(s32[2,10]{1,0:T(2,128)} %off_hbm.3, bf16[256,1280]{1,0:T(8,128)(2,1)} %k_hbm.1, bf16[256,1280]{1,0:T(8,128)(2,1)} %v_ref.5, bf16[256,1280]{1,0:T(8,128)(2,1)} %q_ref.3, bf16[256,1280]{1,0:T(8,128)(2,1)} %g_ref.3), custom_call_target="tpu_custom_call" | custom-call | flops 7000000000 | bytes 1000 | tf_op jit(solution)/shard_map/pack_rows/pallas_call | solution.py:474
  3.5 0.5 %collective-permute-start.3 = (bf16[256,1280]{1,0:T(8,128)(2,1)S(1)}, bf16[256,1280]{1,0:T(8,128)(2,1)}, u32[]{:S(2)}, u32[]{:S(2)}) collective-permute-start(bf16[256,1280]{1,0:T(8,128)(2,1)S(1)} %copy-done.3), channel_id=1, source_target_pairs={{0,1},{1,0},{2,3},{3,2},{4,5},{5,4},{6,7},{7,6},{8,9},{9,8},{10,11... | collective-permute-start | bytes 1966088 | tf_op jit(solution)/shard_map/ppermute | solution.py:489
  4.0 0.1 collective-permute-start.4
  4.1 0.0 collective-permute-done.qf_ref
  4.1 0.0 collective-permute-done.1.gf_ref
  4.1 0.0 copy-start.10
  4.1 1.7 %row_stats.1 = (bf16[32,24,128]{2,1,0:T(8,128)(2,1)}, f32[32,256]{1,0:T(8,128)}, f32[32,256]{1,0:T(8,128)}, bf16[32,128]{1,0:T(8,128)(2,1)}) custom-call(bf16[48,128]{1,0:T(8,128)(2,1)S(1)} %get-tuple-element.22.own_ref, f32[32,256]{1,0:T(8,128)S(1)} %get-tuple-element.23.spot_ref, f32[32,256]{1,0:T(8,128)S(1)} %get-tuple-element.24.weight_ref, ...), custom_call_target="tpu_custom_call" | custom-call | flops 1000 | bytes 1000 | tf_op jit(solution)/shard_map/row_stats/pallas_call | solution.py:491
  5.8 7.3 %all-to-all-start = ((bf16[32,24,128]{2,1,0:T(8,128)(2,1)}), bf16[32,24,128]{2,1,0:T(8,128)(2,1)S(1)}, u32[]{:S(2)}, u32[]{:S(2)}) async-start(bf16[32,24,128]{2,1,0:T(8,128)(2,1)} %get-tuple-element.25), calls=%async_computation | async-start | bytes 393216 | tf_op jit(solution)/shard_map/all_to_all | solution.py:515
  13.1 0.0 collective-permute-done.3.vf_hbm
  13.1 0.0 collective-permute-done.4.kf_ref.kf_hbm
  13.2 7.0 %near_levels.1 = (bf16[256,1280]{1,0:T(8,128)(2,1)}, f32[256,1280]{1,0:T(8,128)}, f32[256,1280]{1,0:T(8,128)}, bf16[256,1280]{1,0:T(8,128)(2,1)}, f32[32,256]{1,0:T(8,128)}, /*index=5*/bf16[10,16,128]{2,1,0:T(8,128)(2,1)}) custom-call(s32[2,10]{1,0:T(2,128)} %off_hbm.3, f32[32,256]{1,0:T(8,128)} %get-tuple-element.29.after_ref.s_ref, ...), custom_call_target="tpu_custom_call" | custom-call | flops 7000000000 | bytes 1000 | tf_op jit(solution)/shard_map/near_levels/pallas_call | solution.py:519
  20.2 0.3 %collective-permute-start.5 = (bf16[256,1280]{1,0:T(8,128)(2,1)}, bf16[256,1280]{1,0:T(8,128)(2,1)S(1)}, u32[]{:S(2)}, u32[]{:S(2)}) collective-permute-start(bf16[256,1280]{1,0:T(8,128)(2,1)} %get-tuple-element.36), channel_id=1, source_target_pairs={{0,1},{1,0},{2,3},{3,2},{4,5},{5,4},{6,7},{7,6},{8,9},{9,8},{10,11... | collective-permute-start | bytes 1966088 | tf_op jit(solution)/shard_map/ppermute | solution.py:552
  20.5 1.5 %all-to-all-done.recv_ref = bf16[32,24,128]{2,1,0:T(8,128)(2,1)S(1)} async-done(((bf16[32,24,128]{2,1,0:T(8,128)(2,1)}), bf16[32,24,128]{2,1,0:T(8,128)(2,1)S(1)}, u32[]{:S(2)}, u32[]{:S(2)}) %all-to-all-start) | async-done | bytes 196640 | tf_op jit(solution)/shard_map/all_to_all | solution.py:515
  22.0 0.6 %third_level.1 = (f32[32,128]{1,0:T(8,128)S(1)}, f32[32,128]{1,0:T(8,128)S(1)}) custom-call(bf16[32,24,128]{2,1,0:T(8,128)(2,1)S(1)} %all-to-all-done.recv_ref), custom_call_target="tpu_custom_call" | custom-call | flops 7000000000 | bytes 1000 | tf_op jit(solution)/shard_map/third_level/pallas_call | solution.py:553
  22.6 0.6 %collective-permute-start.2 = (f32[32,128]{1,0:T(8,128)S(1)}, f32[32,128]{1,0:T(8,128)S(1)}, u32[]{:S(2)}, u32[]{:S(2)}) collective-permute-start(f32[32,128]{1,0:T(8,128)S(1)} %get-tuple-element.27), channel_id=1, source_target_pairs={{0,1},{1,0},{2,3},{3,2},{4,5},{5,4},{6,7},{7,6},{8,9},{9,8},{10,11... | collective-permute-start | bytes 49160 | tf_op jit(solution)/shard_map/ppermute | solution.py:562
  23.3 0.8 %collective-permute-done.2.got_ref = f32[32,128]{1,0:T(8,128)S(1)} collective-permute-done((f32[32,128]{1,0:T(8,128)S(1)}, f32[32,128]{1,0:T(8,128)S(1)}, u32[]{:S(2)}, u32[]{:S(2)}) %collective-permute-start.2) | collective-permute-done | bytes 16416 | tf_op jit(solution)/shard_map/ppermute | solution.py:562
  24.1 0.0 collective-permute-done.5.ret
  24.1 0.0 copy-done.2
  24.1 0.0 copy-done.6
  24.1 0.0 copy-done.7
  24.1 3.0 %join.1 = (bf16[256,1280]{1,0:T(8,128)(2,1)}, bf16[256,1280]{1,0:T(8,128)(2,1)}, bf16[256,1280]{1,0:T(8,128)(2,1)}) custom-call(s32[2,10]{1,0:T(2,128)} %off_hbm.3, f32[32,128]{1,0:T(8,128)S(1)} %get-tuple-element.26.mine_ref, f32[32,128]{1,0:T(8,128)S(1)} %collective-permute-done.2.got_ref, ...), custom_call_target="tpu_custom_call", output_to_operand_aliasing={{0}: (16, {})} | custom-call | flops 1000 | bytes 1000 | tf_op jit(solution)/shard_map/join/pallas_call | solution.py:563
  (17 shorter events, 0.0 us)
Async XLA Ops:
  0.6 3.4 %copy-start = (bf16[256,1280]{1,0:T(8,128)(2,1)S(1)}, bf16[256,1280]{1,0:T(8,128)(2,1)}, u32[]{:S(2)}) copy-start(bf16[256,1280]{1,0:T(8,128)(2,1)} %k_hbm.1) | copy-start | bytes 1966084
  0.6 2.9 %copy-start.3 = (bf16[256,1280]{1,0:T(8,128)(2,1)S(1)}, bf16[256,1280]{1,0:T(8,128)(2,1)}, u32[]{:S(2)}) copy-start(bf16[256,1280]{1,0:T(8,128)(2,1)} %v_ref.5) | copy-start | bytes 1966084
  0.7 3.4 %collective-permute-start = (bf16[256,1280]{1,0:T(8,128)(2,1)}, bf16[256,1280]{1,0:T(8,128)(2,1)S(1)}, u32[]{:S(2)}, u32[]{:S(2)}) collective-permute-start(bf16[256,1280]{1,0:T(8,128)(2,1)} %q_ref.3), channel_id=1, source_target_pairs={{0,1},{1,0},{2,3},{3,2},{4,5},{5,4},{6,7},{7,6},{8,9},{9,8},{10,11... | collective-permute-start | bytes 1966088 | tf_op jit(solution)/shard_map/ppermute | solution.py:471
  1.2 2.9 %collective-permute-start.1 = (bf16[256,1280]{1,0:T(8,128)(2,1)}, bf16[256,1280]{1,0:T(8,128)(2,1)S(1)}, u32[]{:S(2)}, u32[]{:S(2)}) collective-permute-start(bf16[256,1280]{1,0:T(8,128)(2,1)} %g_ref.3), channel_id=1, source_target_pairs={{0,1},{1,0},{2,3},{3,2},{4,5},{5,4},{6,7},{7,6},{8,9},{9,8},{10,11... | collective-permute-start | bytes 1966088 | tf_op jit(solution)/shard_map/ppermute | solution.py:472
  3.5 9.6 %collective-permute-start.3 = (bf16[256,1280]{1,0:T(8,128)(2,1)S(1)}, bf16[256,1280]{1,0:T(8,128)(2,1)}, u32[]{:S(2)}, u32[]{:S(2)}) collective-permute-start(bf16[256,1280]{1,0:T(8,128)(2,1)S(1)} %copy-done.3), channel_id=1, source_target_pairs={{0,1},{1,0},{2,3},{3,2},{4,5},{5,4},{6,7},{7,6},{8,9},{9,8},{10,11... | collective-permute-start | bytes 1966088 | tf_op jit(solution)/shard_map/ppermute | solution.py:489
  4.0 9.1 %collective-permute-start.4 = (bf16[256,1280]{1,0:T(8,128)(2,1)S(1)}, bf16[256,1280]{1,0:T(8,128)(2,1)S(1)}, u32[]{:S(2)}, u32[]{:S(2)}) collective-permute-start(bf16[256,1280]{1,0:T(8,128)(2,1)S(1)} %copy-done), channel_id=1, source_target_pairs={{0,1},{1,0},{2,3},{3,2},{4,5},{5,4},{6,7},{7,6},{8,9},{9,8},{10,11... | collective-permute-start | bytes 1966088 | tf_op jit(solution)/shard_map/ppermute | solution.py:488
  4.1 9.0 %copy-start.9 = (bf16[256,1280]{1,0:T(8,128)(2,1)S(1)}, bf16[256,1280]{1,0:T(8,128)(2,1)}, u32[]{:S(2)}) copy-start(bf16[256,1280]{1,0:T(8,128)(2,1)} %q_ref.3) | copy-start | bytes 1966084
  4.1 9.0 %copy-start.10 = (bf16[256,1280]{1,0:T(8,128)(2,1)S(1)}, bf16[256,1280]{1,0:T(8,128)(2,1)}, u32[]{:S(2)}) copy-start(bf16[256,1280]{1,0:T(8,128)(2,1)} %g_ref.3) | copy-start | bytes 1966084
  5.8 16.2 %all-to-all-start = ((bf16[32,24,128]{2,1,0:T(8,128)(2,1)}), bf16[32,24,128]{2,1,0:T(8,128)(2,1)S(1)}, u32[]{:S(2)}, u32[]{:S(2)}) async-start(bf16[32,24,128]{2,1,0:T(8,128)(2,1)} %get-tuple-element.25), calls=%async_computation | async-start | bytes 393216 | tf_op jit(solution)/shard_map/all_to_all | solution.py:515
  13.1 7.1 %copy-start.4 = (bf16[256,1280]{1,0:T(8,128)(2,1)}, bf16[256,1280]{1,0:T(8,128)(2,1)S(1)}, u32[]{:S(2)}) copy-start(bf16[256,1280]{1,0:T(8,128)(2,1)S(1)} %collective-permute-done.4.kf_ref.kf_hbm) | copy-start | bytes 1966084
  20.2 3.9 %copy-start.1 = (f32[256,1280]{1,0:T(8,128)S(1)}, f32[256,1280]{1,0:T(8,128)}, u32[]{:S(2)}) copy-start(f32[256,1280]{1,0:T(8,128)} %get-tuple-element.33.dki) | copy-start | bytes 3932164
  20.2 3.9 %copy-start.2 = (f32[256,1280]{1,0:T(8,128)S(1)}, f32[256,1280]{1,0:T(8,128)}, u32[]{:S(2)}) copy-start(f32[256,1280]{1,0:T(8,128)} %get-tuple-element.34.dvi) | copy-start | bytes 3932164
  20.2 3.9 %collective-permute-start.5 = (bf16[256,1280]{1,0:T(8,128)(2,1)}, bf16[256,1280]{1,0:T(8,128)(2,1)S(1)}, u32[]{:S(2)}, u32[]{:S(2)}) collective-permute-start(bf16[256,1280]{1,0:T(8,128)(2,1)} %get-tuple-element.36), channel_id=1, source_target_pairs={{0,1},{1,0},{2,3},{3,2},{4,5},{5,4},{6,7},{7,6},{8,9},{9,8},{10,11... | collective-permute-start | bytes 1966088 | tf_op jit(solution)/shard_map/ppermute | solution.py:552
  22.0 2.1 %copy-start.5 = (bf16[10,16,128]{2,1,0:T(8,128)(2,1)S(1)}, bf16[10,16,128]{2,1,0:T(8,128)(2,1)}, u32[]{:S(2)}) copy-start(bf16[10,16,128]{2,1,0:T(8,128)(2,1)} %get-tuple-element.35.blocks_in) | copy-start | bytes 122884
  22.0 2.1 %copy-start.6 = (f32[32,256]{1,0:T(8,128)S(1)}, f32[32,256]{1,0:T(8,128)}, u32[]{:S(2)}) copy-start(f32[32,256]{1,0:T(8,128)} %get-tuple-element.29.after_ref.s_ref) | copy-start | bytes 98308
  22.0 2.1 %copy-start.7 = (f32[32,256]{1,0:T(8,128)S(1)}, f32[32,256]{1,0:T(8,128)}, u32[]{:S(2)}) copy-start(f32[32,256]{1,0:T(8,128)} %get-tuple-element.30.dp_ref) | copy-start | bytes 98308
  22.0 2.1 %copy-start.8 = (bf16[32,128]{1,0:T(8,128)(2,1)S(1)}, bf16[32,128]{1,0:T(8,128)(2,1)}, u32[]{:S(2)}) copy-start(bf16[32,128]{1,0:T(8,128)(2,1)} %get-tuple-element.28.far_ref) | copy-start | bytes 24580
  22.6 1.5 %collective-permute-start.2 = (f32[32,128]{1,0:T(8,128)S(1)}, f32[32,128]{1,0:T(8,128)S(1)}, u32[]{:S(2)}, u32[]{:S(2)}) collective-permute-start(f32[32,128]{1,0:T(8,128)S(1)} %get-tuple-element.27), channel_id=1, source_target_pairs={{0,1},{1,0},{2,3},{3,2},{4,5},{5,4},{6,7},{7,6},{8,9},{9,8},{10,11... | collective-permute-start | bytes 49160 | tf_op jit(solution)/shard_map/ppermute | solution.py:562

commit v3 on v2

--- a/solution.py
+++ b/solution.py
@@ -101,7 +101,7 @@
     load_ref, s_hbm, dp_hbm, far_hbm, s_ref, dp_ref, far_ref, acc, load, sems, row_sems,
 ):
     dh = own_ref.shape[1]
-    part, slots = heads // 2, load_ref.shape[1]
+    part, slots = heads // 2, load_ref.shape[0] // span
     own = own_ref[...].astype(F32)
     spot = spot_ref[0:16, :].astype(BF16)
 
@@ -136,13 +136,13 @@
     table = high + pltpu.roll(middle, 32, 1) + pltpu.roll(low, 64, 1)
     for c in range(2):
         acc[c * slots + 4 * part : (c + 1) * slots, :] = table
-    halves = acc[...].astype(BF16).reshape(2, slots, dh)
-    repeat = load.shape[0]
-    for i in range(repeat // 2):
-        load[2 * i : 2 * i + 2] = halves
+    halves = acc[...].astype(BF16)
+    stride = load.shape[0]
+    for i in range(stride // (2 * slots)):
+        load[2 * i * slots : 2 * (i + 1) * slots, :] = halves
     copies = [
-        pltpu.make_async_copy(load, load_ref.at[pl.ds(i * repeat, repeat)], sems.at[i])
-        for i in range(span // repeat)
+        pltpu.make_async_copy(load, load_ref.at[pl.ds(i * stride, stride), :], sems.at[i])
+        for i in range(span * slots // stride)
     ]
     for i, (near, away) in enumerate(((s_ref, s_hbm), (dp_ref, dp_hbm), (far_ref, far_hbm))):
         copies.append(pltpu.make_async_copy(near, away, row_sems.at[i]))
@@ -259,12 +259,12 @@
 def wide_kernel(
     heads, span, recv_ref, mine_ref, theirs_ref, flat
 ):
-    part, slots, dh = heads // 2, recv_ref.shape[1], recv_ref.shape[2]
+    part, slots, dh = heads // 2, recv_ref.shape[0] // span, recv_ref.shape[1]
     scale = dh**-0.5
     me = lax.rem(lax.axis_index("ctx"), span)
     mate = jnp.bitwise_xor(me, 1)
     first = jnp.bitwise_and(me, 1) == 0
-    flat[...] = recv_ref[...].astype(F32).reshape(span * slots, dh)
+    flat[...] = recv_ref[...].astype(F32)
 
     def gathered(slot):
         return flat[pl.ds(slot, span, stride=slots), :]
@@ -492,7 +492,7 @@
         functools.partial(stats_kernel, heads, span),
         "row_stats",
         (
-            pltpu.HBM((span, slots, dh), BF16),
+            pltpu.HBM((span * slots, dh), BF16),
             pltpu.HBM((32, length), F32),
             pltpu.HBM((32, length), F32),
             pltpu.HBM((32, dh), BF16),
@@ -504,7 +504,7 @@
             table,
             pltpu.VMEM((32, dh), BF16),
             pltpu.VMEM((2 * slots, dh), F32),
-            pltpu.VMEM((repeat, slots, dh), BF16),
+            pltpu.VMEM((repeat * slots, dh), BF16),
             pltpu.SemaphoreType.DMA((span // repeat,)),
             pltpu.SemaphoreType.DMA((3,)),
         ],

time: 27.4 us -> 27.4 us (level)
  no operation moved by 1% of the time
where the time goes in v3:
time: 27.4 us; the launch traced here: 27.2 us
  Pallas kernels  14.6 us (53%)
  starting transfers between devices  9.38 us (34%)
  waiting for transfers between devices  2.33 us (9%)
  between operations  0.8 us (3%)
    all_to_all x1, starting transfers between devices, on_device(): lax.all_to_all(load, 'ctx', 0, 0, axis_index_groups=groups, tiled=True)  7.27 us
    pallas_call x1, Pallas kernels, on_device(): call(functools.partial(main_kernel, heads), 'near_levels', (pltpu.HBM((le...  7.03 us
    pallas_call x1, Pallas kernels, on_device(): call(functools.partial(final_kernel, heads), 'join', (pltpu.HBM((length,...  3 us
    pallas_call x1, Pallas kernels, on_device(): call(functools.partial(pack_kernel, heads), 'pack_rows', (pltpu.VMEM((48,...  2.24 us
    pallas_call x1, Pallas kernels, on_device(): call(functools.partial(stats_kernel, heads, span), 'row_stats', (pltpu.HB...  1.7 us
    all_to_all x1, waiting for transfers between devices, on_device(): lax.all_to_all(load, 'ctx', 0, 0, axis_index_groups=groups, tiled=True)  1.47 us
    ppermute x1, waiting for transfers between devices, on_device(): got = lax.ppermute(theirs, 'ctx', mates)  0.84 us
    pallas_call x1, Pallas kernels, on_device(): call(functools.partial(wide_kernel, heads, span), 'third_level', (rows, r...  0.63 us
  transfers between devices with their start and end apart: 7, of which 2 were waited for; matrix products, arithmetic and copies ran while one was open for 0% of the time, Pallas kernels for 43%

profile of v3, /device:TPU:0, one launch (start us, length us, event | category | flops | bytes accessed | tf_op | source)
XLA Modules:
  0.0 27.2 jit_solution(14102786011455269634)
XLA Ops:
  0.6 0.0 copy-start
  0.6 0.0 copy-start.3
  0.7 0.5 %collective-permute-start = (bf16[256,1280]{1,0:T(8,128)(2,1)}, bf16[256,1280]{1,0:T(8,128)(2,1)S(1)}, u32[]{:S(2)}, u32[]{:S(2)}) collective-permute-start(bf16[256,1280]{1,0:T(8,128)(2,1)} %q_ref.3), channel_id=1, source_target_pairs={{0,1},{1,0},{2,3},{3,2},{4,5},{5,4},{6,7},{7,6},{8,9},{9,8},{10,11... | collective-permute-start | bytes 1966088 | tf_op jit(solution)/shard_map/ppermute | solution.py:471
  1.2 0.1 collective-permute-start.1
  1.3 2.2 %pack_rows.1 = (bf16[48,128]{1,0:T(8,128)(2,1)S(1)}, f32[32,256]{1,0:T(8,128)S(1)}, f32[32,256]{1,0:T(8,128)S(1)}) custom-call(s32[2,10]{1,0:T(2,128)} %off_hbm.3, bf16[256,1280]{1,0:T(8,128)(2,1)} %k_hbm.1, bf16[256,1280]{1,0:T(8,128)(2,1)} %v_ref.5, bf16[256,1280]{1,0:T(8,128)(2,1)} %q_ref.3, bf16[256,1280]{1,0:T(8,128)(2,1)} %g_ref.3), custom_call_target="tpu_custom_call" | custom-call | flops 7000000000 | bytes 1000 | tf_op jit(solution)/shard_map/pack_rows/pallas_call | solution.py:474
  3.5 0.0 copy-done.3
  3.5 0.5 %collective-permute-start.3 = (bf16[256,1280]{1,0:T(8,128)(2,1)S(1)}, bf16[256,1280]{1,0:T(8,128)(2,1)}, u32[]{:S(2)}, u32[]{:S(2)}) collective-permute-start(bf16[256,1280]{1,0:T(8,128)(2,1)S(1)} %copy-done.3), channel_id=1, source_target_pairs={{0,1},{1,0},{2,3},{3,2},{4,5},{5,4},{6,7},{7,6},{8,9},{9,8},{10,11... | collective-permute-start | bytes 1966088 | tf_op jit(solution)/shard_map/ppermute | solution.py:489
  4.0 0.1 collective-permute-start.4
  4.1 0.0 collective-permute-done.qf_ref
  4.1 0.0 collective-permute-done.1.gf_ref
  4.1 0.0 copy-start.10
  4.1 1.7 %row_stats.1 = (bf16[768,128]{1,0:T(8,128)(2,1)}, f32[32,256]{1,0:T(8,128)}, f32[32,256]{1,0:T(8,128)}, bf16[32,128]{1,0:T(8,128)(2,1)}) custom-call(bf16[48,128]{1,0:T(8,128)(2,1)S(1)} %get-tuple-element.22.own_ref, f32[32,256]{1,0:T(8,128)S(1)} %get-tuple-element.23.spot_ref, f32[32,256]{1,0:T(8,128)S(1)} %get-tuple-element.24.weight_ref, ...), custom_call_target="tpu_custom_call" | custom-call | flops 1000 | bytes 1000 | tf_op jit(solution)/shard_map/row_stats/pallas_call | solution.py:491
  5.8 7.3 %all-to-all-start = ((bf16[32,24,128]{2,1,0:T(8,128)(2,1)}), bf16[32,24,128]{2,1,0:T(8,128)(2,1)S(1)}, u32[]{:S(2)}, u32[]{:S(2)}) async-start(bf16[32,24,128]{2,1,0:T(8,128)(2,1)} %bitcast.3), calls=%async_computation | async-start | bytes 393216 | tf_op jit(solution)/shard_map/all_to_all | solution.py:515
  13.1 0.0 collective-permute-done.3.vf_hbm
  13.1 0.0 collective-permute-done.4.kf_ref.kf_hbm
  13.2 7.0 %near_levels.1 = (bf16[256,1280]{1,0:T(8,128)(2,1)}, f32[256,1280]{1,0:T(8,128)}, f32[256,1280]{1,0:T(8,128)}, bf16[256,1280]{1,0:T(8,128)(2,1)}, f32[32,256]{1,0:T(8,128)}, /*index=5*/bf16[10,16,128]{2,1,0:T(8,128)(2,1)}) custom-call(s32[2,10]{1,0:T(2,128)} %off_hbm.3, f32[32,256]{1,0:T(8,128)} %get-tuple-element.29.after_ref.s_ref, ...), custom_call_target="tpu_custom_call" | custom-call | flops 7000000000 | bytes 1000 | tf_op jit(solution)/shard_map/near_levels/pallas_call | solution.py:519
  20.2 0.3 %collective-permute-start.5 = (bf16[256,1280]{1,0:T(8,128)(2,1)}, bf16[256,1280]{1,0:T(8,128)(2,1)S(1)}, u32[]{:S(2)}, u32[]{:S(2)}) collective-permute-start(bf16[256,1280]{1,0:T(8,128)(2,1)} %get-tuple-element.36), channel_id=1, source_target_pairs={{0,1},{1,0},{2,3},{3,2},{4,5},{5,4},{6,7},{7,6},{8,9},{9,8},{10,11... | collective-permute-start | bytes 1966088 | tf_op jit(solution)/shard_map/ppermute | solution.py:552
  20.5 1.5 %all-to-all-done = bf16[32,24,128]{2,1,0:T(8,128)(2,1)S(1)} async-done(((bf16[32,24,128]{2,1,0:T(8,128)(2,1)}), bf16[32,24,128]{2,1,0:T(8,128)(2,1)S(1)}, u32[]{:S(2)}, u32[]{:S(2)}) %all-to-all-start) | async-done | bytes 196640 | tf_op jit(solution)/shard_map/all_to_all | solution.py:515
  22.0 0.6 %third_level.1 = (f32[32,128]{1,0:T(8,128)S(1)}, f32[32,128]{1,0:T(8,128)S(1)}) custom-call(bf16[768,128]{1,0:T(8,128)(2,1)S(1)} %bitcast.2), custom_call_target="tpu_custom_call" | custom-call | flops 7000000000 | bytes 1000 | tf_op jit(solution)/shard_map/third_level/pallas_call | solution.py:553
  22.7 0.6 %collective-permute-start.2 = (f32[32,128]{1,0:T(8,128)S(1)}, f32[32,128]{1,0:T(8,128)S(1)}, u32[]{:S(2)}, u32[]{:S(2)}) collective-permute-start(f32[32,128]{1,0:T(8,128)S(1)} %get-tuple-element.27), channel_id=1, source_target_pairs={{0,1},{1,0},{2,3},{3,2},{4,5},{5,4},{6,7},{7,6},{8,9},{9,8},{10,11... | collective-permute-start | bytes 49160 | tf_op jit(solution)/shard_map/ppermute | solution.py:562
  23.3 0.8 %collective-permute-done.2.got_ref = f32[32,128]{1,0:T(8,128)S(1)} collective-permute-done((f32[32,128]{1,0:T(8,128)S(1)}, f32[32,128]{1,0:T(8,128)S(1)}, u32[]{:S(2)}, u32[]{:S(2)}) %collective-permute-start.2) | collective-permute-done | bytes 16416 | tf_op jit(solution)/shard_map/ppermute | solution.py:562
  24.1 0.0 collective-permute-done.5.ret
  24.1 0.0 copy-done.1
  24.2 3.0 %join.1 = (bf16[256,1280]{1,0:T(8,128)(2,1)}, bf16[256,1280]{1,0:T(8,128)(2,1)}, bf16[256,1280]{1,0:T(8,128)(2,1)}) custom-call(s32[2,10]{1,0:T(2,128)} %off_hbm.3, f32[32,128]{1,0:T(8,128)S(1)} %get-tuple-element.26.mine_ref, f32[32,128]{1,0:T(8,128)S(1)} %collective-permute-done.2.got_ref, ...), custom_call_target="tpu_custom_call", output_to_operand_aliasing={{0}: (16, {})} | custom-call | flops 1000 | bytes 1000 | tf_op jit(solution)/shard_map/join/pallas_call | solution.py:563
  (17 shorter events, 0.0 us)
Async XLA Ops:
  0.6 3.4 %copy-start = (bf16[256,1280]{1,0:T(8,128)(2,1)S(1)}, bf16[256,1280]{1,0:T(8,128)(2,1)}, u32[]{:S(2)}) copy-start(bf16[256,1280]{1,0:T(8,128)(2,1)} %k_hbm.1) | copy-start | bytes 1966084
  0.6 2.9 %copy-start.3 = (bf16[256,1280]{1,0:T(8,128)(2,1)S(1)}, bf16[256,1280]{1,0:T(8,128)(2,1)}, u32[]{:S(2)}) copy-start(bf16[256,1280]{1,0:T(8,128)(2,1)} %v_ref.5) | copy-start | bytes 1966084
  0.7 3.4 %collective-permute-start = (bf16[256,1280]{1,0:T(8,128)(2,1)}, bf16[256,1280]{1,0:T(8,128)(2,1)S(1)}, u32[]{:S(2)}, u32[]{:S(2)}) collective-permute-start(bf16[256,1280]{1,0:T(8,128)(2,1)} %q_ref.3), channel_id=1, source_target_pairs={{0,1},{1,0},{2,3},{3,2},{4,5},{5,4},{6,7},{7,6},{8,9},{9,8},{10,11... | collective-permute-start | bytes 1966088 | tf_op jit(solution)/shard_map/ppermute | solution.py:471
  1.2 2.9 %collective-permute-start.1 = (bf16[256,1280]{1,0:T(8,128)(2,1)}, bf16[256,1280]{1,0:T(8,128)(2,1)S(1)}, u32[]{:S(2)}, u32[]{:S(2)}) collective-permute-start(bf16[256,1280]{1,0:T(8,128)(2,1)} %g_ref.3), channel_id=1, source_target_pairs={{0,1},{1,0},{2,3},{3,2},{4,5},{5,4},{6,7},{7,6},{8,9},{9,8},{10,11... | collective-permute-start | bytes 1966088 | tf_op jit(solution)/shard_map/ppermute | solution.py:472
  3.5 9.6 %collective-permute-start.3 = (bf16[256,1280]{1,0:T(8,128)(2,1)S(1)}, bf16[256,1280]{1,0:T(8,128)(2,1)}, u32[]{:S(2)}, u32[]{:S(2)}) collective-permute-start(bf16[256,1280]{1,0:T(8,128)(2,1)S(1)} %copy-done.3), channel_id=1, source_target_pairs={{0,1},{1,0},{2,3},{3,2},{4,5},{5,4},{6,7},{7,6},{8,9},{9,8},{10,11... | collective-permute-start | bytes 1966088 | tf_op jit(solution)/shard_map/ppermute | solution.py:489
  4.0 9.1 %collective-permute-start.4 = (bf16[256,1280]{1,0:T(8,128)(2,1)S(1)}, bf16[256,1280]{1,0:T(8,128)(2,1)S(1)}, u32[]{:S(2)}, u32[]{:S(2)}) collective-permute-start(bf16[256,1280]{1,0:T(8,128)(2,1)S(1)} %copy-done), channel_id=1, source_target_pairs={{0,1},{1,0},{2,3},{3,2},{4,5},{5,4},{6,7},{7,6},{8,9},{9,8},{10,11... | collective-permute-start | bytes 1966088 | tf_op jit(solution)/shard_map/ppermute | solution.py:488
  4.1 9.0 %copy-start.9 = (bf16[256,1280]{1,0:T(8,128)(2,1)S(1)}, bf16[256,1280]{1,0:T(8,128)(2,1)}, u32[]{:S(2)}) copy-start(bf16[256,1280]{1,0:T(8,128)(2,1)} %q_ref.3) | copy-start | bytes 1966084
  4.1 9.0 %copy-start.10 = (bf16[256,1280]{1,0:T(8,128)(2,1)S(1)}, bf16[256,1280]{1,0:T(8,128)(2,1)}, u32[]{:S(2)}) copy-start(bf16[256,1280]{1,0:T(8,128)(2,1)} %g_ref.3) | copy-start | bytes 1966084
  5.8 16.2 %all-to-all-start = ((bf16[32,24,128]{2,1,0:T(8,128)(2,1)}), bf16[32,24,128]{2,1,0:T(8,128)(2,1)S(1)}, u32[]{:S(2)}, u32[]{:S(2)}) async-start(bf16[32,24,128]{2,1,0:T(8,128)(2,1)} %bitcast.3), calls=%async_computation | async-start | bytes 393216 | tf_op jit(solution)/shard_map/all_to_all | solution.py:515
  13.1 7.1 %copy-start.4 = (bf16[256,1280]{1,0:T(8,128)(2,1)}, bf16[256,1280]{1,0:T(8,128)(2,1)S(1)}, u32[]{:S(2)}) copy-start(bf16[256,1280]{1,0:T(8,128)(2,1)S(1)} %collective-permute-done.4.kf_ref.kf_hbm) | copy-start | bytes 1966084
  20.2 3.9 %collective-permute-start.5 = (bf16[256,1280]{1,0:T(8,128)(2,1)}, bf16[256,1280]{1,0:T(8,128)(2,1)S(1)}, u32[]{:S(2)}, u32[]{:S(2)}) collective-permute-start(bf16[256,1280]{1,0:T(8,128)(2,1)} %get-tuple-element.36), channel_id=1, source_target_pairs={{0,1},{1,0},{2,3},{3,2},{4,5},{5,4},{6,7},{7,6},{8,9},{9,8},{10,11... | collective-permute-start | bytes 1966088 | tf_op jit(solution)/shard_map/ppermute | solution.py:552
  22.0 2.1 %copy-start.1 = (f32[256,1280]{1,0:T(8,128)S(1)}, f32[256,1280]{1,0:T(8,128)}, u32[]{:S(2)}) copy-start(f32[256,1280]{1,0:T(8,128)} %get-tuple-element.33.dki) | copy-start | bytes 3932164
  22.0 2.1 %copy-start.2 = (f32[256,1280]{1,0:T(8,128)S(1)}, f32[256,1280]{1,0:T(8,128)}, u32[]{:S(2)}) copy-start(f32[256,1280]{1,0:T(8,128)} %get-tuple-element.34.dvi) | copy-start | bytes 3932164
  22.0 2.1 %copy-start.5 = (bf16[10,16,128]{2,1,0:T(8,128)(2,1)S(1)}, bf16[10,16,128]{2,1,0:T(8,128)(2,1)}, u32[]{:S(2)}) copy-start(bf16[10,16,128]{2,1,0:T(8,128)(2,1)} %get-tuple-element.35.blocks_in) | copy-start | bytes 122884
  22.0 2.1 %copy-start.6 = (f32[32,256]{1,0:T(8,128)S(1)}, f32[32,256]{1,0:T(8,128)}, u32[]{:S(2)}) copy-start(f32[32,256]{1,0:T(8,128)} %get-tuple-element.29.after_ref.s_ref) | copy-start | bytes 98308
  22.0 2.1 %copy-start.7 = (f32[32,256]{1,0:T(8,128)S(1)}, f32[32,256]{1,0:T(8,128)}, u32[]{:S(2)}) copy-start(f32[32,256]{1,0:T(8,128)} %get-tuple-element.30.dp_ref) | copy-start | bytes 98308
  22.0 2.1 %copy-start.8 = (bf16[32,128]{1,0:T(8,128)(2,1)S(1)}, bf16[32,128]{1,0:T(8,128)(2,1)}, u32[]{:S(2)}) copy-start(bf16[32,128]{1,0:T(8,128)(2,1)} %get-tuple-element.28.far_ref) | copy-start | bytes 24580
  22.7 1.5 %collective-permute-start.2 = (f32[32,128]{1,0:T(8,128)S(1)}, f32[32,128]{1,0:T(8,128)S(1)}, u32[]{:S(2)}, u32[]{:S(2)}) collective-permute-start(f32[32,128]{1,0:T(8,128)S(1)} %get-tuple-element.27), channel_id=1, source_target_pairs={{0,1},{1,0},{2,3},{3,2},{4,5},{5,4},{6,7},{7,6},{8,9},{9,8},{10,11... | collective-permute-start | bytes 49160 | tf_op jit(solution)/shard_map/ppermute | solution.py:562

commit v4 on v3

--- a/solution.py
+++ b/solution.py
@@ -207,16 +207,36 @@
     yield
 
 
+def row_terms(heads, scores, products, weight, keys):
+    masked = jnp.where(weight > 0.0, scores, NEG)
+    peak = jnp.max(masked, axis=1, keepdims=True)
+    e = jnp.exp2(masked - peak) * weight
+    parts = []
+    for x in (e * products, e):
+        high = x.astype(BF16)
+        parts += [high, (x - high.astype(F32)).astype(BF16)]
+    sums = dot_nn(jnp.concatenate(parts, axis=0), keys)
+    first = own_columns(sums[0:16, :] + sums[16:32, :], heads)
+    second = own_columns(sums[32:48, :] + sums[48:64, :], heads)
+    return first, second, peak
+
+
 def main_kernel(
-    heads, off_hbm, after_ref, vf_hbm, own_ref, q_ref, k_ref, v_ref, g_ref, kf_ref,
-    dq_hbm, dk_hbm, dv_hbm, ret_hbm, far_hbm, blocks_hbm,
-    off_ref, vf_ref, dq_ref, dk_ref, dv_ref, ret_ref, far_scores, blocks,
-    off_sem, in_sem, far_sem, block_sem, out_sems,
+    heads, off_hbm, s_hbm, dp_hbm, vf_hbm, own_ref, weight_ref, q_ref, k_ref, v_ref, g_ref, kf_ref,
+    dq_hbm, dk_hbm, dv_hbm, ret_hbm, terms_hbm, blocks_hbm,
+    off_ref, s_ref, dp_ref, vf_ref, dq_ref, dk_ref, dv_ref, ret_ref, terms, blocks,
+    off_sem, in_sem, row_sems, terms_sem, block_sem, out_sems,
 ):
     offsets = pltpu.make_async_copy(off_hbm, off_ref, off_sem)
     offsets.start()
     values = pltpu.make_async_copy(vf_hbm, vf_ref, in_sem)
     values.start()
+    stats = [
+        pltpu.make_async_copy(s_hbm, s_ref, row_sems.at[0]),
+        pltpu.make_async_copy(dp_hbm, dp_ref, row_sems.at[1]),
+    ]
+    for copy in stats:
+        copy.start()
     dh = q_ref.shape[1] // heads
     near = (dq_ref, dk_ref, dv_ref, ret_ref)
     writes = []
@@ -247,9 +267,19 @@
             own = own_ref[...].astype(F32)
             queries = block_rows(own[2 * heads : 2 * heads + 16, :], heads)
             grads = block_rows(own[3 * heads : 3 * heads + 16, :], heads)
-            far_scores[:16, :] = dot_nt(queries, kf_ref[...]) * (dh**-0.5 * LOG2E)
-            far_scores[16:, :] = dot_nt(grads, vf_ref[...])
-            copy = pltpu.make_async_copy(far_scores, far_hbm, far_sem)
+            far_s = dot_nt(queries, kf_ref[...]) * (dh**-0.5 * LOG2E)
+            far_dp = dot_nt(grads, vf_ref[...])
+            for copy in stats:
+                copy.wait()
+            weight = weight_ref[0:16, :]
+            met = (weight > 1.0).astype(F32)
+            near_row = row_terms(heads, s_ref[0:16, :], dp_ref[0:16, :], weight, k_ref[...])
+            far_row = row_terms(heads, far_s, far_dp, met, kf_ref[...])
+            lane = iota((16, dh), 1)
+            peaks = jnp.where(lane == 0, near_row[2], jnp.where(lane == 1, far_row[2], 0.0))
+            for i, term in enumerate(near_row[:2] + far_row[:2] + (peaks,)):
+                terms[16 * i : 16 * i + 16, :] = term
+            copy = pltpu.make_async_copy(terms, terms_hbm, terms_sem)
             copy.start()
             writes.append(copy)
     for copy in writes:
@@ -347,20 +377,12 @@
 
 def final_kernel(
     heads, off_hbm, mine_ref, got_ref, own_ref, far_ref, spot_ref, weight_ref, s_ref, dp_ref,
-    dki, dvi, blocks_in, ret, k_hbm, kf_hbm, far_hbm, dq_in, dq_ref, dk_ref, dv_ref,
-    off_ref, k_ref, kf_ref, far_scores, full, blocks, dko, dvo, off_sem, key_sems, far_sem, block_sems, write_sems,
+    terms_ref, dki, dvi, blocks_in, ret, dq_in, dq_ref, dk_ref, dv_ref,
+    off_ref, full, blocks, dko, dvo, off_sem, block_sems, write_sems,
 ):
     offsets = pltpu.make_async_copy(off_hbm, off_ref, off_sem)
     offsets.start()
-    scores = pltpu.make_async_copy(far_hbm, far_scores, far_sem)
-    scores.start()
-    keys = [
-        pltpu.make_async_copy(k_hbm, k_ref, key_sems.at[0]),
-        pltpu.make_async_copy(kf_hbm, kf_ref, key_sems.at[1]),
-    ]
-    for copy in keys:
-        copy.start()
-    length, dh = k_hbm.shape[0], own_ref.shape[1]
+    length, dh = dki.shape[0], own_ref.shape[1]
     half, part = length // 2, heads // 2
     scale = dh**-0.5
 
@@ -385,10 +407,11 @@
     weight = weight_ref[...]
     p_two = jnp.exp2(jnp.where(weight > 0.0, s_ref[...] - m_two, NEG)) * weight * i_two
     ds_two = scale * p_two * (dp_ref[...] - d_two)
-    met = weight[0:16, :] > 1.0
-    scores.wait()
-    p_far = jnp.exp2(jnp.where(met, far_scores[:16, :] - m_me, NEG)) * i_me
-    ds_far = scale * p_far * (far_scores[16:, :] - d_me)
+    terms = [terms_ref[16 * i : 16 * i + 16, :] for i in range(5)]
+    dq_rows = dq_wide
+    for i in range(2):
+        share = scale * jnp.exp2(terms[4][:, i : i + 1] - m_me) * i_me
+        dq_rows += share * (terms[2 * i] - d_me * terms[2 * i + 1])
     spot = spot_ref[...]
     offsets.wait()
     writes = []
@@ -417,12 +440,6 @@
             copy = pltpu.make_async_copy(out.at[:, chunk], out_ref.at[:, chunk], sem)
             copy.start()
             writes.append(copy)
-    for copy in keys:
-        copy.wait()
-    dq_rows = dq_wide + own_columns(
-        dot_nn(ds_two[0:16, :].astype(BF16), k_ref[...]) + dot_nn(ds_far.astype(BF16), kf_ref[...]),
-        heads,
-    )
     for h in range(heads):
         here = iota((16, dh), 0) == jnp.bitwise_and(off_ref[1, h], 15)
         block = jnp.where(here, dq_rows[h : h + 1, :], blocks_in[h].astype(F32))
@@ -516,7 +533,7 @@
     whole = pltpu.VMEM((length, width), BF16)
     wide = pltpu.VMEM((length, width), F32)
     rows = pltpu.VMEM((32, dh), F32)
-    dq, dk, dv, partial, far_scores, blocks = call(
+    dq, dk, dv, partial, terms, blocks = call(
         functools.partial(main_kernel, heads),
         "near_levels",
         (
@@ -524,30 +541,33 @@
             pltpu.HBM((length, width), F32),
             pltpu.HBM((length, width), F32),
             pltpu.HBM((length, width), BF16),
-            pltpu.HBM((32, length), F32),
+            pltpu.HBM((80, dh), F32),
             pltpu.HBM((heads, 16, dh), BF16),
         ),
-        [hbm] * 3 + [vmem] * 6,
+        [hbm] * 4 + [vmem] * 7,
         (hbm,) * 6,
         [
             pltpu.SMEM(offsets.shape, jnp.int32),
+            table,
+            table,
             whole,
             whole,
             wide,
             wide,
             whole,
-            pltpu.VMEM((32, length), F32),
+            pltpu.VMEM((80, dh), F32),
             pltpu.VMEM((heads, 16, dh), BF16),
             pltpu.SemaphoreType.DMA,
             pltpu.SemaphoreType.DMA,
+            pltpu.SemaphoreType.DMA((2,)),
             pltpu.SemaphoreType.DMA,
             pltpu.SemaphoreType.DMA,
             pltpu.SemaphoreType.DMA((heads // 2, 4)),
         ],
         cost=large,
     )(
-        *far_memory(offsets, s_rows, value_far),
-        *near_memory(own, query, key, value, grad_out, key_far),
+        *far_memory(offsets, s_rows, dp_rows, value_far),
+        *near_memory(own, weight, query, key, value, grad_out, key_far),
     )
     returned = lax.ppermute(partial, "ctx", mates)
     mine, theirs = call(
@@ -564,29 +584,24 @@
         functools.partial(final_kernel, heads),
         "join",
         (pltpu.HBM((length, width), BF16),) * 3,
-        [hbm] + [vmem] * 12 + [hbm] * 4,
+        [hbm] + [vmem] * 13 + [hbm],
         (hbm,) * 3,
         [
             pltpu.SMEM(offsets.shape, jnp.int32),
-            whole,
-            whole,
-            pltpu.VMEM((32, length), F32),
             pltpu.VMEM((64, dh), F32),
             pltpu.VMEM((heads, 16, dh), BF16),
             whole,
             whole,
             pltpu.SemaphoreType.DMA,
-            pltpu.SemaphoreType.DMA((2,)),
-            pltpu.SemaphoreType.DMA,
             pltpu.SemaphoreType.DMA((heads,)),
             pltpu.SemaphoreType.DMA((2, heads // 2)),
         ],
-        input_output_aliases={16: 0},
+        input_output_aliases={14: 0},
     )(
         *far_memory(offsets),
-        *near_memory(mine, got, own, far, spot, weight, s_rows, dp_rows),
+        *near_memory(mine, got, own, far, spot, weight, s_rows, dp_rows, terms),
         *near_memory(dk, dv, blocks, returned),
-        *far_memory(key, key_far, far_scores, dq),
+        *far_memory(dq),
     )
 
 

time: 27.4 us -> 26.9 us (0.982)
  waiting for transfers between devices: 2.33 us -> 1.93 us
    pallas_call x1, Pallas kernels: 3 us -> 2.42 us  [on_device(): call(functools.partial(final_kernel, heads), 'join', (pltpu.HBM((length,...]
    pallas_call x1, Pallas kernels: 7.03 us -> 7.45 us  [on_device(): call(functools.partial(main_kernel, heads), 'near_levels', (pltpu.HBM((le...]
    all_to_all x1, waiting for transfers between devices: 1.47 us -> 1.08 us  [on_device(): lax.all_to_all(load, 'ctx', 0, 0, axis_index_groups=groups, tiled=True)]
  transfers between devices with their start and end apart: 7 -> 7, of which waited for: 2 -> 2; matrix products, arithmetic and copies ran while one was open for 0% -> 0% of each run, Pallas kernels for 43% -> 45%
where the time goes in v4:
time: 26.9 us; the launch traced here: 26.6 us
  Pallas kernels  14.4 us (54%)
  starting transfers between devices  9.37 us (35%)
  waiting for transfers between devices  1.93 us (7%)
  between operations  0.8 us (3%)
    pallas_call x1, Pallas kernels, on_device(): call(functools.partial(main_kernel, heads), 'near_levels', (pltpu.HBM((le...  7.45 us
    all_to_all x1, starting transfers between devices, on_device(): lax.all_to_all(load, 'ctx', 0, 0, axis_index_groups=groups, tiled=True)  7.27 us
    pallas_call x1, Pallas kernels, on_device(): call(functools.partial(final_kernel, heads), 'join', (pltpu.HBM((length,...  2.42 us
    pallas_call x1, Pallas kernels, on_device(): call(functools.partial(pack_kernel, heads), 'pack_rows', (pltpu.VMEM((48,...  2.24 us
    pallas_call x1, Pallas kernels, on_device(): call(functools.partial(stats_kernel, heads, span), 'row_stats', (pltpu.HB...  1.7 us
    all_to_all x1, waiting for transfers between devices, on_device(): lax.all_to_all(load, 'ctx', 0, 0, axis_index_groups=groups, tiled=True)  1.08 us
    ppermute x1, waiting for transfers between devices, on_device(): got = lax.ppermute(theirs, 'ctx', mates)  0.84 us
    pallas_call x1, Pallas kernels, on_device(): call(functools.partial(wide_kernel, heads, span), 'third_level', (rows, r...  0.63 us
  transfers between devices with their start and end apart: 7, of which 2 were waited for; matrix products, arithmetic and copies ran while one was open for 0% of the time, Pallas kernels for 45%

profile of v4, /device:TPU:0, one launch (start us, length us, event | category | flops | bytes accessed | tf_op | source)
XLA Modules:
  0.0 26.6 jit_solution(7628575802442031477)
XLA Ops:
  0.7 0.5 %collective-permute-start = (bf16[256,1280]{1,0:T(8,128)(2,1)}, bf16[256,1280]{1,0:T(8,128)(2,1)S(1)}, u32[]{:S(2)}, u32[]{:S(2)}) collective-permute-start(bf16[256,1280]{1,0:T(8,128)(2,1)} %q_ref.3), channel_id=1, source_target_pairs={{0,1},{1,0},{2,3},{3,2},{4,5},{5,4},{6,7},{7,6},{8,9},{9,8},{10,11... | collective-permute-start | bytes 1966088 | tf_op jit(solution)/shard_map/ppermute | solution.py:488
  1.2 0.1 collective-permute-start.1
  1.2 2.2 %pack_rows.1 = (bf16[48,128]{1,0:T(8,128)(2,1)S(1)}, f32[32,256]{1,0:T(8,128)S(1)}, f32[32,256]{1,0:T(8,128)S(1)}) custom-call(s32[2,10]{1,0:T(2,128)} %off_hbm.3, bf16[256,1280]{1,0:T(8,128)(2,1)} %k_ref.5, bf16[256,1280]{1,0:T(8,128)(2,1)} %v_ref.5, bf16[256,1280]{1,0:T(8,128)(2,1)} %q_ref.3, bf16[256,1280]{1,0:T(8,128)(2,1)} %g_ref.3), custom_call_target="tpu_custom_call" | custom-call | flops 7000000000 | bytes 1000 | tf_op jit(solution)/shard_map/pack_rows/pallas_call | solution.py:491
  3.5 0.5 %collective-permute-start.3 = (bf16[256,1280]{1,0:T(8,128)(2,1)S(1)}, bf16[256,1280]{1,0:T(8,128)(2,1)}, u32[]{:S(2)}, u32[]{:S(2)}) collective-permute-start(bf16[256,1280]{1,0:T(8,128)(2,1)S(1)} %copy-done.3), channel_id=1, source_target_pairs={{0,1},{1,0},{2,3},{3,2},{4,5},{5,4},{6,7},{7,6},{8,9},{9,8},{10,11... | collective-permute-start | bytes 1966088 | tf_op jit(solution)/shard_map/ppermute | solution.py:506
  4.0 0.1 collective-permute-start.4
  4.1 0.0 collective-permute-done.qf_ref
  4.1 0.0 collective-permute-done.1.gf_ref
  4.1 0.0 copy-start.10
  4.1 1.7 %row_stats.1 = (bf16[768,128]{1,0:T(8,128)(2,1)}, f32[32,256]{1,0:T(8,128)}, f32[32,256]{1,0:T(8,128)}, bf16[32,128]{1,0:T(8,128)(2,1)}) custom-call(bf16[48,128]{1,0:T(8,128)(2,1)S(1)} %get-tuple-element.22.own_ref, f32[32,256]{1,0:T(8,128)S(1)} %get-tuple-element.23.spot_ref, f32[32,256]{1,0:T(8,128)S(1)} %get-tuple-element.24.weight_ref, ...), custom_call_target="tpu_custom_call" | custom-call | flops 1000 | bytes 1000 | tf_op jit(solution)/shard_map/row_stats/pallas_call | solution.py:508
  5.8 7.3 %all-to-all-start = ((bf16[32,24,128]{2,1,0:T(8,128)(2,1)}), bf16[32,24,128]{2,1,0:T(8,128)(2,1)S(1)}, u32[]{:S(2)}, u32[]{:S(2)}) async-start(bf16[32,24,128]{2,1,0:T(8,128)(2,1)} %bitcast.3), calls=%async_computation | async-start | bytes 393216 | tf_op jit(solution)/shard_map/all_to_all | solution.py:532
  13.1 0.0 collective-permute-done.3.vf_hbm
  13.1 0.0 collective-permute-done.4.kf_ref
  13.2 7.5 %near_levels.1 = (bf16[256,1280]{1,0:T(8,128)(2,1)}, f32[256,1280]{1,0:T(8,128)}, f32[256,1280]{1,0:T(8,128)}, bf16[256,1280]{1,0:T(8,128)(2,1)}, f32[80,128]{1,0:T(8,128)}, /*index=5*/bf16[10,16,128]{2,1,0:T(8,128)(2,1)}) custom-call(s32[2,10]{1,0:T(2,128)} %off_hbm.3, f32[32,256]{1,0:T(8,128)} %get-tuple-element.29.s_hbm.s_ref, ...), custom_call_target="tpu_custom_call" | custom-call | flops 7000000000 | bytes 1000 | tf_op jit(solution)/shard_map/near_levels/pallas_call | solution.py:536
  20.6 0.3 %collective-permute-start.5 = (bf16[256,1280]{1,0:T(8,128)(2,1)}, bf16[256,1280]{1,0:T(8,128)(2,1)S(1)}, u32[]{:S(2)}, u32[]{:S(2)}) collective-permute-start(bf16[256,1280]{1,0:T(8,128)(2,1)} %get-tuple-element.37), channel_id=1, source_target_pairs={{0,1},{1,0},{2,3},{3,2},{4,5},{5,4},{6,7},{7,6},{8,9},{9,8},{10,11... | collective-permute-start | bytes 1966088 | tf_op jit(solution)/shard_map/ppermute | solution.py:572
  20.9 1.1 %all-to-all-done = bf16[32,24,128]{2,1,0:T(8,128)(2,1)S(1)} async-done(((bf16[32,24,128]{2,1,0:T(8,128)(2,1)}), bf16[32,24,128]{2,1,0:T(8,128)(2,1)S(1)}, u32[]{:S(2)}, u32[]{:S(2)}) %all-to-all-start) | async-done | bytes 196640 | tf_op jit(solution)/shard_map/all_to_all | solution.py:532
  22.0 0.6 %third_level.1 = (f32[32,128]{1,0:T(8,128)S(1)}, f32[32,128]{1,0:T(8,128)S(1)}) custom-call(bf16[768,128]{1,0:T(8,128)(2,1)S(1)} %bitcast.2), custom_call_target="tpu_custom_call" | custom-call | flops 7000000000 | bytes 1000 | tf_op jit(solution)/shard_map/third_level/pallas_call | solution.py:573
  22.7 0.6 %collective-permute-start.2 = (f32[32,128]{1,0:T(8,128)S(1)}, f32[32,128]{1,0:T(8,128)S(1)}, u32[]{:S(2)}, u32[]{:S(2)}) collective-permute-start(f32[32,128]{1,0:T(8,128)S(1)} %get-tuple-element.27), channel_id=1, source_target_pairs={{0,1},{1,0},{2,3},{3,2},{4,5},{5,4},{6,7},{7,6},{8,9},{9,8},{10,11... | collective-permute-start | bytes 49160 | tf_op jit(solution)/shard_map/ppermute | solution.py:582
  23.3 0.8 %collective-permute-done.2.got_ref = f32[32,128]{1,0:T(8,128)S(1)} collective-permute-done((f32[32,128]{1,0:T(8,128)S(1)}, f32[32,128]{1,0:T(8,128)S(1)}, u32[]{:S(2)}, u32[]{:S(2)}) %collective-permute-start.2) | collective-permute-done | bytes 16416 | tf_op jit(solution)/shard_map/ppermute | solution.py:582
  24.1 0.0 collective-permute-done.5.ret
  24.1 0.0 copy-done.5
  24.1 0.0 copy-done.6
  24.2 0.0 copy-done.7
  24.2 0.0 copy-done.8
  24.2 2.4 %join.1 = (bf16[256,1280]{1,0:T(8,128)(2,1)}, bf16[256,1280]{1,0:T(8,128)(2,1)}, bf16[256,1280]{1,0:T(8,128)(2,1)}) custom-call(s32[2,10]{1,0:T(2,128)} %off_hbm.3, f32[32,128]{1,0:T(8,128)S(1)} %get-tuple-element.26.mine_ref, f32[32,128]{1,0:T(8,128)S(1)} %collective-permute-done.2.got_ref, ...), custom_call_target="tpu_custom_call", output_to_operand_aliasing={{0}: (14, {})} | custom-call | flops 1000 | bytes 1000 | tf_op jit(solution)/shard_map/join/pallas_call | solution.py:583
  (17 shorter events, 0.0 us)
Async XLA Ops:
  0.6 2.9 %copy-start.3 = (bf16[256,1280]{1,0:T(8,128)(2,1)S(1)}, bf16[256,1280]{1,0:T(8,128)(2,1)}, u32[]{:S(2)}) copy-start(bf16[256,1280]{1,0:T(8,128)(2,1)} %v_ref.5) | copy-start | bytes 1966084
  0.6 3.4 %copy-start.2 = (bf16[256,1280]{1,0:T(8,128)(2,1)S(1)}, bf16[256,1280]{1,0:T(8,128)(2,1)}, u32[]{:S(2)}) copy-start(bf16[256,1280]{1,0:T(8,128)(2,1)} %k_ref.5) | copy-start | bytes 1966084
  0.7 3.4 %collective-permute-start = (bf16[256,1280]{1,0:T(8,128)(2,1)}, bf16[256,1280]{1,0:T(8,128)(2,1)S(1)}, u32[]{:S(2)}, u32[]{:S(2)}) collective-permute-start(bf16[256,1280]{1,0:T(8,128)(2,1)} %q_ref.3), channel_id=1, source_target_pairs={{0,1},{1,0},{2,3},{3,2},{4,5},{5,4},{6,7},{7,6},{8,9},{9,8},{10,11... | collective-permute-start | bytes 1966088 | tf_op jit(solution)/shard_map/ppermute | solution.py:488
  1.2 2.9 %collective-permute-start.1 = (bf16[256,1280]{1,0:T(8,128)(2,1)}, bf16[256,1280]{1,0:T(8,128)(2,1)S(1)}, u32[]{:S(2)}, u32[]{:S(2)}) collective-permute-start(bf16[256,1280]{1,0:T(8,128)(2,1)} %g_ref.3), channel_id=1, source_target_pairs={{0,1},{1,0},{2,3},{3,2},{4,5},{5,4},{6,7},{7,6},{8,9},{9,8},{10,11... | collective-permute-start | bytes 1966088 | tf_op jit(solution)/shard_map/ppermute | solution.py:489
  3.5 9.6 %collective-permute-start.3 = (bf16[256,1280]{1,0:T(8,128)(2,1)S(1)}, bf16[256,1280]{1,0:T(8,128)(2,1)}, u32[]{:S(2)}, u32[]{:S(2)}) collective-permute-start(bf16[256,1280]{1,0:T(8,128)(2,1)S(1)} %copy-done.3), channel_id=1, source_target_pairs={{0,1},{1,0},{2,3},{3,2},{4,5},{5,4},{6,7},{7,6},{8,9},{9,8},{10,11... | collective-permute-start | bytes 1966088 | tf_op jit(solution)/shard_map/ppermute | solution.py:506
  4.0 9.1 %collective-permute-start.4 = (bf16[256,1280]{1,0:T(8,128)(2,1)S(1)}, bf16[256,1280]{1,0:T(8,128)(2,1)S(1)}, u32[]{:S(2)}, u32[]{:S(2)}) collective-permute-start(bf16[256,1280]{1,0:T(8,128)(2,1)S(1)} %copy-done.2), channel_id=1, source_target_pairs={{0,1},{1,0},{2,3},{3,2},{4,5},{5,4},{6,7},{7,6},{8,9},{9,8},{10,11... | collective-permute-start | bytes 1966088 | tf_op jit(solution)/shard_map/ppermute | solution.py:505
  4.1 9.0 %copy-start.9 = (bf16[256,1280]{1,0:T(8,128)(2,1)S(1)}, bf16[256,1280]{1,0:T(8,128)(2,1)}, u32[]{:S(2)}) copy-start(bf16[256,1280]{1,0:T(8,128)(2,1)} %q_ref.3) | copy-start | bytes 1966084
  4.1 9.0 %copy-start.10 = (bf16[256,1280]{1,0:T(8,128)(2,1)S(1)}, bf16[256,1280]{1,0:T(8,128)(2,1)}, u32[]{:S(2)}) copy-start(bf16[256,1280]{1,0:T(8,128)(2,1)} %g_ref.3) | copy-start | bytes 1966084
  5.8 16.2 %all-to-all-start = ((bf16[32,24,128]{2,1,0:T(8,128)(2,1)}), bf16[32,24,128]{2,1,0:T(8,128)(2,1)S(1)}, u32[]{:S(2)}, u32[]{:S(2)}) async-start(bf16[32,24,128]{2,1,0:T(8,128)(2,1)} %bitcast.3), calls=%async_computation | async-start | bytes 393216 | tf_op jit(solution)/shard_map/all_to_all | solution.py:532
  20.6 3.5 %collective-permute-start.5 = (bf16[256,1280]{1,0:T(8,128)(2,1)}, bf16[256,1280]{1,0:T(8,128)(2,1)S(1)}, u32[]{:S(2)}, u32[]{:S(2)}) collective-permute-start(bf16[256,1280]{1,0:T(8,128)(2,1)} %get-tuple-element.37), channel_id=1, source_target_pairs={{0,1},{1,0},{2,3},{3,2},{4,5},{5,4},{6,7},{7,6},{8,9},{9,8},{10,11... | collective-permute-start | bytes 1966088 | tf_op jit(solution)/shard_map/ppermute | solution.py:572
  22.0 2.1 %copy-start = (f32[256,1280]{1,0:T(8,128)S(1)}, f32[256,1280]{1,0:T(8,128)}, u32[]{:S(2)}) copy-start(f32[256,1280]{1,0:T(8,128)} %get-tuple-element.34.dki) | copy-start | bytes 3932164
  22.0 2.1 %copy-start.1 = (f32[256,1280]{1,0:T(8,128)S(1)}, f32[256,1280]{1,0:T(8,128)}, u32[]{:S(2)}) copy-start(f32[256,1280]{1,0:T(8,128)} %get-tuple-element.35.dvi) | copy-start | bytes 3932164
  22.0 2.1 %copy-start.4 = (f32[80,128]{1,0:T(8,128)S(1)}, f32[80,128]{1,0:T(8,128)}, u32[]{:S(2)}) copy-start(f32[80,128]{1,0:T(8,128)} %get-tuple-element.33.terms_ref) | copy-start | bytes 122884
  22.0 2.1 %copy-start.5 = (bf16[10,16,128]{2,1,0:T(8,128)(2,1)S(1)}, bf16[10,16,128]{2,1,0:T(8,128)(2,1)}, u32[]{:S(2)}) copy-start(bf16[10,16,128]{2,1,0:T(8,128)(2,1)} %get-tuple-element.36.blocks_in) | copy-start | bytes 122884
  22.0 2.1 %copy-start.6 = (f32[32,256]{1,0:T(8,128)S(1)}, f32[32,256]{1,0:T(8,128)}, u32[]{:S(2)}) copy-start(f32[32,256]{1,0:T(8,128)} %get-tuple-element.29.s_hbm.s_ref) | copy-start | bytes 98308
  22.0 2.1 %copy-start.7 = (f32[32,256]{1,0:T(8,128)S(1)}, f32[32,256]{1,0:T(8,128)}, u32[]{:S(2)}) copy-start(f32[32,256]{1,0:T(8,128)} %get-tuple-element.30.dp_hbm.dp_ref) | copy-start | bytes 98308
  22.0 2.1 %copy-start.8 = (bf16[32,128]{1,0:T(8,128)(2,1)S(1)}, bf16[32,128]{1,0:T(8,128)(2,1)}, u32[]{:S(2)}) copy-start(bf16[32,128]{1,0:T(8,128)(2,1)} %get-tuple-element.28.far_ref) | copy-start | bytes 24580
  22.7 1.5 %collective-permute-start.2 = (f32[32,128]{1,0:T(8,128)S(1)}, f32[32,128]{1,0:T(8,128)S(1)}, u32[]{:S(2)}, u32[]{:S(2)}) collective-permute-start(f32[32,128]{1,0:T(8,128)S(1)} %get-tuple-element.27), channel_id=1, source_target_pairs={{0,1},{1,0},{2,3},{3,2},{4,5},{5,4},{6,7},{7,6},{8,9},{9,8},{10,11... | collective-permute-start | bytes 49160 | tf_op jit(solution)/shard_map/ppermute | solution.py:582

commit v5 on v4

--- a/solution.py
+++ b/solution.py
@@ -68,11 +68,11 @@
 
 
 def pack_kernel(
-    heads, off_ref, k_ref, v_ref, q_ref, g_ref, out_ref, spot_ref, weight_ref, buf, acc, sems
+    heads, off_ref, q_ref, g_ref, out_ref, spot_ref, weight_ref, buf, acc, sems
 ):
-    length, dh = k_ref.shape[0], out_ref.shape[1]
+    length, dh = q_ref.shape[0], out_ref.shape[1]
     copies = []
-    for s, ref in enumerate((k_ref, v_ref, q_ref, g_ref)):
+    for s, ref in enumerate((q_ref, g_ref)):
         for h in range(heads):
             base = pl.multiple_of(jnp.bitwise_and(off_ref[1, h], ~15), 16)
             slot = s * heads + h
@@ -86,13 +86,13 @@
     weight_ref[...] = row_weights(off_ref, heads, length)
     acc[...] = jnp.zeros_like(acc)
     row = iota((16, dh), 0)
-    for s in range(4):
+    for s in range(2):
         for h in range(heads):
             slot = s * heads + h
             copies[slot].wait()
             own = row == jnp.bitwise_and(off_ref[1, h], 15)
             block = jnp.where(own, buf[slot].astype(F32), 0.0)
-            acc[slot : slot + 1, :] = jnp.sum(block, axis=0, keepdims=True)
+            acc[16 * s + h : 16 * s + h + 1, :] = jnp.sum(block, axis=0, keepdims=True)
     out_ref[...] = acc[...].astype(BF16)
 
 
@@ -105,21 +105,23 @@
     own = own_ref[...].astype(F32)
     spot = spot_ref[0:16, :].astype(BF16)
 
-    def both_rows(array, whole, first):
+    def both_rows(whole, first):
         far = own_columns(dot_nn(spot, whole), heads)
         far_ref[first : first + 16, :] = far.astype(BF16)
-        near = own[array * heads : array * heads + 16, :]
+        near = own[first : first + 16, :]
         return jnp.concatenate([block_rows(near, heads), block_rows(far, heads)], axis=0)
 
-    queries, grads = both_rows(2, qf_ref[...], 0), both_rows(3, gf_ref[...], 16)
+    queries, grads = both_rows(qf_ref[...], 0), both_rows(gf_ref[...], 16)
     s = dot_nt(queries, k_ref[...]) * (dh**-0.5 * LOG2E)
     dp = dot_nt(grads, v_ref[...])
     s_ref[...] = s
     dp_ref[...] = dp
+    rows = [own_columns(dot_nn(spot, ref[...]), heads) for ref in (k_ref, v_ref)]
+    rows += [own[0:16, :], own[16:32, :]]
     for i in range(4):
         for c in range(2):
-            slot, row = c * slots + i * part, i * heads + c * part
-            acc[slot : slot + part, :] = own[row : row + part, :]
+            slot = c * slots + i * part
+            acc[slot : slot + part, :] = rows[i][c * part : (c + 1) * part, :]
     weight = weight_ref[...]
     masked = jnp.where(weight > 0.0, s, NEG)
     m = jnp.max(masked, axis=1, keepdims=True)
@@ -265,8 +267,7 @@
                 next(work[h])
         if turn == steps:
             own = own_ref[...].astype(F32)
-            queries = block_rows(own[2 * heads : 2 * heads + 16, :], heads)
-            grads = block_rows(own[3 * heads : 3 * heads + 16, :], heads)
+            queries, grads = block_rows(own[:16, :], heads), block_rows(own[16:, :], heads)
             far_s = dot_nt(queries, kf_ref[...]) * (dh**-0.5 * LOG2E)
             far_dp = dot_nt(grads, vf_ref[...])
             for copy in stats:
@@ -417,7 +418,7 @@
     writes = []
 
     def spread(left, array, rows):
-        near = own[(array + 2) * heads : (array + 2) * heads + 16, :]
+        near = own[16 * array : 16 * array + 16, :]
         high = rows.astype(BF16).astype(F32)
         left = jnp.concatenate([left, spot], axis=0).T.astype(BF16)
         parts = (near, far[16 * array : 16 * array + 16, :], high, rows - high)
@@ -491,16 +492,16 @@
     own, spot, weight = call(
         functools.partial(pack_kernel, heads),
         "pack_rows",
-        (pltpu.VMEM((48, dh), BF16), table, table),
-        [smem] + [hbm] * 4,
+        (pltpu.VMEM((32, dh), BF16), table, table),
+        [smem] + [hbm] * 2,
         (vmem,) * 3,
         [
-            pltpu.VMEM((4 * heads, 16, dh), BF16),
-            pltpu.VMEM((48, dh), F32),
-            pltpu.SemaphoreType.DMA((4 * heads,)),
+            pltpu.VMEM((2 * heads, 16, dh), BF16),
+            pltpu.VMEM((32, dh), F32),
+            pltpu.SemaphoreType.DMA((2 * heads,)),
         ],
         cost=large,
-    )(*far_memory(offsets, key, value, query, grad_out))
+    )(*far_memory(offsets, query, grad_out))
     key_later, value_later, own = lax.optimization_barrier((key, value, own))
     key_far = lax.ppermute(key_later, "ctx", mates)
     value_far = lax.ppermute(value_later, "ctx", mates)

time: 26.9 us -> 26.7 us (level)
  Pallas kernels: 14.4 us -> 14.1 us
    pallas_call x1, Pallas kernels: 2.24 us -> 1.83 us  [on_device(): call(functools.partial(pack_kernel, heads), 'pack_rows', (pltpu.VMEM((32,...]
    ppermute x1, waiting for transfers between devices: 0.01 us -> 0.35 us  [on_device(): grad_far = lax.ppermute(grad_out, 'ctx', mates)]
  transfers between devices with their start and end apart: 7 -> 7, of which waited for: 2 -> 3; matrix products, arithmetic and copies ran while one was open for 0% -> 0% of each run, Pallas kernels for 45% -> 44%
where the time goes in v5:
time: 26.7 us; the launch traced here: 26.5 us
  Pallas kernels  14.1 us (53%)
  starting transfers between devices  9.33 us (35%)
  waiting for transfers between devices  2.19 us (8%)
  between operations  0.79 us (3%)
    pallas_call x1, Pallas kernels, on_device(): call(functools.partial(main_kernel, heads), 'near_levels', (pltpu.HBM((le...  7.54 us
    all_to_all x1, starting transfers between devices, on_device(): lax.all_to_all(load, 'ctx', 0, 0, axis_index_groups=groups, tiled=True)  7.22 us
    pallas_call x1, Pallas kernels, on_device(): call(functools.partial(final_kernel, heads), 'join', (pltpu.HBM((length,...  2.42 us
    pallas_call x1, Pallas kernels, on_device(): call(functools.partial(pack_kernel, heads), 'pack_rows', (pltpu.VMEM((32,...  1.83 us
    pallas_call x1, Pallas kernels, on_device(): call(functools.partial(stats_kernel, heads, span), 'row_stats', (pltpu.HB...  1.71 us
    all_to_all x1, waiting for transfers between devices, on_device(): lax.all_to_all(load, 'ctx', 0, 0, axis_index_groups=groups, tiled=True)  0.99 us
    ppermute x1, waiting for transfers between devices, on_device(): got = lax.ppermute(theirs, 'ctx', mates)  0.84 us
    pallas_call x1, Pallas kernels, on_device(): call(functools.partial(wide_kernel, heads, span), 'third_level', (rows, r...  0.63 us
  transfers between devices with their start and end apart: 7, of which 3 were waited for; matrix products, arithmetic and copies ran while one was open for 0% of the time, Pallas kernels for 44%

profile of v5, /device:TPU:0, one launch (start us, length us, event | category | flops | bytes accessed | tf_op | source)
XLA Modules:
  0.0 26.5 jit_solution(2681319235919132566)
XLA Ops:
  0.6 0.0 copy-start.3
  0.6 0.0 copy-start.2
  0.7 0.5 %collective-permute-start = (bf16[256,1280]{1,0:T(8,128)(2,1)}, bf16[256,1280]{1,0:T(8,128)(2,1)S(1)}, u32[]{:S(2)}, u32[]{:S(2)}) collective-permute-start(bf16[256,1280]{1,0:T(8,128)(2,1)} %q_ref.3), channel_id=1, source_target_pairs={{0,1},{1,0},{2,3},{3,2},{4,5},{5,4},{6,7},{7,6},{8,9},{9,8},{10,11... | collective-permute-start | bytes 1966088 | tf_op jit(solution)/shard_map/ppermute | solution.py:489
  1.2 0.1 collective-permute-start.1
  1.2 1.8 %pack_rows.1 = (bf16[32,128]{1,0:T(8,128)(2,1)S(1)}, f32[32,256]{1,0:T(8,128)S(1)}, f32[32,256]{1,0:T(8,128)S(1)}) custom-call(s32[2,10]{1,0:T(2,128)} %off_hbm.3, bf16[256,1280]{1,0:T(8,128)(2,1)} %q_ref.3, bf16[256,1280]{1,0:T(8,128)(2,1)} %g_ref.3), custom_call_target="tpu_custom_call" | custom-call | flops 7000000000 | bytes 1000 | tf_op jit(solution)/shard_map/pack_rows/pallas_call | solution.py:492
  3.1 0.0 copy-done.3
  3.1 0.5 %collective-permute-start.3 = (bf16[256,1280]{1,0:T(8,128)(2,1)S(1)}, bf16[256,1280]{1,0:T(8,128)(2,1)}, u32[]{:S(2)}, u32[]{:S(2)}) collective-permute-start(bf16[256,1280]{1,0:T(8,128)(2,1)S(1)} %copy-done.3), channel_id=1, source_target_pairs={{0,1},{1,0},{2,3},{3,2},{4,5},{5,4},{6,7},{7,6},{8,9},{9,8},{10,11... | collective-permute-start | bytes 1966088 | tf_op jit(solution)/shard_map/ppermute | solution.py:507
  3.6 0.0 copy-done.2
  3.6 0.1 collective-permute-start.4
  3.7 0.0 collective-permute-done.qf_ref
  3.7 0.4 %collective-permute-done.1.gf_ref = bf16[256,1280]{1,0:T(8,128)(2,1)S(1)} collective-permute-done((bf16[256,1280]{1,0:T(8,128)(2,1)}, bf16[256,1280]{1,0:T(8,128)(2,1)S(1)}, u32[]{:S(2)}, u32[]{:S(2)}) %collective-permute-start.1) | collective-permute-done | bytes 655392 | tf_op jit(solution)/shard_map/ppermute | solution.py:490
  4.0 1.7 %row_stats.1 = (bf16[768,128]{1,0:T(8,128)(2,1)}, f32[32,256]{1,0:T(8,128)}, f32[32,256]{1,0:T(8,128)}, bf16[32,128]{1,0:T(8,128)(2,1)}) custom-call(bf16[32,128]{1,0:T(8,128)(2,1)S(1)} %get-tuple-element.22.own_ref, f32[32,256]{1,0:T(8,128)S(1)} %get-tuple-element.23.spot_ref, f32[32,256]{1,0:T(8,128)S(1)} %get-tuple-element.24.weight_ref, ...), custom_call_target="tpu_custom_call" | custom-call | flops 1000 | bytes 1000 | tf_op jit(solution)/shard_map/row_stats/pallas_call | solution.py:509
  5.8 7.2 %all-to-all-start = ((bf16[32,24,128]{2,1,0:T(8,128)(2,1)}), bf16[32,24,128]{2,1,0:T(8,128)(2,1)S(1)}, u32[]{:S(2)}, u32[]{:S(2)}) async-start(bf16[32,24,128]{2,1,0:T(8,128)(2,1)} %bitcast.3), calls=%async_computation | async-start | bytes 393216 | tf_op jit(solution)/shard_map/all_to_all | solution.py:533
  13.0 0.0 collective-permute-done.3.vf_hbm
  13.0 0.0 collective-permute-done.4.kf_ref
  13.0 7.5 %near_levels.1 = (bf16[256,1280]{1,0:T(8,128)(2,1)}, f32[256,1280]{1,0:T(8,128)}, f32[256,1280]{1,0:T(8,128)}, bf16[256,1280]{1,0:T(8,128)(2,1)}, f32[80,128]{1,0:T(8,128)}, /*index=5*/bf16[10,16,128]{2,1,0:T(8,128)(2,1)}) custom-call(s32[2,10]{1,0:T(2,128)} %off_hbm.3, f32[32,256]{1,0:T(8,128)} %get-tuple-element.29.s_hbm.s_ref, ...), custom_call_target="tpu_custom_call" | custom-call | flops 7000000000 | bytes 1000 | tf_op jit(solution)/shard_map/near_levels/pallas_call | solution.py:537
  20.6 0.3 %collective-permute-start.5 = (bf16[256,1280]{1,0:T(8,128)(2,1)}, bf16[256,1280]{1,0:T(8,128)(2,1)S(1)}, u32[]{:S(2)}, u32[]{:S(2)}) collective-permute-start(bf16[256,1280]{1,0:T(8,128)(2,1)} %get-tuple-element.37), channel_id=1, source_target_pairs={{0,1},{1,0},{2,3},{3,2},{4,5},{5,4},{6,7},{7,6},{8,9},{9,8},{10,11... | collective-permute-start | bytes 1966088 | tf_op jit(solution)/shard_map/ppermute | solution.py:573
  20.9 1.0 %all-to-all-done = bf16[32,24,128]{2,1,0:T(8,128)(2,1)S(1)} async-done(((bf16[32,24,128]{2,1,0:T(8,128)(2,1)}), bf16[32,24,128]{2,1,0:T(8,128)(2,1)S(1)}, u32[]{:S(2)}, u32[]{:S(2)}) %all-to-all-start) | async-done | bytes 196640 | tf_op jit(solution)/shard_map/all_to_all | solution.py:533
  21.9 0.6 %third_level.1 = (f32[32,128]{1,0:T(8,128)S(1)}, f32[32,128]{1,0:T(8,128)S(1)}) custom-call(bf16[768,128]{1,0:T(8,128)(2,1)S(1)} %bitcast.2), custom_call_target="tpu_custom_call" | custom-call | flops 7000000000 | bytes 1000 | tf_op jit(solution)/shard_map/third_level/pallas_call | solution.py:574
  22.6 0.6 %collective-permute-start.2 = (f32[32,128]{1,0:T(8,128)S(1)}, f32[32,128]{1,0:T(8,128)S(1)}, u32[]{:S(2)}, u32[]{:S(2)}) collective-permute-start(f32[32,128]{1,0:T(8,128)S(1)} %get-tuple-element.27), channel_id=1, source_target_pairs={{0,1},{1,0},{2,3},{3,2},{4,5},{5,4},{6,7},{7,6},{8,9},{9,8},{10,11... | collective-permute-start | bytes 49160 | tf_op jit(solution)/shard_map/ppermute | solution.py:583
  23.2 0.8 %collective-permute-done.2.got_ref = f32[32,128]{1,0:T(8,128)S(1)} collective-permute-done((f32[32,128]{1,0:T(8,128)S(1)}, f32[32,128]{1,0:T(8,128)S(1)}, u32[]{:S(2)}, u32[]{:S(2)}) %collective-permute-start.2) | collective-permute-done | bytes 16416 | tf_op jit(solution)/shard_map/ppermute | solution.py:583
  24.0 0.0 collective-permute-done.5.ret
  24.0 0.0 copy-done.4
  24.1 2.4 %join.1 = (bf16[256,1280]{1,0:T(8,128)(2,1)}, bf16[256,1280]{1,0:T(8,128)(2,1)}, bf16[256,1280]{1,0:T(8,128)(2,1)}) custom-call(s32[2,10]{1,0:T(2,128)} %off_hbm.3, f32[32,128]{1,0:T(8,128)S(1)} %get-tuple-element.26.mine_ref, f32[32,128]{1,0:T(8,128)S(1)} %collective-permute-done.2.got_ref, ...), custom_call_target="tpu_custom_call", output_to_operand_aliasing={{0}: (14, {})} | custom-call | flops 1000 | bytes 1000 | tf_op jit(solution)/shard_map/join/pallas_call | solution.py:584
  (17 shorter events, 0.0 us)
Async XLA Ops:
  0.6 2.5 %copy-start.3 = (bf16[256,1280]{1,0:T(8,128)(2,1)S(1)}, bf16[256,1280]{1,0:T(8,128)(2,1)}, u32[]{:S(2)}) copy-start(bf16[256,1280]{1,0:T(8,128)(2,1)} %v_ref.3) | copy-start | bytes 1966084
  0.6 3.0 %copy-start.2 = (bf16[256,1280]{1,0:T(8,128)(2,1)S(1)}, bf16[256,1280]{1,0:T(8,128)(2,1)}, u32[]{:S(2)}) copy-start(bf16[256,1280]{1,0:T(8,128)(2,1)} %k_ref.3) | copy-start | bytes 1966084
  0.7 3.0 %collective-permute-start = (bf16[256,1280]{1,0:T(8,128)(2,1)}, bf16[256,1280]{1,0:T(8,128)(2,1)S(1)}, u32[]{:S(2)}, u32[]{:S(2)}) collective-permute-start(bf16[256,1280]{1,0:T(8,128)(2,1)} %q_ref.3), channel_id=1, source_target_pairs={{0,1},{1,0},{2,3},{3,2},{4,5},{5,4},{6,7},{7,6},{8,9},{9,8},{10,11... | collective-permute-start | bytes 1966088 | tf_op jit(solution)/shard_map/ppermute | solution.py:489
  1.2 2.9 %collective-permute-start.1 = (bf16[256,1280]{1,0:T(8,128)(2,1)}, bf16[256,1280]{1,0:T(8,128)(2,1)S(1)}, u32[]{:S(2)}, u32[]{:S(2)}) collective-permute-start(bf16[256,1280]{1,0:T(8,128)(2,1)} %g_ref.3), channel_id=1, source_target_pairs={{0,1},{1,0},{2,3},{3,2},{4,5},{5,4},{6,7},{7,6},{8,9},{9,8},{10,11... | collective-permute-start | bytes 1966088 | tf_op jit(solution)/shard_map/ppermute | solution.py:490
  3.1 9.9 %collective-permute-start.3 = (bf16[256,1280]{1,0:T(8,128)(2,1)S(1)}, bf16[256,1280]{1,0:T(8,128)(2,1)}, u32[]{:S(2)}, u32[]{:S(2)}) collective-permute-start(bf16[256,1280]{1,0:T(8,128)(2,1)S(1)} %copy-done.3), channel_id=1, source_target_pairs={{0,1},{1,0},{2,3},{3,2},{4,5},{5,4},{6,7},{7,6},{8,9},{9,8},{10,11... | collective-permute-start | bytes 1966088 | tf_op jit(solution)/shard_map/ppermute | solution.py:507
  3.6 9.4 %collective-permute-start.4 = (bf16[256,1280]{1,0:T(8,128)(2,1)S(1)}, bf16[256,1280]{1,0:T(8,128)(2,1)S(1)}, u32[]{:S(2)}, u32[]{:S(2)}) collective-permute-start(bf16[256,1280]{1,0:T(8,128)(2,1)S(1)} %copy-done.2), channel_id=1, source_target_pairs={{0,1},{1,0},{2,3},{3,2},{4,5},{5,4},{6,7},{7,6},{8,9},{9,8},{10,11... | collective-permute-start | bytes 1966088 | tf_op jit(solution)/shard_map/ppermute | solution.py:506
  4.0 9.0 %copy-start.9 = (bf16[256,1280]{1,0:T(8,128)(2,1)S(1)}, bf16[256,1280]{1,0:T(8,128)(2,1)}, u32[]{:S(2)}) copy-start(bf16[256,1280]{1,0:T(8,128)(2,1)} %q_ref.3) | copy-start | bytes 1966084
  4.0 9.0 %copy-start.10 = (bf16[256,1280]{1,0:T(8,128)(2,1)S(1)}, bf16[256,1280]{1,0:T(8,128)(2,1)}, u32[]{:S(2)}) copy-start(bf16[256,1280]{1,0:T(8,128)(2,1)} %g_ref.3) | copy-start | bytes 1966084
  5.8 16.1 %all-to-all-start = ((bf16[32,24,128]{2,1,0:T(8,128)(2,1)}), bf16[32,24,128]{2,1,0:T(8,128)(2,1)S(1)}, u32[]{:S(2)}, u32[]{:S(2)}) async-start(bf16[32,24,128]{2,1,0:T(8,128)(2,1)} %bitcast.3), calls=%async_computation | async-start | bytes 393216 | tf_op jit(solution)/shard_map/all_to_all | solution.py:533
  20.6 3.4 %collective-permute-start.5 = (bf16[256,1280]{1,0:T(8,128)(2,1)}, bf16[256,1280]{1,0:T(8,128)(2,1)S(1)}, u32[]{:S(2)}, u32[]{:S(2)}) collective-permute-start(bf16[256,1280]{1,0:T(8,128)(2,1)} %get-tuple-element.37), channel_id=1, source_target_pairs={{0,1},{1,0},{2,3},{3,2},{4,5},{5,4},{6,7},{7,6},{8,9},{9,8},{10,11... | collective-permute-start | bytes 1966088 | tf_op jit(solution)/shard_map/ppermute | solution.py:573
  21.9 2.1 %copy-start = (f32[256,1280]{1,0:T(8,128)S(1)}, f32[256,1280]{1,0:T(8,128)}, u32[]{:S(2)}) copy-start(f32[256,1280]{1,0:T(8,128)} %get-tuple-element.34.dki) | copy-start | bytes 3932164
  21.9 2.1 %copy-start.1 = (f32[256,1280]{1,0:T(8,128)S(1)}, f32[256,1280]{1,0:T(8,128)}, u32[]{:S(2)}) copy-start(f32[256,1280]{1,0:T(8,128)} %get-tuple-element.35.dvi) | copy-start | bytes 3932164
  21.9 2.1 %copy-start.4 = (f32[80,128]{1,0:T(8,128)S(1)}, f32[80,128]{1,0:T(8,128)}, u32[]{:S(2)}) copy-start(f32[80,128]{1,0:T(8,128)} %get-tuple-element.33.terms_ref) | copy-start | bytes 122884
  21.9 2.1 %copy-start.5 = (bf16[10,16,128]{2,1,0:T(8,128)(2,1)S(1)}, bf16[10,16,128]{2,1,0:T(8,128)(2,1)}, u32[]{:S(2)}) copy-start(bf16[10,16,128]{2,1,0:T(8,128)(2,1)} %get-tuple-element.36.blocks_in) | copy-start | bytes 122884
  21.9 2.1 %copy-start.6 = (f32[32,256]{1,0:T(8,128)S(1)}, f32[32,256]{1,0:T(8,128)}, u32[]{:S(2)}) copy-start(f32[32,256]{1,0:T(8,128)} %get-tuple-element.29.s_hbm.s_ref) | copy-start | bytes 98308
  21.9 2.1 %copy-start.7 = (f32[32,256]{1,0:T(8,128)S(1)}, f32[32,256]{1,0:T(8,128)}, u32[]{:S(2)}) copy-start(f32[32,256]{1,0:T(8,128)} %get-tuple-element.30.dp_hbm.dp_ref) | copy-start | bytes 98308
  21.9 2.1 %copy-start.8 = (bf16[32,128]{1,0:T(8,128)(2,1)S(1)}, bf16[32,128]{1,0:T(8,128)(2,1)}, u32[]{:S(2)}) copy-start(bf16[32,128]{1,0:T(8,128)(2,1)} %get-tuple-element.28.far_ref) | copy-start | bytes 24580
  22.6 1.5 %collective-permute-start.2 = (f32[32,128]{1,0:T(8,128)S(1)}, f32[32,128]{1,0:T(8,128)S(1)}, u32[]{:S(2)}, u32[]{:S(2)}) collective-permute-start(f32[32,128]{1,0:T(8,128)S(1)} %get-tuple-element.27), channel_id=1, source_target_pairs={{0,1},{1,0},{2,3},{3,2},{4,5},{5,4},{6,7},{7,6},{8,9},{9,8},{10,11... | collective-permute-start | bytes 49160 | tf_op jit(solution)/shard_map/ppermute | solution.py:583

commit v6 on v5

--- a/solution.py
+++ b/solution.py
@@ -106,16 +106,22 @@
     spot = spot_ref[0:16, :].astype(BF16)
 
     def both_rows(whole, first):
-        far = own_columns(dot_nn(spot, whole), heads)
-        far_ref[first : first + 16, :] = far.astype(BF16)
-        near = own[first : first + 16, :]
-        return jnp.concatenate([block_rows(near, heads), block_rows(far, heads)], axis=0)
+        picked = dot_nn(spot, whole)
+        far_ref[first : first + 16, :] = own_columns(picked, heads).astype(BF16)
+        diagonal = iota(picked.shape, 1) // dh == iota(picked.shape, 0)
+        far = jnp.where(diagonal, picked, 0.0).astype(BF16)
+        return jnp.concatenate([block_rows(own[first : first + 16, :], heads), far], axis=0)
 
     queries, grads = both_rows(qf_ref[...], 0), both_rows(gf_ref[...], 16)
     s = dot_nt(queries, k_ref[...]) * (dh**-0.5 * LOG2E)
     dp = dot_nt(grads, v_ref[...])
     s_ref[...] = s
     dp_ref[...] = dp
+    early = []
+    for i, (near, away) in enumerate(((s_ref, s_hbm), (dp_ref, dp_hbm), (far_ref, far_hbm))):
+        copy = pltpu.make_async_copy(near, away, row_sems.at[i])
+        copy.start()
+        early.append(copy)
     rows = [own_columns(dot_nn(spot, ref[...]), heads) for ref in (k_ref, v_ref)]
     rows += [own[0:16, :], own[16:32, :]]
     for i in range(4):
@@ -146,11 +152,9 @@
         pltpu.make_async_copy(load, load_ref.at[pl.ds(i * stride, stride), :], sems.at[i])
         for i in range(span * slots // stride)
     ]
-    for i, (near, away) in enumerate(((s_ref, s_hbm), (dp_ref, dp_hbm), (far_ref, far_hbm))):
-        copies.append(pltpu.make_async_copy(near, away, row_sems.at[i]))
     for copy in copies:
         copy.start()
-    for copy in copies:
+    for copy in copies + early:
         copy.wait()
 
 
@@ -505,7 +509,7 @@
     key_later, value_later, own = lax.optimization_barrier((key, value, own))
     key_far = lax.ppermute(key_later, "ctx", mates)
     value_far = lax.ppermute(value_later, "ctx", mates)
-    repeat = min(span, 8)
+    repeat = min(span, 32)
     load, s_rows, dp_rows, far = call(
         functools.partial(stats_kernel, heads, span),
         "row_stats",

time: 26.7 us -> 26.7 us (level)
  no operation moved by 1% of the time
where the time goes in v6:
time: 26.7 us; the launch traced here: 26.5 us
  Pallas kernels  14.1 us (53%)
  starting transfers between devices  9.33 us (35%)
  waiting for transfers between devices  2.19 us (8%)
  between operations  0.79 us (3%)
    pallas_call x1, Pallas kernels, on_device(): call(functools.partial(main_kernel, heads), 'near_levels', (pltpu.HBM((le...  7.54 us
    all_to_all x1, starting transfers between devices, on_device(): lax.all_to_all(load, 'ctx', 0, 0, axis_index_groups=groups, tiled=True)  7.22 us
    pallas_call x1, Pallas kernels, on_device(): call(functools.partial(final_kernel, heads), 'join', (pltpu.HBM((length,...  2.42 us
    pallas_call x1, Pallas kernels, on_device(): call(functools.partial(pack_kernel, heads), 'pack_rows', (pltpu.VMEM((32,...  1.83 us
    pallas_call x1, Pallas kernels, on_device(): call(functools.partial(stats_kernel, heads, span), 'row_stats', (pltpu.HB...  1.72 us
    all_to_all x1, waiting for transfers between devices, on_device(): lax.all_to_all(load, 'ctx', 0, 0, axis_index_groups=groups, tiled=True)  0.99 us
    ppermute x1, waiting for transfers between devices, on_device(): got = lax.ppermute(theirs, 'ctx', mates)  0.84 us
    pallas_call x1, Pallas kernels, on_device(): call(functools.partial(wide_kernel, heads, span), 'third_level', (rows, r...  0.63 us
  transfers between devices with their start and end apart: 7, of which 3 were waited for; matrix products, arithmetic and copies ran while one was open for 0% of the time, Pallas kernels for 44%

profile of v6, /device:TPU:0, one launch (start us, length us, event | category | flops | bytes accessed | tf_op | source)
XLA Modules:
  0.0 26.5 jit_solution(16804479998425096843)
XLA Ops:
  0.6 0.0 copy-start.3
  0.6 0.0 copy-start.2
  0.7 0.5 %collective-permute-start = (bf16[256,1280]{1,0:T(8,128)(2,1)}, bf16[256,1280]{1,0:T(8,128)(2,1)S(1)}, u32[]{:S(2)}, u32[]{:S(2)}) collective-permute-start(bf16[256,1280]{1,0:T(8,128)(2,1)} %q_ref.3), channel_id=1, source_target_pairs={{0,1},{1,0},{2,3},{3,2},{4,5},{5,4},{6,7},{7,6},{8,9},{9,8},{10,11... | collective-permute-start | bytes 1966088 | tf_op jit(solution)/shard_map/ppermute | solution.py:493
  1.2 0.1 collective-permute-start.1
  1.2 1.8 %pack_rows.1 = (bf16[32,128]{1,0:T(8,128)(2,1)S(1)}, f32[32,256]{1,0:T(8,128)S(1)}, f32[32,256]{1,0:T(8,128)S(1)}) custom-call(s32[2,10]{1,0:T(2,128)} %off_hbm.3, bf16[256,1280]{1,0:T(8,128)(2,1)} %q_ref.3, bf16[256,1280]{1,0:T(8,128)(2,1)} %g_ref.3), custom_call_target="tpu_custom_call" | custom-call | flops 7000000000 | bytes 1000 | tf_op jit(solution)/shard_map/pack_rows/pallas_call | solution.py:496
  3.1 0.5 %collective-permute-start.3 = (bf16[256,1280]{1,0:T(8,128)(2,1)S(1)}, bf16[256,1280]{1,0:T(8,128)(2,1)}, u32[]{:S(2)}, u32[]{:S(2)}) collective-permute-start(bf16[256,1280]{1,0:T(8,128)(2,1)S(1)} %copy-done.3), channel_id=1, source_target_pairs={{0,1},{1,0},{2,3},{3,2},{4,5},{5,4},{6,7},{7,6},{8,9},{9,8},{10,11... | collective-permute-start | bytes 1966088 | tf_op jit(solution)/shard_map/ppermute | solution.py:511
  3.6 0.1 collective-permute-start.4
  3.7 0.0 collective-permute-done.qf_ref
  3.7 0.4 %collective-permute-done.1.gf_ref = bf16[256,1280]{1,0:T(8,128)(2,1)S(1)} collective-permute-done((bf16[256,1280]{1,0:T(8,128)(2,1)}, bf16[256,1280]{1,0:T(8,128)(2,1)S(1)}, u32[]{:S(2)}, u32[]{:S(2)}) %collective-permute-start.1) | collective-permute-done | bytes 655392 | tf_op jit(solution)/shard_map/ppermute | solution.py:494
  4.0 1.7 %row_stats.1 = (bf16[768,128]{1,0:T(8,128)(2,1)}, f32[32,256]{1,0:T(8,128)}, f32[32,256]{1,0:T(8,128)}, bf16[32,128]{1,0:T(8,128)(2,1)}) custom-call(bf16[32,128]{1,0:T(8,128)(2,1)S(1)} %get-tuple-element.22.own_ref, f32[32,256]{1,0:T(8,128)S(1)} %get-tuple-element.23.spot_ref, f32[32,256]{1,0:T(8,128)S(1)} %get-tuple-element.24.weight_ref, ...), custom_call_target="tpu_custom_call" | custom-call | flops 1000 | bytes 1000 | tf_op jit(solution)/shard_map/row_stats/pallas_call | solution.py:513
  5.8 7.2 %all-to-all-start = ((bf16[32,24,128]{2,1,0:T(8,128)(2,1)}), bf16[32,24,128]{2,1,0:T(8,128)(2,1)S(1)}, u32[]{:S(2)}, u32[]{:S(2)}) async-start(bf16[32,24,128]{2,1,0:T(8,128)(2,1)} %bitcast.3), calls=%async_computation | async-start | bytes 393216 | tf_op jit(solution)/shard_map/all_to_all | solution.py:537
  13.0 0.0 collective-permute-done.3.vf_hbm
  13.0 0.0 collective-permute-done.4.kf_ref
  13.0 0.0 copy-done.9
  13.0 0.0 copy-done.10
  13.0 7.5 %near_levels.1 = (bf16[256,1280]{1,0:T(8,128)(2,1)}, f32[256,1280]{1,0:T(8,128)}, f32[256,1280]{1,0:T(8,128)}, bf16[256,1280]{1,0:T(8,128)(2,1)}, f32[80,128]{1,0:T(8,128)}, /*index=5*/bf16[10,16,128]{2,1,0:T(8,128)(2,1)}) custom-call(s32[2,10]{1,0:T(2,128)} %off_hbm.3, f32[32,256]{1,0:T(8,128)} %get-tuple-element.29.s_hbm.s_ref, ...), custom_call_target="tpu_custom_call" | custom-call | flops 7000000000 | bytes 1000 | tf_op jit(solution)/shard_map/near_levels/pallas_call | solution.py:541
  20.6 0.3 %collective-permute-start.5 = (bf16[256,1280]{1,0:T(8,128)(2,1)}, bf16[256,1280]{1,0:T(8,128)(2,1)S(1)}, u32[]{:S(2)}, u32[]{:S(2)}) collective-permute-start(bf16[256,1280]{1,0:T(8,128)(2,1)} %get-tuple-element.37), channel_id=1, source_target_pairs={{0,1},{1,0},{2,3},{3,2},{4,5},{5,4},{6,7},{7,6},{8,9},{9,8},{10,11... | collective-permute-start | bytes 1966088 | tf_op jit(solution)/shard_map/ppermute | solution.py:577
  20.9 1.0 %all-to-all-done = bf16[32,24,128]{2,1,0:T(8,128)(2,1)S(1)} async-done(((bf16[32,24,128]{2,1,0:T(8,128)(2,1)}), bf16[32,24,128]{2,1,0:T(8,128)(2,1)S(1)}, u32[]{:S(2)}, u32[]{:S(2)}) %all-to-all-start) | async-done | bytes 196640 | tf_op jit(solution)/shard_map/all_to_all | solution.py:537
  21.9 0.6 %third_level.1 = (f32[32,128]{1,0:T(8,128)S(1)}, f32[32,128]{1,0:T(8,128)S(1)}) custom-call(bf16[768,128]{1,0:T(8,128)(2,1)S(1)} %bitcast.2), custom_call_target="tpu_custom_call" | custom-call | flops 7000000000 | bytes 1000 | tf_op jit(solution)/shard_map/third_level/pallas_call | solution.py:578
  22.6 0.6 %collective-permute-start.2 = (f32[32,128]{1,0:T(8,128)S(1)}, f32[32,128]{1,0:T(8,128)S(1)}, u32[]{:S(2)}, u32[]{:S(2)}) collective-permute-start(f32[32,128]{1,0:T(8,128)S(1)} %get-tuple-element.27), channel_id=1, source_target_pairs={{0,1},{1,0},{2,3},{3,2},{4,5},{5,4},{6,7},{7,6},{8,9},{9,8},{10,11... | collective-permute-start | bytes 49160 | tf_op jit(solution)/shard_map/ppermute | solution.py:587
  23.2 0.8 %collective-permute-done.2.got_ref = f32[32,128]{1,0:T(8,128)S(1)} collective-permute-done((f32[32,128]{1,0:T(8,128)S(1)}, f32[32,128]{1,0:T(8,128)S(1)}, u32[]{:S(2)}, u32[]{:S(2)}) %collective-permute-start.2) | collective-permute-done | bytes 16416 | tf_op jit(solution)/shard_map/ppermute | solution.py:587
  24.0 0.0 collective-permute-done.5.ret
  24.0 0.0 copy-done.1
  24.1 2.4 %join.1 = (bf16[256,1280]{1,0:T(8,128)(2,1)}, bf16[256,1280]{1,0:T(8,128)(2,1)}, bf16[256,1280]{1,0:T(8,128)(2,1)}) custom-call(s32[2,10]{1,0:T(2,128)} %off_hbm.3, f32[32,128]{1,0:T(8,128)S(1)} %get-tuple-element.26.mine_ref, f32[32,128]{1,0:T(8,128)S(1)} %collective-permute-done.2.got_ref, ...), custom_call_target="tpu_custom_call", output_to_operand_aliasing={{0}: (14, {})} | custom-call | flops 1000 | bytes 1000 | tf_op jit(solution)/shard_map/join/pallas_call | solution.py:588
  (17 shorter events, 0.0 us)
Async XLA Ops:
  0.6 2.5 %copy-start.3 = (bf16[256,1280]{1,0:T(8,128)(2,1)S(1)}, bf16[256,1280]{1,0:T(8,128)(2,1)}, u32[]{:S(2)}) copy-start(bf16[256,1280]{1,0:T(8,128)(2,1)} %v_ref.3) | copy-start | bytes 1966084
  0.6 3.0 %copy-start.2 = (bf16[256,1280]{1,0:T(8,128)(2,1)S(1)}, bf16[256,1280]{1,0:T(8,128)(2,1)}, u32[]{:S(2)}) copy-start(bf16[256,1280]{1,0:T(8,128)(2,1)} %k_ref.3) | copy-start | bytes 1966084
  0.7 3.0 %collective-permute-start = (bf16[256,1280]{1,0:T(8,128)(2,1)}, bf16[256,1280]{1,0:T(8,128)(2,1)S(1)}, u32[]{:S(2)}, u32[]{:S(2)}) collective-permute-start(bf16[256,1280]{1,0:T(8,128)(2,1)} %q_ref.3), channel_id=1, source_target_pairs={{0,1},{1,0},{2,3},{3,2},{4,5},{5,4},{6,7},{7,6},{8,9},{9,8},{10,11... | collective-permute-start | bytes 1966088 | tf_op jit(solution)/shard_map/ppermute | solution.py:493
  1.2 2.9 %collective-permute-start.1 = (bf16[256,1280]{1,0:T(8,128)(2,1)}, bf16[256,1280]{1,0:T(8,128)(2,1)S(1)}, u32[]{:S(2)}, u32[]{:S(2)}) collective-permute-start(bf16[256,1280]{1,0:T(8,128)(2,1)} %g_ref.3), channel_id=1, source_target_pairs={{0,1},{1,0},{2,3},{3,2},{4,5},{5,4},{6,7},{7,6},{8,9},{9,8},{10,11... | collective-permute-start | bytes 1966088 | tf_op jit(solution)/shard_map/ppermute | solution.py:494
  3.1 9.9 %collective-permute-start.3 = (bf16[256,1280]{1,0:T(8,128)(2,1)S(1)}, bf16[256,1280]{1,0:T(8,128)(2,1)}, u32[]{:S(2)}, u32[]{:S(2)}) collective-permute-start(bf16[256,1280]{1,0:T(8,128)(2,1)S(1)} %copy-done.3), channel_id=1, source_target_pairs={{0,1},{1,0},{2,3},{3,2},{4,5},{5,4},{6,7},{7,6},{8,9},{9,8},{10,11... | collective-permute-start | bytes 1966088 | tf_op jit(solution)/shard_map/ppermute | solution.py:511
  3.6 9.4 %collective-permute-start.4 = (bf16[256,1280]{1,0:T(8,128)(2,1)S(1)}, bf16[256,1280]{1,0:T(8,128)(2,1)S(1)}, u32[]{:S(2)}, u32[]{:S(2)}) collective-permute-start(bf16[256,1280]{1,0:T(8,128)(2,1)S(1)} %copy-done.2), channel_id=1, source_target_pairs={{0,1},{1,0},{2,3},{3,2},{4,5},{5,4},{6,7},{7,6},{8,9},{9,8},{10,11... | collective-permute-start | bytes 1966088 | tf_op jit(solution)/shard_map/ppermute | solution.py:510
  4.0 9.0 %copy-start.9 = (bf16[256,1280]{1,0:T(8,128)(2,1)S(1)}, bf16[256,1280]{1,0:T(8,128)(2,1)}, u32[]{:S(2)}) copy-start(bf16[256,1280]{1,0:T(8,128)(2,1)} %q_ref.3) | copy-start | bytes 1966084
  4.0 9.0 %copy-start.10 = (bf16[256,1280]{1,0:T(8,128)(2,1)S(1)}, bf16[256,1280]{1,0:T(8,128)(2,1)}, u32[]{:S(2)}) copy-start(bf16[256,1280]{1,0:T(8,128)(2,1)} %g_ref.3) | copy-start | bytes 1966084
  5.8 16.1 %all-to-all-start = ((bf16[32,24,128]{2,1,0:T(8,128)(2,1)}), bf16[32,24,128]{2,1,0:T(8,128)(2,1)S(1)}, u32[]{:S(2)}, u32[]{:S(2)}) async-start(bf16[32,24,128]{2,1,0:T(8,128)(2,1)} %bitcast.3), calls=%async_computation | async-start | bytes 393216 | tf_op jit(solution)/shard_map/all_to_all | solution.py:537
  20.6 3.4 %collective-permute-start.5 = (bf16[256,1280]{1,0:T(8,128)(2,1)}, bf16[256,1280]{1,0:T(8,128)(2,1)S(1)}, u32[]{:S(2)}, u32[]{:S(2)}) collective-permute-start(bf16[256,1280]{1,0:T(8,128)(2,1)} %get-tuple-element.37), channel_id=1, source_target_pairs={{0,1},{1,0},{2,3},{3,2},{4,5},{5,4},{6,7},{7,6},{8,9},{9,8},{10,11... | collective-permute-start | bytes 1966088 | tf_op jit(solution)/shard_map/ppermute | solution.py:577
  21.9 2.1 %copy-start = (f32[256,1280]{1,0:T(8,128)S(1)}, f32[256,1280]{1,0:T(8,128)}, u32[]{:S(2)}) copy-start(f32[256,1280]{1,0:T(8,128)} %get-tuple-element.34.dki) | copy-start | bytes 3932164
  21.9 2.1 %copy-start.1 = (f32[256,1280]{1,0:T(8,128)S(1)}, f32[256,1280]{1,0:T(8,128)}, u32[]{:S(2)}) copy-start(f32[256,1280]{1,0:T(8,128)} %get-tuple-element.35.dvi) | copy-start | bytes 3932164
  21.9 2.1 %copy-start.4 = (f32[80,128]{1,0:T(8,128)S(1)}, f32[80,128]{1,0:T(8,128)}, u32[]{:S(2)}) copy-start(f32[80,128]{1,0:T(8,128)} %get-tuple-element.33.terms_ref) | copy-start | bytes 122884
  21.9 2.1 %copy-start.5 = (bf16[10,16,128]{2,1,0:T(8,128)(2,1)S(1)}, bf16[10,16,128]{2,1,0:T(8,128)(2,1)}, u32[]{:S(2)}) copy-start(bf16[10,16,128]{2,1,0:T(8,128)(2,1)} %get-tuple-element.36.blocks_in) | copy-start | bytes 122884
  21.9 2.1 %copy-start.6 = (f32[32,256]{1,0:T(8,128)S(1)}, f32[32,256]{1,0:T(8,128)}, u32[]{:S(2)}) copy-start(f32[32,256]{1,0:T(8,128)} %get-tuple-element.29.s_hbm.s_ref) | copy-start | bytes 98308
  21.9 2.1 %copy-start.7 = (f32[32,256]{1,0:T(8,128)S(1)}, f32[32,256]{1,0:T(8,128)}, u32[]{:S(2)}) copy-start(f32[32,256]{1,0:T(8,128)} %get-tuple-element.30.dp_hbm.dp_ref) | copy-start | bytes 98308
  21.9 2.1 %copy-start.8 = (bf16[32,128]{1,0:T(8,128)(2,1)S(1)}, bf16[32,128]{1,0:T(8,128)(2,1)}, u32[]{:S(2)}) copy-start(bf16[32,128]{1,0:T(8,128)(2,1)} %get-tuple-element.28.far_ref) | copy-start | bytes 24580
  22.6 1.5 %collective-permute-start.2 = (f32[32,128]{1,0:T(8,128)S(1)}, f32[32,128]{1,0:T(8,128)S(1)}, u32[]{:S(2)}, u32[]{:S(2)}) collective-permute-start(f32[32,128]{1,0:T(8,128)S(1)} %get-tuple-element.27), channel_id=1, source_target_pairs={{0,1},{1,0},{2,3},{3,2},{4,5},{5,4},{6,7},{7,6},{8,9},{9,8},{10,11... | collective-permute-start | bytes 49160 | tf_op jit(solution)/shard_map/ppermute | solution.py:587

commit v7 on v6

--- a/solution.py
+++ b/solution.py
@@ -436,11 +436,13 @@
     ):
         back = slice(index * half, (index + 1) * half)
         for j, chunk in enumerate(chunks):
+            added = base[:, chunk] + dot_nn(left, right[:, chunk])
             for h in (2 * j, 2 * j + 1):
                 cols = slice(h * dh, (h + 1) * dh)
+                mine_part = slice((h - 2 * j) * dh, (h - 2 * j + 1) * dh)
                 pick = iota((length, half), 0) == 2 * iota((length, half), 1) + off_ref[0, h]
-                added = dot_nn(left, right[:, cols]) + dot_nn(pick.astype(BF16), ret[back, cols])
-                out[:, cols] = (base[:, cols] + added).astype(BF16)
+                back_part = dot_nn(pick.astype(BF16), ret[back, cols])
+                out[:, cols] = (added[:, mine_part] + back_part).astype(BF16)
             sem = write_sems.at[index, j]
             copy = pltpu.make_async_copy(out.at[:, chunk], out_ref.at[:, chunk], sem)
             copy.start()

time: 26.7 us -> 26.8 us (level)
  no operation moved by 1% of the time
where the time goes in v7:
time: 26.8 us; the launch traced here: 26.5 us
  Pallas kernels  14.2 us (53%)
  starting transfers between devices  9.33 us (35%)
  waiting for transfers between devices  2.19 us (8%)
  between operations  0.79 us (3%)
    pallas_call x1, Pallas kernels, on_device(): call(functools.partial(main_kernel, heads), 'near_levels', (pltpu.HBM((le...  7.54 us
    all_to_all x1, starting transfers between devices, on_device(): lax.all_to_all(load, 'ctx', 0, 0, axis_index_groups=groups, tiled=True)  7.22 us
    pallas_call x1, Pallas kernels, on_device(): call(functools.partial(final_kernel, heads), 'join', (pltpu.HBM((length,...  2.47 us
    pallas_call x1, Pallas kernels, on_device(): call(functools.partial(pack_kernel, heads), 'pack_rows', (pltpu.VMEM((32,...  1.83 us
    pallas_call x1, Pallas kernels, on_device(): call(functools.partial(stats_kernel, heads, span), 'row_stats', (pltpu.HB...  1.72 us
    all_to_all x1, waiting for transfers between devices, on_device(): lax.all_to_all(load, 'ctx', 0, 0, axis_index_groups=groups, tiled=True)  0.99 us
    ppermute x1, waiting for transfers between devices, on_device(): got = lax.ppermute(theirs, 'ctx', mates)  0.84 us
    pallas_call x1, Pallas kernels, on_device(): call(functools.partial(wide_kernel, heads, span), 'third_level', (rows, r...  0.63 us
  transfers between devices with their start and end apart: 7, of which 3 were waited for; matrix products, arithmetic and copies ran while one was open for 0% of the time, Pallas kernels for 44%

profile of v7, /device:TPU:0, one launch (start us, length us, event | category | flops | bytes accessed | tf_op | source)
XLA Modules:
  0.0 26.5 jit_solution(11617542860492872879)
XLA Ops:
  0.6 0.0 copy-start.3
  0.7 0.5 %collective-permute-start = (bf16[256,1280]{1,0:T(8,128)(2,1)}, bf16[256,1280]{1,0:T(8,128)(2,1)S(1)}, u32[]{:S(2)}, u32[]{:S(2)}) collective-permute-start(bf16[256,1280]{1,0:T(8,128)(2,1)} %q_ref.3), channel_id=1, source_target_pairs={{0,1},{1,0},{2,3},{3,2},{4,5},{5,4},{6,7},{7,6},{8,9},{9,8},{10,11... | collective-permute-start | bytes 1966088 | tf_op jit(solution)/shard_map/ppermute | solution.py:495
  1.2 0.1 collective-permute-start.1
  1.2 1.8 %pack_rows.1 = (bf16[32,128]{1,0:T(8,128)(2,1)S(1)}, f32[32,256]{1,0:T(8,128)S(1)}, f32[32,256]{1,0:T(8,128)S(1)}) custom-call(s32[2,10]{1,0:T(2,128)} %off_hbm.3, bf16[256,1280]{1,0:T(8,128)(2,1)} %q_ref.3, bf16[256,1280]{1,0:T(8,128)(2,1)} %g_ref.3), custom_call_target="tpu_custom_call" | custom-call | flops 7000000000 | bytes 1000 | tf_op jit(solution)/shard_map/pack_rows/pallas_call | solution.py:498
  3.1 0.5 %collective-permute-start.3 = (bf16[256,1280]{1,0:T(8,128)(2,1)S(1)}, bf16[256,1280]{1,0:T(8,128)(2,1)}, u32[]{:S(2)}, u32[]{:S(2)}) collective-permute-start(bf16[256,1280]{1,0:T(8,128)(2,1)S(1)} %copy-done.3), channel_id=1, source_target_pairs={{0,1},{1,0},{2,3},{3,2},{4,5},{5,4},{6,7},{7,6},{8,9},{9,8},{10,11... | collective-permute-start | bytes 1966088 | tf_op jit(solution)/shard_map/ppermute | solution.py:513
  3.6 0.1 collective-permute-start.4
  3.7 0.0 collective-permute-done.qf_ref
  3.7 0.4 %collective-permute-done.1.gf_ref = bf16[256,1280]{1,0:T(8,128)(2,1)S(1)} collective-permute-done((bf16[256,1280]{1,0:T(8,128)(2,1)}, bf16[256,1280]{1,0:T(8,128)(2,1)S(1)}, u32[]{:S(2)}, u32[]{:S(2)}) %collective-permute-start.1) | collective-permute-done | bytes 655392 | tf_op jit(solution)/shard_map/ppermute | solution.py:496
  4.0 1.7 %row_stats.1 = (bf16[768,128]{1,0:T(8,128)(2,1)}, f32[32,256]{1,0:T(8,128)}, f32[32,256]{1,0:T(8,128)}, bf16[32,128]{1,0:T(8,128)(2,1)}) custom-call(bf16[32,128]{1,0:T(8,128)(2,1)S(1)} %get-tuple-element.22.own_ref, f32[32,256]{1,0:T(8,128)S(1)} %get-tuple-element.23.spot_ref, f32[32,256]{1,0:T(8,128)S(1)} %get-tuple-element.24.weight_ref, ...), custom_call_target="tpu_custom_call" | custom-call | flops 1000 | bytes 1000 | tf_op jit(solution)/shard_map/row_stats/pallas_call | solution.py:515
  5.8 7.2 %all-to-all-start = ((bf16[32,24,128]{2,1,0:T(8,128)(2,1)}), bf16[32,24,128]{2,1,0:T(8,128)(2,1)S(1)}, u32[]{:S(2)}, u32[]{:S(2)}) async-start(bf16[32,24,128]{2,1,0:T(8,128)(2,1)} %bitcast.3), calls=%async_computation | async-start | bytes 393216 | tf_op jit(solution)/shard_map/all_to_all | solution.py:539
  13.0 0.0 collective-permute-done.3.vf_hbm
  13.0 0.0 collective-permute-done.4.kf_ref
  13.0 7.5 %near_levels.1 = (bf16[256,1280]{1,0:T(8,128)(2,1)}, f32[256,1280]{1,0:T(8,128)}, f32[256,1280]{1,0:T(8,128)}, bf16[256,1280]{1,0:T(8,128)(2,1)}, f32[80,128]{1,0:T(8,128)}, /*index=5*/bf16[10,16,128]{2,1,0:T(8,128)(2,1)}) custom-call(s32[2,10]{1,0:T(2,128)} %off_hbm.3, f32[32,256]{1,0:T(8,128)} %get-tuple-element.29.s_hbm.s_ref, ...), custom_call_target="tpu_custom_call" | custom-call | flops 7000000000 | bytes 1000 | tf_op jit(solution)/shard_map/near_levels/pallas_call | solution.py:543
  20.6 0.3 %collective-permute-start.5 = (bf16[256,1280]{1,0:T(8,128)(2,1)}, bf16[256,1280]{1,0:T(8,128)(2,1)S(1)}, u32[]{:S(2)}, u32[]{:S(2)}) collective-permute-start(bf16[256,1280]{1,0:T(8,128)(2,1)} %get-tuple-element.37), channel_id=1, source_target_pairs={{0,1},{1,0},{2,3},{3,2},{4,5},{5,4},{6,7},{7,6},{8,9},{9,8},{10,11... | collective-permute-start | bytes 1966088 | tf_op jit(solution)/shard_map/ppermute | solution.py:579
  20.9 1.0 %all-to-all-done = bf16[32,24,128]{2,1,0:T(8,128)(2,1)S(1)} async-done(((bf16[32,24,128]{2,1,0:T(8,128)(2,1)}), bf16[32,24,128]{2,1,0:T(8,128)(2,1)S(1)}, u32[]{:S(2)}, u32[]{:S(2)}) %all-to-all-start) | async-done | bytes 196640 | tf_op jit(solution)/shard_map/all_to_all | solution.py:539
  21.9 0.0 copy-start.6
  21.9 0.0 copy-start.7
  21.9 0.0 copy-start.8
  21.9 0.6 %third_level.1 = (f32[32,128]{1,0:T(8,128)S(1)}, f32[32,128]{1,0:T(8,128)S(1)}) custom-call(bf16[768,128]{1,0:T(8,128)(2,1)S(1)} %bitcast.2), custom_call_target="tpu_custom_call" | custom-call | flops 7000000000 | bytes 1000 | tf_op jit(solution)/shard_map/third_level/pallas_call | solution.py:580
  22.6 0.6 %collective-permute-start.2 = (f32[32,128]{1,0:T(8,128)S(1)}, f32[32,128]{1,0:T(8,128)S(1)}, u32[]{:S(2)}, u32[]{:S(2)}) collective-permute-start(f32[32,128]{1,0:T(8,128)S(1)} %get-tuple-element.27), channel_id=1, source_target_pairs={{0,1},{1,0},{2,3},{3,2},{4,5},{5,4},{6,7},{7,6},{8,9},{9,8},{10,11... | collective-permute-start | bytes 49160 | tf_op jit(solution)/shard_map/ppermute | solution.py:589
  23.2 0.8 %collective-permute-done.2.got_ref = f32[32,128]{1,0:T(8,128)S(1)} collective-permute-done((f32[32,128]{1,0:T(8,128)S(1)}, f32[32,128]{1,0:T(8,128)S(1)}, u32[]{:S(2)}, u32[]{:S(2)}) %collective-permute-start.2) | collective-permute-done | bytes 16416 | tf_op jit(solution)/shard_map/ppermute | solution.py:589
  24.0 0.0 collective-permute-done.5.ret
  24.0 0.0 copy-done
  24.1 2.5 %join.1 = (bf16[256,1280]{1,0:T(8,128)(2,1)}, bf16[256,1280]{1,0:T(8,128)(2,1)}, bf16[256,1280]{1,0:T(8,128)(2,1)}) custom-call(s32[2,10]{1,0:T(2,128)} %off_hbm.3, f32[32,128]{1,0:T(8,128)S(1)} %get-tuple-element.26.mine_ref, f32[32,128]{1,0:T(8,128)S(1)} %collective-permute-done.2.got_ref, ...), custom_call_target="tpu_custom_call", output_to_operand_aliasing={{0}: (14, {})} | custom-call | flops 1000 | bytes 1000 | tf_op jit(solution)/shard_map/join/pallas_call | solution.py:590
  (17 shorter events, 0.0 us)
Async XLA Ops:
  0.6 2.5 %copy-start.3 = (bf16[256,1280]{1,0:T(8,128)(2,1)S(1)}, bf16[256,1280]{1,0:T(8,128)(2,1)}, u32[]{:S(2)}) copy-start(bf16[256,1280]{1,0:T(8,128)(2,1)} %v_ref.3) | copy-start | bytes 1966084
  0.6 3.0 %copy-start.2 = (bf16[256,1280]{1,0:T(8,128)(2,1)S(1)}, bf16[256,1280]{1,0:T(8,128)(2,1)}, u32[]{:S(2)}) copy-start(bf16[256,1280]{1,0:T(8,128)(2,1)} %k_ref.3) | copy-start | bytes 1966084
  0.7 3.0 %collective-permute-start = (bf16[256,1280]{1,0:T(8,128)(2,1)}, bf16[256,1280]{1,0:T(8,128)(2,1)S(1)}, u32[]{:S(2)}, u32[]{:S(2)}) collective-permute-start(bf16[256,1280]{1,0:T(8,128)(2,1)} %q_ref.3), channel_id=1, source_target_pairs={{0,1},{1,0},{2,3},{3,2},{4,5},{5,4},{6,7},{7,6},{8,9},{9,8},{10,11... | collective-permute-start | bytes 1966088 | tf_op jit(solution)/shard_map/ppermute | solution.py:495
  1.2 2.9 %collective-permute-start.1 = (bf16[256,1280]{1,0:T(8,128)(2,1)}, bf16[256,1280]{1,0:T(8,128)(2,1)S(1)}, u32[]{:S(2)}, u32[]{:S(2)}) collective-permute-start(bf16[256,1280]{1,0:T(8,128)(2,1)} %g_ref.3), channel_id=1, source_target_pairs={{0,1},{1,0},{2,3},{3,2},{4,5},{5,4},{6,7},{7,6},{8,9},{9,8},{10,11... | collective-permute-start | bytes 1966088 | tf_op jit(solution)/shard_map/ppermute | solution.py:496
  3.1 9.9 %collective-permute-start.3 = (bf16[256,1280]{1,0:T(8,128)(2,1)S(1)}, bf16[256,1280]{1,0:T(8,128)(2,1)}, u32[]{:S(2)}, u32[]{:S(2)}) collective-permute-start(bf16[256,1280]{1,0:T(8,128)(2,1)S(1)} %copy-done.3), channel_id=1, source_target_pairs={{0,1},{1,0},{2,3},{3,2},{4,5},{5,4},{6,7},{7,6},{8,9},{9,8},{10,11... | collective-permute-start | bytes 1966088 | tf_op jit(solution)/shard_map/ppermute | solution.py:513
  3.6 9.4 %collective-permute-start.4 = (bf16[256,1280]{1,0:T(8,128)(2,1)S(1)}, bf16[256,1280]{1,0:T(8,128)(2,1)S(1)}, u32[]{:S(2)}, u32[]{:S(2)}) collective-permute-start(bf16[256,1280]{1,0:T(8,128)(2,1)S(1)} %copy-done.2), channel_id=1, source_target_pairs={{0,1},{1,0},{2,3},{3,2},{4,5},{5,4},{6,7},{7,6},{8,9},{9,8},{10,11... | collective-permute-start | bytes 1966088 | tf_op jit(solution)/shard_map/ppermute | solution.py:512
  4.0 9.0 %copy-start.9 = (bf16[256,1280]{1,0:T(8,128)(2,1)S(1)}, bf16[256,1280]{1,0:T(8,128)(2,1)}, u32[]{:S(2)}) copy-start(bf16[256,1280]{1,0:T(8,128)(2,1)} %q_ref.3) | copy-start | bytes 1966084
  4.0 9.0 %copy-start.10 = (bf16[256,1280]{1,0:T(8,128)(2,1)S(1)}, bf16[256,1280]{1,0:T(8,128)(2,1)}, u32[]{:S(2)}) copy-start(bf16[256,1280]{1,0:T(8,128)(2,1)} %g_ref.3) | copy-start | bytes 1966084
  5.8 16.1 %all-to-all-start = ((bf16[32,24,128]{2,1,0:T(8,128)(2,1)}), bf16[32,24,128]{2,1,0:T(8,128)(2,1)S(1)}, u32[]{:S(2)}, u32[]{:S(2)}) async-start(bf16[32,24,128]{2,1,0:T(8,128)(2,1)} %bitcast.3), calls=%async_computation | async-start | bytes 393216 | tf_op jit(solution)/shard_map/all_to_all | solution.py:539
  20.6 3.4 %collective-permute-start.5 = (bf16[256,1280]{1,0:T(8,128)(2,1)}, bf16[256,1280]{1,0:T(8,128)(2,1)S(1)}, u32[]{:S(2)}, u32[]{:S(2)}) collective-permute-start(bf16[256,1280]{1,0:T(8,128)(2,1)} %get-tuple-element.37), channel_id=1, source_target_pairs={{0,1},{1,0},{2,3},{3,2},{4,5},{5,4},{6,7},{7,6},{8,9},{9,8},{10,11... | collective-permute-start | bytes 1966088 | tf_op jit(solution)/shard_map/ppermute | solution.py:579
  21.9 2.1 %copy-start = (f32[256,1280]{1,0:T(8,128)S(1)}, f32[256,1280]{1,0:T(8,128)}, u32[]{:S(2)}) copy-start(f32[256,1280]{1,0:T(8,128)} %get-tuple-element.34.dki) | copy-start | bytes 3932164
  21.9 2.1 %copy-start.1 = (f32[256,1280]{1,0:T(8,128)S(1)}, f32[256,1280]{1,0:T(8,128)}, u32[]{:S(2)}) copy-start(f32[256,1280]{1,0:T(8,128)} %get-tuple-element.35.dvi) | copy-start | bytes 3932164
  21.9 2.1 %copy-start.4 = (f32[80,128]{1,0:T(8,128)S(1)}, f32[80,128]{1,0:T(8,128)}, u32[]{:S(2)}) copy-start(f32[80,128]{1,0:T(8,128)} %get-tuple-element.33.terms_ref) | copy-start | bytes 122884
  21.9 2.1 %copy-start.5 = (bf16[10,16,128]{2,1,0:T(8,128)(2,1)S(1)}, bf16[10,16,128]{2,1,0:T(8,128)(2,1)}, u32[]{:S(2)}) copy-start(bf16[10,16,128]{2,1,0:T(8,128)(2,1)} %get-tuple-element.36.blocks_in) | copy-start | bytes 122884
  21.9 2.1 %copy-start.6 = (f32[32,256]{1,0:T(8,128)S(1)}, f32[32,256]{1,0:T(8,128)}, u32[]{:S(2)}) copy-start(f32[32,256]{1,0:T(8,128)} %get-tuple-element.29.s_hbm.s_ref) | copy-start | bytes 98308
  21.9 2.1 %copy-start.7 = (f32[32,256]{1,0:T(8,128)S(1)}, f32[32,256]{1,0:T(8,128)}, u32[]{:S(2)}) copy-start(f32[32,256]{1,0:T(8,128)} %get-tuple-element.30.dp_hbm.dp_ref) | copy-start | bytes 98308
  21.9 2.1 %copy-start.8 = (bf16[32,128]{1,0:T(8,128)(2,1)S(1)}, bf16[32,128]{1,0:T(8,128)(2,1)}, u32[]{:S(2)}) copy-start(bf16[32,128]{1,0:T(8,128)(2,1)} %get-tuple-element.28.far_ref) | copy-start | bytes 24580
  22.6 1.5 %collective-permute-start.2 = (f32[32,128]{1,0:T(8,128)S(1)}, f32[32,128]{1,0:T(8,128)S(1)}, u32[]{:S(2)}, u32[]{:S(2)}) collective-permute-start(f32[32,128]{1,0:T(8,128)S(1)} %get-tuple-element.27), channel_id=1, source_target_pairs={{0,1},{1,0},{2,3},{3,2},{4,5},{5,4},{6,7},{7,6},{8,9},{9,8},{10,11... | collective-permute-start | bytes 49160 | tf_op jit(solution)/shard_map/ppermute | solution.py:589
